TPU v7x, 32 devices: a whole 2x2x4 slice. The times are simulated.
32 devices in a mesh: lat: 8 (over z, x), tok: 4 (over y, core).
Axes of the slice: x: 2, y: 2, z: 4, core: 2. Of those that a mesh axis runs over, the one named last changes fastest.
Arguments:
- streams: bfloat16 [512, 2, 5120], P('tok', None, 'lat')
- active_mask: int32 [512, 16384], P('tok', 'lat'), may hold values from 0 to 1, as said below
- enc_weight: bfloat16 [16384, 2, 5120], P('lat'), may hold values from -0.0625 to 0.0625
- enc_bias: float32 [16384], P('lat'), may hold values from -3 to 3
- dec_weight: bfloat16 [16384, 2, 5120], P('lat'), may hold values from -0.5 to 0.5
- dec_bias: float32 [2, 5120], replicated, may hold values from -3 to 3
Outputs:
- enc_grad: bfloat16 [16384, 2, 5120], P(('lat', 'tok'))
- dec_grad: bfloat16 [16384, 2, 5120], P(('lat', 'tok'))
- mean_error: float32 [], replicated
Inputs may be any that keep to these rules, and one draw needn't show every extreme that they name: `active_mask`: each token has exactly 128 active latents.
All inputs are finite; a program needn't handle non-finite values.
Results may differ from a plain program's by a relative error of at most 0.0065.
Values may be sent and summed in bfloat16 or wider, within the bound.
No kernel may reach another device: no remote copies, remote signals or barrier semaphores. Data moves between devices by JAX's collectives and lax.ppermute only.
A program may use at most 576 MiB of HBM per device.

v0:
```python
import jax
import jax.numpy as jnp
from jax import lax
from jax.sharding import PartitionSpec as P

LOSS_SCALE = 128.0


def per_device(streams, active_mask, enc_weight, enc_bias, dec_weight, dec_bias):
    lat_count = lax.axis_size("lat")
    tok_count = lax.axis_size("tok")
    tok_dev, layers, width_part = streams.shape
    full_width = width_part * lat_count
    tokens = tok_dev * tok_count
    whole_x = lax.all_gather(streams, "lat", axis=2, tiled=True)
    own_x = streams.astype(jnp.float32)
    squares = jnp.sum(own_x * own_x, axis=(0, 2))
    square_sums = lax.psum(squares, ("lat", "tok"))
    norm_scale = lax.rsqrt(square_sums / (tokens * full_width) + 1e-06)
    enc_parts = jnp.einsum("tld,hld->lth", whole_x, enc_weight, preferred_element_type=jnp.float32)
    pre_act = jnp.sum(norm_scale[:, None, None] * enc_parts, axis=0) + enc_bias[None, :]
    mask_float = active_mask.astype(jnp.float32)
    act_low = (mask_float * pre_act).astype(jnp.bfloat16)
    recon_term = jnp.einsum("th,hld->tld", act_low, dec_weight, preferred_element_type=jnp.float32)
    factor = LOSS_SCALE / tokens
    recon_share = lax.psum_scatter(recon_term, "lat", scatter_dimension=2, tiled=True)
    bias_part = lax.dynamic_slice_in_dim(
        dec_bias, lax.axis_index("lat") * width_part, width_part, 1
    )
    diff = recon_share + bias_part[None] - norm_scale[None, :, None] * streams.astype(jnp.float32)
    error_sum = lax.psum(jnp.sum(diff * diff), ("lat", "tok"))
    err_low = lax.all_gather((diff * factor).astype(jnp.bfloat16), "lat", axis=2, tiled=True)
    mean_error = error_sum / (tokens * layers * full_width)
    lat_grad = jnp.einsum("tld,hld->th", err_low, dec_weight, preferred_element_type=jnp.float32)
    grad_low = (mask_float * lat_grad).astype(jnp.bfloat16)
    enc_part = jnp.einsum("th,tld->hld", grad_low, whole_x, preferred_element_type=jnp.float32)
    enc_part = enc_part * norm_scale[None, :, None]
    dec_part = jnp.einsum("th,tld->hld", act_low, err_low, preferred_element_type=jnp.float32)
    summed = lax.psum_scatter(
        jnp.stack([enc_part, dec_part], axis=1), "tok", scatter_dimension=0, tiled=True
    )
    enc_grad = summed[:, 0]
    dec_grad = summed[:, 1]
    return (enc_grad.astype(jnp.bfloat16), dec_grad.astype(jnp.bfloat16), mean_error)


def solution(mesh):
    in_specs = (
        P("tok", None, "lat"),
        P("tok", "lat"),
        P("lat", None, None),
        P("lat"),
        P("lat", None, None),
        P(),
    )
    out_specs = (P(("lat", "tok"), None, None), P(("lat", "tok"), None, None), P())
    return jax.shard_map(
        per_device, mesh=mesh, in_specs=in_specs, out_specs=out_specs, check_vma=False
    )
```

profile of v0, /device:TPU:0, one launch (start us, length us, event | category | flops | bytes accessed | tf_op | source)
XLA Modules:
  0.0 1755.7 jit_solution(17887768165004165735)
XLA Ops:
  7.2 0.0 copy-start
  7.2 0.0 all-gather.3.cloned.1.call-start
  7.2 1.7 copy.9
  9.0 0.0 all-gather.3.cloned.1.call-update
  9.0 0.0 reduce-scatter.3.cloned.1.call-start
  9.0 1.2 fusion.11
  10.2 42.9 %psum.14 = f32[2]{0:T(128)S(1)} all-reduce(f32[2]{0:T(128)S(1)} %fusion.11), channel_id=1, replica_groups=mesh['lat'=8,'tok'=4] {'lat','tok'}, use_global_device_ids=true, to_apply=%region_1.0 | all-reduce | flops 2 | bytes 16 | tf_op jit(solution)/shard_map/psum | solution.py:18
  53.1 100.5 %copy.17 = bf16[2048,2,5120]{0,2,1:T(8,128)(2,1)} copy(bf16[2048,2,5120]{2,1,0:T(2,128)(2,1)} %param.10) | data formatting | bytes 83886080 | tf_op args[4]
  153.7 0.0 all-gather.3.cloned.1.call-done
  153.7 34.1 %fusion.8 = f32[128,2048]{1,0:T(8,128)S(1)} fusion(bf16[128,2,5120]{2,0,1:T(8,128)(2,1)} %all-gather.3.cloned.1.call-done, bf16[2048,2,5120]{2,1,0:T(2,128)(2,1)} %param.8, f32[2]{0:T(128)S(1)} %add_rsqrt_fusion), kind=kOutput, calls=%fused_computation.12 | convolution fusion | flops 5369495552 | bytes 45613064 | tf_op jit(solution)/shard_map/tld,hld->lth/dot_general | solution.py:20
  187.9 0.1 fusion.13
  188.0 0.0 copy-start.4
  188.0 21.0 %fusion.14 = f32[128,2,5120]{2,0,1:T(8,128)} fusion(bf16[128,2048,1]{1,0,2:T(8,128)(2,1)S(1)} %fusion.13, bf16[2048,2,5120]{0,2,1:T(8,128)(2,1)} %copy.17), kind=kOutput, calls=%fused_computation.23 | convolution fusion | flops 5368709120 | bytes 47710208 | tf_op jit(solution)/shard_map/th,hld->tld/dot_general | solution.py:24
  209.0 0.0 reduce-scatter.3.cloned.1.call-update
  209.1 0.0 all-gather.5.cloned.1.call-start
  209.1 0.0 copy-done
  209.1 102.5 %reduce-scatter.3.cloned.1.call-done = f32[128,2,640]{2,0,1:T(8,128)} async-done(((f32[128,2,5120]{2,0,1:T(8,128)}), f32[128,2,640]{2,0,1:T(8,128)}) %reduce-scatter.3.cloned.1.call-update) | async-done | bytes 655376 | tf_op jit(solution)/shard_map/reduce_scatter | solution.py:26
  311.6 2.6 multiply_reduce_fusion
  314.2 0.0 all-gather.5.cloned.1.call-update
  314.3 0.2 reduce-scatter.5.cloned.1.call-start
  314.5 54.9 %all-gather.5.cloned.1.call-done = bf16[128,2,5120]{2,0,1:T(8,128)(2,1)} async-done(((bf16[128,2,640]{2,0,1:T(8,128)(2,1)}), bf16[128,2,5120]{2,0,1:T(8,128)(2,1)}) %all-gather.5.cloned.1.call-update) | async-done | bytes 2621456 | tf_op jit(solution)/shard_map/all_gather | solution.py:32
  369.4 20.4 %fusion.7.clone.4 = bf16[128,2048,1]{1,0,2:T(8,128)(2,1)} fusion(bf16[128,2,5120]{2,0,1:T(8,128)(2,1)} %all-gather.5.cloned.1.call-done, bf16[2048,2,5120]{0,2,1:T(8,128)(2,1)} %copy.17, s32[128,2048]{1,0:T(8,128)} %param.7), kind=kOutput, calls=%fused_computation.11.clone.clone.clone.1 | convolution fusion | flops 5369495552 | bytes 46137344 | tf_op jit(solution)/shard_map/tld,hld->th/dot_general | solution.py:34
  389.7 28.8 %convolution_bitcast_fusion = f32[2048,1,2,5120]{3,0,2,1:T(8,128)} fusion(bf16[128,2048,1]{1,0,2:T(8,128)(2,1)S(1)} %fusion.13, bf16[128,2,5120]{2,0,1:T(8,128)(2,1)S(1)} %copy-done.2), kind=kOutput, calls=%fused_computation.4 | convolution fusion | flops 5368709120 | bytes 87031808 | tf_op jit(solution)/shard_map/th,tld->hld/dot_general | solution.py:38
  418.5 31.7 %multiply_bitcast_fusion = f32[2048,1,2,5120]{3,0,2,1:T(8,128)} fusion(f32[2]{0:T(128)S(1)} %add_rsqrt_fusion, bf16[128,2,5120]{2,0,1:T(8,128)(2,1)} %all-gather.3.cloned.1.call-done, bf16[128,2048,1]{1,0,2:T(8,128)(2,1)} %fusion.7.clone.4), kind=kOutput, calls=%fused_computation.1 | convolution fusion | flops 5389680640 | bytes 87031816 | tf_op jit(solution)/shard_map/th,tld->hld/dot_general | solution.py:36
  450.2 107.9 %pad_maximum_fusion = f32[2048,2,2,5120]{3,0,2,1:T(8,128)} fusion(f32[2048,1,2,5120]{3,0,2,1:T(8,128)} %convolution_bitcast_fusion, f32[2048,1,2,5120]{3,0,2,1:T(8,128)} %multiply_bitcast_fusion), kind=kLoop, calls=%fused_computation | loop fusion | flops 41943040 | bytes 335544320 | tf_op jit(solution)/shard_map/stack | solution.py:40
  558.2 0.0 reduce-scatter.5.cloned.1.call-update
  558.2 39.7 %psum.15 = f32[]{:T(128)} all-reduce(f32[]{:T(128)} %get-tuple-element.8), channel_id=1, replica_groups=mesh['lat'=8,'tok'=4] {'lat','tok'}, use_global_device_ids=true, to_apply=%region_6.0 | all-reduce | flops 1 | bytes 8 | tf_op jit(solution)/shard_map/psum | solution.py:31
  598.6 1060.8 %reduce-scatter.5.cloned.1.call-done = f32[512,2,2,5120]{3,0,2,1:T(8,128)} async-done(((f32[2048,2,2,5120]{3,0,2,1:T(8,128)}), f32[512,2,2,5120]{3,0,2,1:T(8,128)}) %reduce-scatter.5.cloned.1.call-update) | async-done | bytes 41943056 | tf_op jit(solution)/shard_map/reduce_scatter | solution.py:39
  1659.4 14.9 convert.4
  1674.2 5.5 slice_bitcast_fusion
  1679.7 20.1 %copy.16 = bf16[512,2,5120]{2,1,0:T(2,128)(2,1)} copy(bf16[512,2,5120]{2,0,1:T(8,128)(2,1)} %get-tuple-element.6) | data formatting | bytes 20971520
  1699.9 48.2 %copy.15 = bf16[512,2,5120]{2,1,0:T(2,128)(2,1)} copy(bf16[512,2,5120]{2,0,1:T(8,128)(2,1)S(1)} %get-tuple-element.7) | data formatting | bytes 20971520
  (11 shorter events, 0.0 us)
Async XLA Ops:
  7.2 202.0 %copy-start = (f32[2,5120]{1,0:T(2,128)S(1)}, f32[2,5120]{1,0:T(2,128)}, u32[]{:S(2)}) copy-start(f32[2,5120]{1,0:T(2,128)} %param.11) | copy-start | bytes 122884
  7.2 146.5 %all-gather.3.cloned.1.call-start = ((), (), s32[]{:S(2)}) async-start(), calls=%async_computation.2 | async-start | bytes 2949120 | tf_op jit(solution)/shard_map/all_gather | solution.py:15
  9.0 302.6 %reduce-scatter.3.cloned.1.call-start = ((), (), s32[]{:S(2)}) async-start(), calls=%async_computation.3 | async-start | bytes 5898240 | tf_op jit(solution)/shard_map/reduce_scatter | solution.py:26
  153.7 34.2 %copy-start.3 = (s32[128,2048]{1,0:T(8,128)S(1)}, s32[128,2048]{1,0:T(8,128)}, u32[]{:S(2)}) copy-start(s32[128,2048]{1,0:T(8,128)} %param.7) | copy-start | bytes 3145732
  153.7 34.2 %copy-start.5 = (f32[2048]{0:T(1024)S(1)}, f32[2048]{0:T(1024)}, u32[]{:S(2)}) copy-start(f32[2048]{0:T(1024)} %param.9) | copy-start | bytes 24580
  188.0 123.6 %copy-start.4 = (bf16[128,2,640]{2,1,0:T(2,128)(2,1)S(1)}, bf16[128,2,640]{2,1,0:T(2,128)(2,1)}, u32[]{:S(2)}) copy-start(bf16[128,2,640]{2,1,0:T(2,128)(2,1)} %param.6) | copy-start | bytes 983044
  209.1 160.3 %all-gather.5.cloned.1.call-start = ((), (), s32[]{:S(2)}) async-start(), calls=%async_computation.4 | async-start | bytes 2949120 | tf_op jit(solution)/shard_map/all_gather | solution.py:32
  314.3 1345.1 %reduce-scatter.5.cloned.1.call-start = ((), (), s32[]{:S(2)}) async-start(), calls=%async_computation.5 | async-start | bytes 209715200 | tf_op jit(solution)/shard_map/reduce_scatter | solution.py:39
  369.4 20.4 %copy-start.2 = (bf16[128,2,5120]{2,0,1:T(8,128)(2,1)S(1)}, bf16[128,2,5120]{2,0,1:T(8,128)(2,1)}, u32[]{:S(2)}) copy-start(bf16[128,2,5120]{2,0,1:T(8,128)(2,1)} %all-gather.5.cloned.1.call-done) | copy-start | bytes 7864324
  1679.7 68.3 %copy-start.1 = (f32[2,5120]{1,0:T(2,128)S(1)}, f32[2,5120]{1,0:T(2,128)}, u32[]{:S(2)}) copy-start(f32[2,5120]{1,0:T(2,128)} %param.11) | copy-start | bytes 122884
Sparse Core Ops, SparseCore 0:
  10.8 58.7 all-gather.2
  209.2 102.3 reduce-scatter.2
  314.4 54.9 all-gather.4
  558.3 1101.0 reduce-scatter.4
where the time goes:
time: 1760 us
  waiting for transfers between devices  1220 us (69%)
  local copies, waits for them, and re-layouts  176 us (10%)
  matrix products  136 us (8%)
  other arithmetic  127 us (7%)
  blocking collectives  82.7 us (5%)
    reduce_scatter x1, waiting for transfers between devices, per_device(): lax.psum_scatter(jnp.stack([enc_part, dec_part], axis=1), 'tok', scatter_...  1060 us
    unnamed x16, local copies, waits for them, and re-layouts  171 us
    another operation x1, other arithmetic, per_device(): jnp.stack([enc_part, dec_part], axis=1)  108 us
    reduce_scatter x1, waiting for transfers between devices, per_device(): lax.psum_scatter(recon_term, 'lat', scatter_dimension=2, tiled=True)  102 us
    all_gather x1, waiting for transfers between devices, per_device(): lax.all_gather((diff * factor).astype(jnp.bfloat16), 'lat', axis=2, tiled...  54.9 us
    psum x1, blocking collectives, per_device(): square_sums = lax.psum(squares, ('lat', 'tok'))  42.9 us
    psum x1, blocking collectives, per_device(): error_sum = lax.psum(jnp.sum(diff * diff), ('lat', 'tok'))  39.7 us
  transfers between devices with their start and end apart: 4, of which 3 were waited for; matrix products, arithmetic and copies ran while one was open for 6% of the time, Pallas kernels for 0%

commit v1 on v0

v1 whole, which is shorter than its diff:
```python
import functools

import jax
import jax.numpy as jnp
from jax import lax
from jax.experimental import pallas as pl
from jax.experimental.pallas import tpu as pltpu
from jax.sharding import PartitionSpec as P

LOSS_SCALE = 128.0
LANES = 128
BF16 = jnp.bfloat16
F32 = jnp.float32
LATENT_ROWS = 256
VMEM_BYTES = 63 * 1024 * 1024
SMALL = pl.CostEstimate(flops=1024, bytes_accessed=1024, transcendentals=0)


def exchange(value, axis, mask):
    size = lax.axis_size(axis)
    return lax.ppermute(value, axis, [(i, i ^ mask) for i in range(size)])


def after(value, *others):
    return lax.optimization_barrier((value, *others))[0]


def sum_tokens(value):
    step = 1
    while step < lax.axis_size("tok"):
        value = value + exchange(value, "tok", step)
        step *= 2
    return value


def squares_kernel(ref, out_ref):
    layers, sub, lanes = out_ref.shape
    count, height, width = ref.shape
    tokens = height // layers
    for l in range(layers):
        sums = []
        for i in range(count):
            value = ref[i, l * tokens:(l + 1) * tokens, :].astype(F32)
            value = jnp.sum((value * value).reshape(tokens // sub, sub, width), axis=0)
            total = value[:, :lanes]
            for c in range(1, width // lanes):
                total = total + value[:, c * lanes:(c + 1) * lanes]
            sums.append(total)
        while len(sums) > 1:
            sums = [sums[i] + sums[i + 1] for i in range(0, len(sums), 2)]
        out_ref[l] = sums[0]


def squares(stacked, layers):
    return pl.pallas_call(
        squares_kernel,
        out_shape=jax.ShapeDtypeStruct((layers, 8, LANES), F32),
        compiler_params=pltpu.CompilerParams(vmem_limit_bytes=VMEM_BYTES),
        cost_estimate=SMALL,
        name="squares",
    )(stacked)


def block_order(count):
    return list(range(0, count, 2)), list(range(1, count, 2))


def gather_features(own, beside=(), over_tok=False):
    beside = list(beside)
    count = lax.axis_size("lat")
    if own.shape[1] % LANES:
        blocks = jnp.split(lax.all_gather(own, "lat", axis=1, tiled=True), 8, axis=1)
        return blocks, {k: exchange(block, "tok", 2) for k, block in enumerate(blocks) if over_tok}
    direct = {}
    step = count // 2
    while step:
        direct[step] = exchange(own, "lat", step)
        step //= 2
    held = {0: own}
    crossed = {1: direct[1]}
    far = {k: exchange(value, "tok", 2) for k, value in ((0, own), (1, direct[1])) if over_tok}
    early = [value for k, value in direct.items() if k < count // 2]
    early += [far[k] for k in far if k == 0]
    step = count // 2
    while step > 1:
        if beside:
            early += beside.pop(0)
        fresh = {
            k | step: exchange(value, "lat", step) if k else direct[step] for k, value in held.items()
        }
        for k, value in held.items():
            if k | 1 not in crossed:
                crossed[k | 1] = exchange(value, "lat", 1)
                early.append(crossed[k | 1])
        if step < count // 2:
            if over_tok:
                for k in (count // 2, step):
                    far[k] = exchange(held.get(k, direct[k]), "tok", 2)
                    early.append(far[k])
                early.append(far[1])
            else:
                crossed[step | 1] = exchange(direct[step], "lat", 1)
                early.append(crossed[step | 1])
        for k, value in fresh.items():
            held[k] = value if k in direct and k < count // 2 else after(value, *early)
        early = []
        step //= 2
    for k, value in held.items():
        if k | 1 not in crossed:
            crossed[k | 1] = exchange(value, "lat", 1)
    held.update(crossed)
    if over_tok:
        far.update({k: exchange(held[k], "tok", 2) for k in held if k not in far})
    return [held[k] for k in range(count)], far


def stack_kernel(*refs):
    for i, ref in enumerate(refs[:-1]):
        refs[-1][i] = ref[...]


def stack(blocks):
    return pl.pallas_call(
        stack_kernel,
        out_shape=jax.ShapeDtypeStruct((len(blocks), *blocks[0].shape), blocks[0].dtype),
        compiler_params=pltpu.CompilerParams(vmem_limit_bytes=VMEM_BYTES),
        cost_estimate=SMALL,
        name="stack",
    )(*blocks)


def scatter_features(pieces):
    pieces = dict(pieces)
    step = 4
    while step < lax.axis_size("lat"):
        for k in sorted(pieces, reverse=True):
            if k & step:
                sent = pieces.pop(k).astype(BF16)
                pieces[k ^ step] = pieces[k ^ step] + exchange(sent, "lat", step).astype(F32)
        step *= 2
    return pieces[0]


def run_slices(value, mask, axis):
    count = lax.axis_size("tok")
    rows = value.shape[axis] // count
    me = lax.axis_index("tok") ^ mask
    return jnp.concatenate(
        [lax.dynamic_slice_in_dim(value, (me ^ r) * rows, rows, axis) for r in range(0, count, 2)],
        axis=axis,
    )


def weight_copies(place, w_ref, buffer, sems, half):
    latents, layers, full = w_ref.shape
    pairs, parts, height, width = buffer.shape
    block = width // 2
    runs = lax.axis_size("tok") // 2
    quarter = layers * latents // (2 * runs)
    rows = min(height, quarter)
    pieces = height // rows
    flat = w_ref.reshape(latents * layers, full)

    def copies_of(pair, part):
        copies = []
        for piece in range(pieces):
            run, row = divmod(part * height + piece * rows, quarter)
            start = (place[1] ^ (2 * run)) * quarter + row
            for b in range(2):
                column = (place[0] ^ half[2 * pair + b]) * block
                copies.append(
                    pltpu.make_async_copy(
                        flat.at[
                            pl.ds(pl.multiple_of(start, rows), rows),
                            pl.ds(pl.multiple_of(column, LANES), block),
                        ],
                        buffer.at[pair, part, pl.ds(piece * rows, rows), pl.ds(b * block, block)],
                        sems.at[((pair * parts + part) * pieces + piece) * 2 + b],
                    )
                )
        return copies

    return copies_of


def weight_buffers(weight, half, block):
    latents, layers, full = weight.shape
    runs = lax.axis_size("tok") // 2
    quarter = latents // (2 * runs)
    rows = min(LATENT_ROWS, runs * quarter)
    parts = runs * quarter // rows
    pieces = max(1, rows // quarter)
    pairs = len(half) // 2
    return (
        pltpu.VMEM((pairs, parts, layers * rows, 2 * block), BF16),
        pltpu.SemaphoreType.DMA((pairs * parts * pieces * 2,)),
    )


def encode_kernel(place, w_ref, *refs, half, mode, earlier):
    blocks = refs[:2]
    sums = refs[2:2 + earlier]
    buffer, sems, values, scratch = refs[-4:]
    rest = refs[2 + earlier:-4]
    layers = w_ref.shape[1]
    count, height, width = blocks[0].shape
    tokens = height // layers
    pairs, parts, rows, _ = buffer.shape
    step = pl.program_id(0)
    copies_of = weight_copies(place, w_ref, buffer, sems, half)

    @pl.when(step == 0)
    def _():
        for part in range(parts):
            for pair in range(pairs):
                for copy in copies_of(pair, part):
                    copy.start()
        for l in range(layers):
            for e, ref in enumerate(blocks):
                start = (2 * l + e) * tokens
                for i in range(count):
                    values[start:start + tokens, i * width:(i + 1) * width] = ref[
                        i, l * tokens:(l + 1) * tokens, :
                    ]

    for part in range(parts):

        @pl.when(step == part)
        def _():
            for pair in range(pairs):
                for copy in copies_of(pair, part):
                    copy.wait()

    product = None
    for pair in range(pairs):
        term = lax.dot_general(
            buffer[pair, step],
            values[:, pair * 2 * width:(pair + 1) * 2 * width],
            (((1,), (1,)), ((), ())),
            preferred_element_type=F32,
        )
        product = term if product is None else product + term
    sums_of = []
    for l in range(layers):
        for e in range(2):
            scratch[l, e] = product[:, (2 * l + e) * tokens:(2 * l + e + 1) * tokens]
        sums_of.append(
            jnp.concatenate(
                [scratch[l, e, pl.ds(l, rows // layers, stride=layers)] for e in range(2)], axis=1
            )
        )
    if mode == "parts":
        for l in range(layers):
            rest[0][l] = sums_of[l]
    else:
        norm_ref, bias_ref, mask_ref, across_ref, act_ref = rest
        for ref in sums:
            sums_of = [value + ref[l] for l, value in enumerate(sums_of)]
        pre = norm_ref[0] * sums_of[0] + norm_ref[1] * sums_of[1] + bias_ref[...]
        act = mask_ref[...].astype(F32).T * pre
        act_ref[...] = act.astype(BF16)
        across_ref[...] = act.T.astype(BF16)


def encode(weight, half, own, near, place, mode, sums=(), norm=None, bias=None, mask=None):
    layers, full = weight.shape[1:]
    tokens = 2 * own.shape[1] // layers
    block = own.shape[2]
    buffer, sems = weight_buffers(weight, half, block)
    _, parts, height, _ = buffer.shape
    rows = height // layers
    latents = parts * rows
    whole = pl.BlockSpec(own.shape, lambda i, s: (0, 0, 0))
    flat = pl.BlockSpec((rows, tokens), lambda i, s: (i, 0))
    split = pl.BlockSpec((layers, rows, tokens), lambda i, s: (0, i, 0))
    in_specs = [pl.BlockSpec(memory_space=pl.ANY)] + [whole] * 2
    in_specs += [flat if value.ndim == 2 else split for value in sums]
    args = [weight, own, near, *sums]
    if mode == "act":
        across = pl.BlockSpec((tokens, rows), lambda i, s: (0, i))
        in_specs += [
            pl.BlockSpec(memory_space=pltpu.SMEM),
            pl.BlockSpec((rows, 1), lambda i, s: (i, 0)),
            across,
        ]
        args += [norm, bias, mask]
        out_specs = (across, flat)
        out_shape = (
            jax.ShapeDtypeStruct((tokens, latents), BF16),
            jax.ShapeDtypeStruct((latents, tokens), BF16),
        )
    else:
        out_specs = split
        out_shape = jax.ShapeDtypeStruct((layers, latents, tokens), F32)
    return pl.pallas_call(
        functools.partial(encode_kernel, half=half, mode=mode, earlier=len(sums)),
        grid_spec=pltpu.PrefetchScalarGridSpec(
            num_scalar_prefetch=1,
            grid=(parts,),
            in_specs=in_specs,
            out_specs=out_specs,
            scratch_shapes=[
                buffer,
                sems,
                pltpu.VMEM((layers * tokens, len(half) * block), BF16),
                pltpu.VMEM((layers, 2, height, tokens // 2), F32),
            ],
        ),
        out_shape=out_shape,
        compiler_params=pltpu.CompilerParams(vmem_limit_bytes=VMEM_BYTES),
        cost_estimate=SMALL,
        name="encode_" + mode,
    )(place, *args)


def rearrange_kernel(place, *refs, halves, count):
    parts = refs[:count]
    outs = refs[-3:-1]
    wide = refs[-1]
    rows, layers, full = parts[0].shape
    chunks = full // LANES
    each = outs[0].shape[2] // len(halves[0]) // LANES
    for p, w_ref in enumerate(parts):
        for c in range(chunks):
            wide[c] = (
                w_ref[:, :, c * LANES:(c + 1) * LANES].reshape(rows * layers, LANES).astype(F32)
            )
        for half, out_ref in zip(halves, outs):
            for i, k in enumerate(half):
                for c in range(each):
                    chunk = (place[0] ^ k) * each + c
                    column = (i * each + c) * LANES
                    for l in range(layers):
                        out_ref[l, p * rows:(p + 1) * rows, column:column + LANES] = wide[
                            chunk, pl.ds(l, rows, stride=layers)
                        ].astype(BF16)


def rearrange(weight, place, halves, runs, run, earlier=()):
    latents, layers, full = weight.shape
    quarter = latents // (2 * runs)
    part = min(64, quarter // 2)
    count = 2
    rows = count * part
    steps = quarter // rows

    def index_of(p):
        return lambda i, s: (((s[1] ^ (2 * run)) * steps + i) * count + p, 0, 0)

    out = pl.BlockSpec((layers, rows, full // 2), lambda i, s: (0, run * steps + i, 0))
    shape = jax.ShapeDtypeStruct((layers, runs * quarter, full // 2), BF16)
    return pl.pallas_call(
        functools.partial(rearrange_kernel, halves=halves, count=count),
        grid_spec=pltpu.PrefetchScalarGridSpec(
            num_scalar_prefetch=1,
            grid=(steps,),
            in_specs=[pl.BlockSpec((part, layers, full), index_of(p)) for p in range(count)]
            + [pl.BlockSpec(memory_space=pl.ANY)] * len(earlier),
            out_specs=(out, out),
            scratch_shapes=[pltpu.VMEM((full // LANES, part * layers, LANES), F32)],
        ),
        out_shape=(shape, shape),
        input_output_aliases={1 + count + i: i for i in range(len(earlier))},
        compiler_params=pltpu.CompilerParams(vmem_limit_bytes=VMEM_BYTES),
        cost_estimate=SMALL,
        name="rearrange",
    )(place, *[weight] * count, *earlier)


def project_kernel(*refs, layers, mode, earlier):
    w_refs = refs[:layers]
    blocks = refs[layers:layers + 2]
    sums = refs[layers + 2:layers + 2 + earlier]
    values = refs[-1]
    rest = refs[layers + 2 + earlier:-1]
    count, height, width = blocks[0].shape
    tokens = height // layers

    @pl.when(pl.program_id(0) == 0)
    def _():
        for e, ref in enumerate(blocks):
            for l in range(layers):
                for i in range(count):
                    values[l, e * tokens:(e + 1) * tokens, i * width:(i + 1) * width] = ref[
                        i, l * tokens:(l + 1) * tokens, :
                    ]

    parts = [
        lax.dot_general(
            w_refs[l][0], values[l], (((1,), (1,)), ((), ())), preferred_element_type=F32
        )
        for l in range(layers)
    ]
    if mode == "sum":
        rest[0][...] = parts[0] + parts[1]
    else:
        mask_ref, grad_ref = rest
        total = parts[0] + parts[1]
        for ref in sums:
            total = total + ref[...]
        grad_ref[...] = (mask_ref[...].astype(F32).T * total).astype(BF16)


def project(matrix, own, near, mode, sums=(), mask=None):
    layers, latents, width = matrix.shape
    tokens = 2 * own.shape[1] // layers
    rows = min(LATENT_ROWS, latents)
    whole = pl.BlockSpec(own.shape, lambda i: (0, 0, 0))
    flat = pl.BlockSpec((rows, tokens), lambda i: (i, 0))
    across = pl.BlockSpec((tokens, rows), lambda i: (0, i))

    def layer(l):
        return pl.BlockSpec((1, rows, width), lambda i: (l, i, 0))

    in_specs = [layer(l) for l in range(layers)] + [whole] * 2
    in_specs += [flat] * len(sums)
    args = [matrix] * layers + [own, near, *sums]
    if mode == "grad":
        in_specs.append(across)
        args.append(mask)
    out_specs = flat
    out_shape = jax.ShapeDtypeStruct((latents, tokens), BF16 if mode == "grad" else F32)
    return pl.pallas_call(
        functools.partial(project_kernel, layers=layers, mode=mode, earlier=len(sums)),
        grid=(latents // rows,),
        in_specs=in_specs,
        out_specs=out_specs,
        scratch_shapes=[pltpu.VMEM((layers, tokens, width), BF16)],
        out_shape=out_shape,
        compiler_params=pltpu.CompilerParams(vmem_limit_bytes=VMEM_BYTES),
        cost_estimate=SMALL,
        name="project_" + mode,
    )(*args)


def recon_kernel(act_ref, *refs, parts):
    w_refs = refs[:parts]
    keep_ref = refs[parts]
    send_refs = refs[parts + 1:]
    depth = w_refs[0].shape[1]
    product = None
    for p, w_ref in enumerate(w_refs):
        term = jnp.dot(
            act_ref[:, p * depth:(p + 1) * depth], w_ref[0], preferred_element_type=F32
        )
        product = term if product is None else product + term
    blocks, own, width = keep_ref.shape
    for i in range(blocks):
        keep_ref[i] = product[:own, i * width:(i + 1) * width]
    if len(send_refs) == 1:
        for i in range(blocks):
            send_refs[0][i] = product[own:, i * width:(i + 1) * width].astype(BF16)
    else:
        for pair in range(len(send_refs) // 2):

            @pl.when(pl.program_id(0) == pair)
            def _():
                for i in range(2):
                    send_refs[2 * pair + i][...] = product[
                        own:, i * width:(i + 1) * width
                    ].astype(BF16)


def recon_half(act, matrix, blocks, apart):
    layers, latents, full = matrix.shape
    width = full // blocks
    tokens = act.shape[0] // 2
    parts = 2

    def part(p):
        return pl.BlockSpec((1, latents // parts, 2 * width), lambda i, j: (j, p, i))

    def single(b):
        def index(i, j):
            return jnp.where(i < b // 2, 0, jnp.where(i > b // 2, layers - 1, j)), 0

        return pl.BlockSpec((tokens, width), index)

    out = pl.BlockSpec((2, tokens, width), lambda i, j: (i, j, 0))
    shape = (blocks, layers * tokens, width)
    if apart:
        send_specs = [single(b) for b in range(blocks)]
        send_shapes = [jax.ShapeDtypeStruct(shape[1:], BF16)] * blocks
    else:
        send_specs, send_shapes = [out], [jax.ShapeDtypeStruct(shape, BF16)]
    keep, *send = pl.pallas_call(
        functools.partial(recon_kernel, parts=parts),
        grid=(blocks // 2, layers),
        in_specs=[pl.BlockSpec(act.shape, lambda i, j: (0, 0))] + [part(p) for p in range(parts)],
        out_specs=[out] + send_specs,
        out_shape=[jax.ShapeDtypeStruct(shape, F32)] + send_shapes,
        compiler_params=pltpu.CompilerParams(vmem_limit_bytes=VMEM_BYTES),
        cost_estimate=SMALL,
        name="recon_half",
    )(act, *[matrix] * parts)
    return keep, send


def grad_kernel(place, scale_ref, own_ref, far_ref, *refs, groups, where, sources, scaled):
    value_refs = refs[:sources]
    out_ref, values, left, wide, results, sems, out_sems = refs[sources:]
    pair, pairs = pl.program_id(0), pl.num_programs(0)
    pairs_held, layers, depth, width = values.shape
    tokens = depth // groups
    half = width // 2
    rows = out_ref.shape[0]
    blocks = len(where) // groups
    flat = out_ref.reshape(rows * layers, out_ref.shape[2])

    def copy_of(g, k, l):
        side = (k % 2) ^ place[1]
        source, index = where[g * blocks + k]
        if source is None:
            piece = value_refs[index[0]].at[place[2] ^ g, index[1]]
        elif index < 0:
            piece = value_refs[source]
        else:
            piece = value_refs[source].at[index]
        return pltpu.make_async_copy(
            piece.at[pl.ds(l * tokens, tokens)],
            values.at[
                k // 2, l, pl.ds(g * tokens, tokens), pl.ds(pl.multiple_of(side * half, LANES), half)
            ],
            sems.at[(g * blocks + k) * layers + l],
        )

    def copy_out(turn):
        return pltpu.make_async_copy(
            results.at[lax.rem(turn, 2)],
            flat.at[:, pl.ds(pl.multiple_of((place[0] ^ turn) * width, LANES), width)],
            out_sems.at[lax.rem(turn, 2)],
        )

    @pl.when(pair == 0)
    def _():
        for k in range(blocks):
            for g in range(groups):
                for l in range(layers):
                    copy_of(g, k, l).start()
        near = own_ref.shape[1]
        left[:, :near] = own_ref[...]
        left[:, near:] = far_ref[...]

    for j in range(blocks // 2):

        @pl.when(pair == j)
        def _():
            for b in range(2):
                for g in range(groups):
                    for l in range(layers):
                        copy_of(g, 2 * j + b, l).wait()

    for l in range(layers):
        product = jnp.dot(left[...], values[pair, l], preferred_element_type=F32)
        if scaled:
            product = product * scale_ref[l]
        for c in range(width // LANES):
            wide[c, pl.ds(l, rows, stride=layers)] = product[:, c * LANES:(c + 1) * LANES]

    @pl.when(pair >= 2)
    def _():
        copy_out(pair - 2).wait()

    for c in range(width // LANES):
        results[lax.rem(pair, 2), :, c * LANES:(c + 1) * LANES] = wide[c].astype(BF16)
    copy_out(pair).start()

    @pl.when(pair == pairs - 1)
    def _():
        copy_out(pair - 1).wait()
        copy_out(pair).wait()


def weight_grad(own, far, sources, where, place, scale, scaled, shape):
    rows = far.shape[0]
    layers, full = shape
    groups = lax.axis_size("tok")
    depth = own.shape[1] + far.shape[1]
    blocks = len(where) // groups
    width = full // (blocks // 2)
    anywhere = pl.BlockSpec(memory_space=pl.ANY)
    return pl.pallas_call(
        functools.partial(
            grad_kernel, groups=groups, where=where, sources=len(sources), scaled=scaled
        ),
        grid_spec=pltpu.PrefetchScalarGridSpec(
            num_scalar_prefetch=1,
            grid=(blocks // 2,),
            in_specs=[
                pl.BlockSpec(memory_space=pltpu.SMEM),
                pl.BlockSpec(far.shape, lambda i, s: (0, 0)),
                pl.BlockSpec(far.shape, lambda i, s: (0, 0)),
            ]
            + [anywhere] * len(sources),
            out_specs=anywhere,
            scratch_shapes=[
                pltpu.VMEM((blocks // 2, layers, depth, width), BF16),
                pltpu.VMEM((rows, depth), BF16),
                pltpu.VMEM((width // LANES, rows * layers, LANES), F32),
                pltpu.VMEM((2, rows * layers, width), BF16),
                pltpu.SemaphoreType.DMA((groups * blocks * layers,)),
                pltpu.SemaphoreType.DMA((2,)),
            ],
        ),
        out_shape=jax.ShapeDtypeStruct((rows, layers, full), BF16),
        compiler_params=pltpu.CompilerParams(vmem_limit_bytes=VMEM_BYTES),
        cost_estimate=SMALL,
        name="weight_grad",
    )(place, scale, own, far, *sources)


def per_device(streams, active_mask, enc_weight, enc_bias, dec_weight, dec_bias):
    lat_count = lax.axis_size("lat")
    tok_count = lax.axis_size("tok")
    tok_dev, layers, width_part = streams.shape
    full_width = width_part * lat_count
    tokens = tok_dev * tok_count
    me = lax.axis_index("lat")
    aligned = width_part % LANES == 0
    block_count = lat_count if aligned else 8
    block_width = full_width // block_count
    here = me if aligned else jnp.zeros_like(me)

    own_x = streams.transpose(1, 0, 2).reshape(layers * tok_dev, width_part)
    own_f = own_x.astype(F32).reshape(layers, tok_dev, width_part)
    runs = tok_count // 2
    tok_me = lax.axis_index("tok")
    halves = block_order(block_count)
    spot = jnp.stack([here, tok_me]).astype(jnp.int32)
    place = jnp.stack([here >> 1, here & 1, tok_me]).astype(jnp.int32)

    mask_low = active_mask.astype(BF16)
    mask_far = exchange(run_slices(mask_low, 1, 1), "tok", 1)
    mask = jnp.concatenate([run_slices(mask_low, 0, 1), mask_far], axis=0)
    bias = run_slices(enc_bias.reshape(-1, 1), 0, 0)

    def gather_halves(own, multiply, beside=(), over_tok=False):
        blocks, far = gather_features(own, beside, over_tok)
        first = stack([blocks[k] for k in halves[0]])
        first_near = exchange(first, "tok", 1)
        sums = multiply(first, first_near)
        squared = squares(first, layers)
        early = [sums, squared]
        if over_tok:
            early += [far[k] for k in (6, 5)]
        final = halves[1][-1]
        blocks[final] = after(blocks[final], *early)
        second = stack([blocks[k] for k in halves[1]])
        near = [first_near, exchange(second, "tok", 1)]
        return [first, second], near, sums, squared, far

    dec_first = rearrange(dec_weight, spot, halves, runs, 0)
    dec_halves = rearrange(dec_weight, spot, halves, runs, 1, dec_first)
    x_own, x_near, sums, squared, _ = gather_halves(
        own_x,
        lambda own, near: encode(enc_weight, halves[0], own, near, spot, "parts"),
        beside=([*dec_first, mask, bias], dec_halves),
    )
    square_sums = jnp.sum(sum_tokens(squared + squares(x_own[1], layers)), axis=(1, 2))
    norm_scale = lax.rsqrt(square_sums / (tokens * full_width) + 1e-06)
    act_across, act = encode(
        enc_weight, halves[1], x_own[1], x_near[1], spot, "act", [sums], norm_scale, bias, mask
    )
    x_all = [lax.all_gather(value, "tok") for value in x_own]
    quarter = act.shape[0] // runs

    bias_part = lax.dynamic_slice_in_dim(dec_bias, me * width_part, width_part, 1)
    keep, send = recon_half(act_across, dec_halves[1], block_count // 2, False)
    cross = keep + exchange(send[0], "tok", 1).astype(F32)
    starts = range(block_count // 2 - 2, -2, -2)
    if aligned:
        bundles = [cross[start:start + 2].astype(BF16) for start in starts]
        act_across = after(act_across, *bundles)
        bundles = [exchange(bundle, "lat", 1) for bundle in bundles]
    keep, send = recon_half(act_across, dec_halves[0], block_count // 2, True)
    send = [exchange(value, "tok", 1) for value in send]
    act_far = exchange(act[quarter:], "tok", 2)
    if aligned:
        pieces = {}
        received = None
        for start, bundle in zip(starts, bundles):
            if received is not None:
                bundle = after(bundle, received)
            low, high = [
                keep[i] + send[i].astype(F32) + bundle[i - start].astype(F32)
                for i in (start, start + 1)
            ]
            received = exchange(high.astype(BF16), "lat", 2)
            pieces[2 * start] = low + received.astype(F32)
        recon = scatter_features(pieces)
    else:
        own = keep + jnp.stack(send).astype(F32)
        whole = jnp.stack([own, cross], axis=1).reshape(block_count, layers * tok_dev, block_width)
        whole = whole.transpose(1, 0, 2).reshape(layers * tok_dev, full_width)
        recon = lax.psum_scatter(whole, "lat", scatter_dimension=1, tiled=True)
    recon = after(recon, act_far, *x_all)

    recon = recon.reshape(layers, tok_dev, width_part) + bias_part[:, None]
    diff = recon - norm_scale[:, None, None] * own_f
    factor = LOSS_SCALE / tokens
    err_low = (diff * factor).astype(BF16).reshape(layers * tok_dev, width_part)
    err_own, err_near, sums, squared, far = gather_halves(
        err_low, lambda own, near: project(dec_halves[0], own, near, "sum"), over_tok=True
    )
    grad = project(dec_halves[1], err_own[1], err_near[1], "grad", [sums], mask=mask)
    grad_far = exchange(grad[quarter:], "tok", 2)
    error_sums = squared + squares(err_own[1], layers)
    soon = [k for k in range(block_count) if k not in (3, 7)]
    last = {k: exchange(far[k], "tok", 1) for k in soon}
    grad_far, error_sums, far[3], far[7] = lax.optimization_barrier(
        (grad_far, error_sums, far[3], far[7])
    )

    shape = (layers, full_width)
    spots = {k: (h, i) for h, half in enumerate(halves) for i, k in enumerate(half)}
    order = [spots[k] for k in range(block_count)]
    enc_grad = weight_grad(
        grad, grad_far, x_all, [(None, spot) for spot in order] * tok_count, place,
        norm_scale, True, shape,
    )
    error_sums = error_sums + exchange(error_sums, "tok", 1)
    act, error_sums = lax.optimization_barrier((act, error_sums))
    for k in (3, 7):
        last[k] = exchange(far[k], "tok", 1)
    where = [(2 * g + h, i) for g in range(2) for h, i in order]
    where += [(4 + g * block_count + k, -1) for g in range(2) for k in range(block_count)]
    sources = err_own + err_near + [group[k] for group in (far, last) for k in range(block_count)]
    dec_grad = weight_grad(act, act_far, sources, where, place, norm_scale, False, shape)
    error_sum = jnp.sum(error_sums + exchange(error_sums, "tok", 2))
    mean_error = error_sum / (factor * factor * tokens * layers * full_width)
    return (enc_grad, dec_grad, mean_error)


def solution(mesh):
    in_specs = (
        P("tok", None, "lat"),
        P("tok", "lat"),
        P("lat", None, None),
        P("lat"),
        P("lat", None, None),
        P(),
    )
    out_specs = (P(("lat", "tok"), None, None), P(("lat", "tok"), None, None), P())
    return jax.shard_map(
        per_device, mesh=mesh, in_specs=in_specs, out_specs=out_specs, check_vma=False
    )
```

time: 1760 us -> 288 us (0.16)
  waiting for transfers between devices: 1220 us -> 79.6 us
  local copies, waits for them, and re-layouts: 176 us -> 7.09 us
  matrix products: 136 us -> 0 us
  Pallas kernels: 0 us -> 128 us
  other arithmetic: 127 us -> 14.3 us
  blocking collectives: 82.7 us -> 0 us
  starting transfers between devices: 0.34 us -> 41.1 us
    reduce_scatter x2 -> x0, waiting for transfers between devices: 1160 us -> none  [the longest x1 1060 us: per_device(): lax.psum_scatter(jnp.stack([enc_part, dec_part], axis=1), 'tok', scatter_...]
    unnamed x16 -> x51, local copies, waits for them, and re-layouts: 171 us -> 3.3 us
    dot_general x5 -> x0, matrix products: 136 us -> none  [the longest x1 34.1 us: per_device(): jnp.einsum('tld,hld->lth', whole_x, enc_weight, preferred_element_type=jn...]
    pallas_call x0 -> x18, Pallas kernels: none -> 128 us  [the longest x2 26.9 us: weight_grad(): pl.pallas_call(functools.partial(grad_kernel, groups=groups, where=where,...]
    another operation x2 -> x3, other arithmetic: 123 us -> 3.41 us  [the longest x1 108 us: per_device(): jnp.stack([enc_part, dec_part], axis=1)]
    psum x2 -> x0, blocking collectives: 82.7 us -> none  [the longest x1 42.9 us: per_device(): square_sums = lax.psum(squares, ('lat', 'tok'))]
    ppermute x0 -> x51, waiting for transfers between devices: none -> 79.5 us  [exchange(): return lax.ppermute(value, axis, [(i, i ^ mask) for i in range(size)])]
    all_gather x2, waiting for transfers between devices: 54.9 us -> 0.04 us  [per_device(): x_all = [lax.all_gather(value, 'tok') for value in x_own]]
  transfers between devices with their start and end apart: 4 -> 53, of which waited for: 3 -> 22; matrix products, arithmetic and copies ran while one was open for 6% -> 6% of each run, Pallas kernels for 0% -> 38%
where the time goes in v1:
time: 288 us; the launch traced here: 287 us
  Pallas kernels  128 us (44%)
  waiting for transfers between devices  79.6 us (28%)
  starting transfers between devices  41.1 us (14%)
  between operations  16.2 us (6%)
  other arithmetic  14.3 us (5%)
  local copies, waits for them, and re-layouts  7.09 us (2%)
    ppermute x51, waiting for transfers between devices, exchange(): return lax.ppermute(value, axis, [(i, i ^ mask) for i in range(size)])  79.5 us
    ppermute x51, starting transfers between devices, exchange(): return lax.ppermute(value, axis, [(i, i ^ mask) for i in range(size)])  41 us
    pallas_call x2, Pallas kernels, weight_grad(): pl.pallas_call(functools.partial(grad_kernel, groups=groups, where=where,...  26.9 us
    pallas_call x2, Pallas kernels, rearrange(): pl.pallas_call(functools.partial(rearrange_kernel, halves=halves, count=c...  26.1 us
    pallas_call x2, Pallas kernels, encode(): pl.pallas_call(functools.partial(encode_kernel, half=half, mode=mode, ear...  24.9 us
    pallas_call x2, Pallas kernels, project(): pl.pallas_call(functools.partial(project_kernel, layers=layers, mode=mode...  16.7 us
    pallas_call x2, Pallas kernels, recon_half(): pl.pallas_call(functools.partial(recon_kernel, parts=parts), grid=(blocks...  15.8 us
    pallas_call x4, Pallas kernels, stack(): pl.pallas_call(stack_kernel, out_shape=jax.ShapeDtypeStruct((len(blocks),...  9.8 us
  transfers between devices with their start and end apart: 53, of which 22 were waited for; matrix products, arithmetic and copies ran while one was open for 6% of the time, Pallas kernels for 38%

profile of v1, /device:TPU:0, one launch (start us, length us, event | category | flops | bytes accessed | tf_op | source)
XLA Modules:
  0.0 286.8 jit_solution(6697487868723100535)
XLA Ops:
  8.2 3.1 %collective-permute-start = (bf16[256,640]{1,0:T(8,128)(2,1)S(1)}, bf16[256,640]{1,0:T(8,128)(2,1)}, u32[]{:S(2)}, u32[]{:S(2)}) collective-permute-start(bf16[256,640]{1,0:T(8,128)(2,1)S(1)} %bitcast.49), channel_id=1, source_target_pairs={{0,8},{4,12},{8,0},{12,4},{16,24},{20,28},{24,16},{28,20},{1,9},{5... | collective-permute-start | bytes 983048 | tf_op jit(solution)/shard_map/ppermute | solution.py:21
  11.3 2.6 collective-permute-start.1
  18.2 13.1 %rearrange.2 = (bf16[2,1024,2560]{2,1,0:T(8,128)(2,1)}, bf16[2,1024,2560]{2,1,0:T(8,128)(2,1)}) custom-call(s32[2]{0:T(128)} %pad_add_fusion.1.place, bf16[2048,2,5120]{2,1,0:T(2,128)(2,1)} %refs_1_.3, bf16[2048,2,5120]{2,1,0:T(2,128)(2,1)} %refs_1_.3), custom_call_target="tpu_custom_call" | custom-call | flops 1024 | bytes 1024 | tf_op jit(solution)/shard_map/rearrange/pallas_call | solution.py:352
  35.8 13.0 %rearrange.3 = (bf16[2,1024,2560]{2,1,0:T(8,128)(2,1)}, bf16[2,1024,2560]{2,1,0:T(8,128)(2,1)}) custom-call(s32[2]{0:T(128)} %pad_add_fusion.1.place, bf16[2048,2,5120]{2,1,0:T(2,128)(2,1)} %refs_1_.3, bf16[2048,2,5120]{2,1,0:T(2,128)(2,1)} %refs_1_.3, ...), custom_call_target="tpu_custom_call", output_to_operand_aliasing={{0}: (3, {}), {1}: (4, {})} | custom-call | flops 1024 | bytes 1024 | tf_op jit(solution)/shard_map/rearrange/pallas_call | solution.py:352
  48.8 2.1 collective-permute-done.6.refs_1_
  50.9 2.4 stack.29.ref.refs_0_
  56.9 12.6 %encode_parts.1.refs_2_ = f32[2,1024,256]{2,1,0:T(8,128)} custom-call(s32[2]{0:T(128)} %pad_add_fusion.1.place, bf16[2048,2,5120]{2,1,0:T(2,128)(2,1)} %w_ref.3, bf16[4,256,640]{2,1,0:T(8,128)(2,1)} %stack.29.ref.refs_0_, bf16[4,256,640]{2,1,0:T(8,128)(2,1)} %collective-permute-done.8.refs_1_), custom_call_target="tpu_custom_call" | custom-call | flops 1024 | bytes 1024 | tf_op jit(solution)/shard_map/encode_parts/pallas_call | solution.py:295
  70.3 2.5 stack.30.ref.refs_0_
  72.8 2.0 squares.5
  81.4 12.3 %encode_act.1 = (bf16[256,1024]{1,0:T(8,128)(2,1)}, bf16[1024,256]{1,0:T(8,128)(2,1)}) custom-call(s32[2]{0:T(128)} %pad_add_fusion.1.place, bf16[2048,2,5120]{2,1,0:T(2,128)(2,1)} %w_ref.3, bf16[4,256,640]{2,1,0:T(8,128)(2,1)} %stack.30.ref.refs_0_, bf16[4,256,640]{2,1,0:T(8,128)(2,1)} %collective-permute-done.11.refs_1_, ...), custom_call_target="tpu_custom_call" | custom-call | flops 1024 | bytes 1024 | tf_op jit(solution)/shard_map/encode_act/pallas_call | solution.py:295
  93.7 7.9 %recon_half.2 = (f32[4,256,640]{2,1,0:T(8,128)}, bf16[4,256,640]{2,1,0:T(8,128)(2,1)}) custom-call(bf16[256,1024]{1,0:T(8,128)(2,1)} %get-tuple-element.41.act_ref, bf16[2,1024,2560]{2,1,0:T(8,128)(2,1)} %get-tuple-element.35.refs_0_.refs_1_, bf16[2,1024,2560]{2,1,0:T(8,128)(2,1)} %get-tuple-element.35.refs_0_.refs_1_), custom_call_target="tpu_custom_call" | custom-call | flops 1024 | bytes 1024 | tf_op jit(solution)/shard_map/recon_half/pallas_call | solution.py:486
  101.5 3.2 %collective-permute-done.12 = bf16[4,256,640]{2,1,0:T(8,128)(2,1)S(1)} collective-permute-done((bf16[4,256,640]{2,1,0:T(8,128)(2,1)}, bf16[4,256,640]{2,1,0:T(8,128)(2,1)S(1)}, u32[]{:S(2)}, u32[]{:S(2)}) %collective-permute-start.12) | collective-permute-done | bytes 1310752 | tf_op jit(solution)/shard_map/ppermute | solution.py:21
  104.8 2.1 add_convert_fusion
  108.6 8.0 %recon_half.3 = (f32[4,256,640]{2,1,0:T(8,128)}, bf16[256,640]{1,0:T(8,128)(2,1)}, bf16[256,640]{1,0:T(8,128)(2,1)}, bf16[256,640]{1,0:T(8,128)(2,1)}, bf16[256,640]{1,0:T(8,128)(2,1)}) custom-call(bf16[256,1024]{1,0:T(8,128)(2,1)} %get-tuple-element.41.act_ref, bf16[2,1024,2560]{2,1,0:T(8,128)(2,1)} %get-tuple-element.34.refs_0_.refs_1_, ...), custom_call_target="tpu_custom_call" | custom-call | flops 1024 | bytes 1024 | tf_op jit(solution)/shard_map/recon_half/pallas_call | solution.py:486
  118.4 7.1 %collective-permute-done.16 = bf16[2,256,640]{2,1,0:T(8,128)(2,1)} collective-permute-done((bf16[2,256,640]{2,1,0:T(8,128)(2,1)S(1)}, bf16[2,256,640]{2,1,0:T(8,128)(2,1)}, u32[]{:S(2)}, u32[]{:S(2)}) %collective-permute-start.16) | collective-permute-done | bytes 655392 | tf_op jit(solution)/shard_map/ppermute | solution.py:21
  128.9 9.8 %collective-permute-done.14 = bf16[2,256,640]{2,1,0:T(8,128)(2,1)S(1)} collective-permute-done((bf16[2,256,640]{2,1,0:T(8,128)(2,1)}, bf16[2,256,640]{2,1,0:T(8,128)(2,1)S(1)}, u32[]{:S(2)}, u32[]{:S(2)}) %collective-permute-start.14) | collective-permute-done | bytes 655392 | tf_op jit(solution)/shard_map/ppermute | solution.py:21
  143.7 13.5 %collective-permute-done.21 = bf16[256,640]{1,0:T(8,128)(2,1)S(1)} collective-permute-done((bf16[256,640]{1,0:T(8,128)(2,1)S(1)}, bf16[256,640]{1,0:T(8,128)(2,1)S(1)}, u32[]{:S(2)}, u32[]{:S(2)}) %collective-permute-start.21) | collective-permute-done | bytes 327712 | tf_op jit(solution)/shard_map/ppermute | solution.py:21
  159.6 3.2 %collective-permute-start.26 = (bf16[256,640]{1,0:T(8,128)(2,1)S(1)}, bf16[256,640]{1,0:T(8,128)(2,1)S(1)}, u32[]{:S(2)}, u32[]{:S(2)}) collective-permute-start(bf16[256,640]{1,0:T(8,128)(2,1)S(1)} %bitcast.55), channel_id=1, source_target_pairs={{0,16},{4,20},{8,24},{12,28},{16,0},{20,4},{24,8},{28,12},{1,17},{... | collective-permute-start | bytes 983048 | tf_op jit(solution)/shard_map/ppermute | solution.py:21
  164.4 3.2 %collective-permute-done.23.refs_0_ = bf16[256,640]{1,0:T(8,128)(2,1)S(1)} collective-permute-done((bf16[256,640]{1,0:T(8,128)(2,1)S(1)}, bf16[256,640]{1,0:T(8,128)(2,1)S(1)}, u32[]{:S(2)}, u32[]{:S(2)}) %collective-permute-start.23) | collective-permute-done | bytes 327712 | tf_op jit(solution)/shard_map/ppermute | solution.py:21
  167.6 7.0 %collective-permute-done.24.refs_1_ = bf16[256,640]{1,0:T(8,128)(2,1)S(1)} collective-permute-done((bf16[256,640]{1,0:T(8,128)(2,1)S(1)}, bf16[256,640]{1,0:T(8,128)(2,1)S(1)}, u32[]{:S(2)}, u32[]{:S(2)}) %collective-permute-start.24) | collective-permute-done | bytes 327712 | tf_op jit(solution)/shard_map/ppermute | solution.py:21
  180.8 2.6 collective-permute-done.28.refs_2_
  184.4 3.7 %collective-permute-done.30.refs_8_ = bf16[256,640]{1,0:T(8,128)(2,1)S(1)} collective-permute-done((bf16[256,640]{1,0:T(8,128)(2,1)S(1)}, bf16[256,640]{1,0:T(8,128)(2,1)S(1)}, u32[]{:S(2)}, u32[]{:S(2)}) %collective-permute-start.30) | collective-permute-done | bytes 327712 | tf_op jit(solution)/shard_map/ppermute | solution.py:21
  188.1 6.8 %collective-permute-done.31.refs_6_ = bf16[256,640]{1,0:T(8,128)(2,1)S(1)} collective-permute-done((bf16[256,640]{1,0:T(8,128)(2,1)S(1)}, bf16[256,640]{1,0:T(8,128)(2,1)S(1)}, u32[]{:S(2)}, u32[]{:S(2)}) %collective-permute-start.31) | collective-permute-done | bytes 327712 | tf_op jit(solution)/shard_map/ppermute | solution.py:21
  195.7 2.9 collective-permute-done.32.refs_5_
  198.5 2.4 stack.31.refs_2_.ref.refs_0_
  207.1 8.1 %project_sum.1.refs_4_ = f32[1024,256]{1,0:T(8,128)} custom-call(bf16[2,1024,2560]{2,1,0:T(8,128)(2,1)} %get-tuple-element.34.refs_0_.refs_1_, bf16[2,1024,2560]{2,1,0:T(8,128)(2,1)} %get-tuple-element.34.refs_0_.refs_1_, bf16[4,256,640]{2,1,0:T(8,128)(2,1)} %stack.31.refs_2_.ref.refs_0_, bf16[4,256,640]{2,1,0:T(8,128)(2,1)} %collective-permute-done.34.refs_3_.refs_2_), custom_call_target="tpu_custom_call" | custom-call | flops 1024 | bytes 1024 | tf_op jit(solution)/shard_map/project_sum/pallas_call | solution.py:423
  215.2 3.7 %collective-permute-done.36.refs_9_ = bf16[256,640]{1,0:T(8,128)(2,1)} collective-permute-done((bf16[256,640]{1,0:T(8,128)(2,1)}, bf16[256,640]{1,0:T(8,128)(2,1)}, u32[]{:S(2)}, u32[]{:S(2)}) %collective-permute-start.36) | collective-permute-done | bytes 327712 | tf_op jit(solution)/shard_map/ppermute | solution.py:21
  218.9 2.5 stack.32.refs_2_.ref.refs_1_
  224.9 8.6 %project_grad.1.own_ref = bf16[1024,256]{1,0:T(8,128)(2,1)} custom-call(bf16[2,1024,2560]{2,1,0:T(8,128)(2,1)} %get-tuple-element.35.refs_0_.refs_1_, bf16[2,1024,2560]{2,1,0:T(8,128)(2,1)} %get-tuple-element.35.refs_0_.refs_1_, bf16[4,256,640]{2,1,0:T(8,128)(2,1)} %stack.32.refs_2_.ref.refs_1_, bf16[4,256,640]{2,1,0:T(8,128)(2,1)} %collective-permute-done.37.refs_3_, ...), custom_call_target="tpu_custom_call" | custom-call | flops 1024 | bytes 1024 | tf_op jit(solution)/shard_map/project_grad/pallas_call | solution.py:423
  239.5 4.8 %collective-permute-done.38.far_ref = bf16[512,256]{1,0:T(8,128)(2,1)S(1)} collective-permute-done((bf16[512,256]{1,0:T(8,128)(2,1)}, bf16[512,256]{1,0:T(8,128)(2,1)S(1)}, u32[]{:S(2)}, u32[]{:S(2)}) %collective-permute-start.38) | collective-permute-done | bytes 262176 | tf_op jit(solution)/shard_map/ppermute | solution.py:21
  249.8 13.6 %weight_grad.2 = bf16[512,2,5120]{2,1,0:T(2,128)(2,1)} custom-call(s32[3]{0:T(128)} %pad_add_fusion.place, f32[2]{0:T(128)} %add_rsqrt_fusion.refs_3_.scale_ref, bf16[1024,256]{1,0:T(8,128)(2,1)} %project_grad.1.own_ref, bf16[512,256]{1,0:T(8,128)(2,1)} %copy-done.20, bf16[4,4,256,640]{3,2,1,0:T(8,128)(2,1)} %bitcast.46, bf16[4,4,256,640]{3,2,1,0:T(8,128)(2,1)} %bitcast.47), custom_call_target="tpu_custom_call" | custom-call | flops 1024 | bytes 1024 | tf_op jit(solution)/shard_map/weight_grad/pallas_call | solution.py:582
  265.4 13.3 %weight_grad.3 = bf16[512,2,5120]{2,1,0:T(2,128)(2,1)} custom-call(s32[3]{0:T(128)} %pad_add_fusion.place, f32[2]{0:T(128)} %add_rsqrt_fusion.refs_3_.scale_ref, bf16[1024,256]{1,0:T(8,128)(2,1)} %get-tuple-element.55.own_ref, bf16[512,256]{1,0:T(8,128)(2,1)} %copy-done.19, bf16[4,256,640]{2,1,0:T(8,128)(2,1)} %stack.31.refs_2_.ref.refs_0_, ...), custom_call_target="tpu_custom_call" | custom-call | flops 1024 | bytes 1024 | tf_op jit(solution)/shard_map/weight_grad/pallas_call | solution.py:582
  (170 shorter events, 66.7 us)
Async XLA Ops:
  7.2 151.4 %all-gather.5.cloned.1.call-start = ((), (), s32[]{:S(2)}) async-start(), calls=%async_computation | async-start | bytes 6553600 | tf_op jit(solution)/shard_map/all_gather | solution.py:664
  8.2 25.0 %collective-permute-start = (bf16[256,640]{1,0:T(8,128)(2,1)S(1)}, bf16[256,640]{1,0:T(8,128)(2,1)}, u32[]{:S(2)}, u32[]{:S(2)}) collective-permute-start(bf16[256,640]{1,0:T(8,128)(2,1)S(1)} %bitcast.49), channel_id=1, source_target_pairs={{0,8},{4,12},{8,0},{12,4},{16,24},{20,28},{24,16},{28,20},{1,9},{5... | collective-permute-start | bytes 983048 | tf_op jit(solution)/shard_map/ppermute | solution.py:21
  11.3 21.9 %collective-permute-start.1 = (bf16[256,640]{1,0:T(8,128)(2,1)S(1)}, bf16[256,640]{1,0:T(8,128)(2,1)}, u32[]{:S(2)}, u32[]{:S(2)}) collective-permute-start(bf16[256,640]{1,0:T(8,128)(2,1)S(1)} %bitcast.50), channel_id=1, source_target_pairs={{0,16},{4,20},{8,24},{12,28},{16,0},{20,4},{24,8},{28,12},{1,17},{... | collective-permute-start | bytes 983048 | tf_op jit(solution)/shard_map/ppermute | solution.py:21
  13.9 19.3 %collective-permute-start.2 = (bf16[256,640]{1,0:T(8,128)(2,1)S(1)}, bf16[256,640]{1,0:T(8,128)(2,1)S(1)}, u32[]{:S(2)}, u32[]{:S(2)}) collective-permute-start(bf16[256,640]{1,0:T(8,128)(2,1)S(1)} %bitcast.51), channel_id=1, source_target_pairs={{0,4},{4,0},{8,12},{12,8},{16,20},{20,16},{24,28},{28,24},{1,5},{5... | collective-permute-start | bytes 983048 | tf_op jit(solution)/shard_map/ppermute | solution.py:21
  17.5 13.9 %collective-permute-start.3 = (bf16[128,1024]{1,0:T(8,128)(2,1)}, bf16[128,1024]{1,0:T(8,128)(2,1)}, u32[]{:S(2)}, u32[]{:S(2)}) collective-permute-start(bf16[128,1024]{1,0:T(8,128)(2,1)} %pad_maximum_fusion.1), channel_id=1, source_target_pairs={{0,1},{1,0},{2,3},{3,2},{4,5},{5,4},{6,7},{7,6},{8,9},{9,8},{10,11... | collective-permute-start | bytes 786440 | tf_op jit(solution)/shard_map/ppermute | solution.py:21
  33.2 15.6 %collective-permute-start.4 = (bf16[256,640]{1,0:T(8,128)(2,1)}, bf16[256,640]{1,0:T(8,128)(2,1)}, u32[]{:S(2)}, u32[]{:S(2)}) collective-permute-start(bf16[256,640]{1,0:T(8,128)(2,1)} %collective-permute-done.1.refs_2_), channel_id=1, source_target_pairs={{0,8},{4,12},{8,0},{12,4},{16,24},{20,28},{24,16},{28,20},{1,9},{5... | collective-permute-start | bytes 983048 | tf_op jit(solution)/shard_map/ppermute | solution.py:21
  33.8 15.0 %collective-permute-start.5 = (bf16[256,640]{1,0:T(8,128)(2,1)}, bf16[256,640]{1,0:T(8,128)(2,1)S(1)}, u32[]{:S(2)}, u32[]{:S(2)}) collective-permute-start(bf16[256,640]{1,0:T(8,128)(2,1)} %collective-permute-done.1.refs_2_), channel_id=1, source_target_pairs={{0,4},{4,0},{8,12},{12,8},{16,20},{20,16},{24,28},{28,24},{1,5},{5... | collective-permute-start | bytes 983048 | tf_op jit(solution)/shard_map/ppermute | solution.py:21
  34.3 16.6 %collective-permute-start.6 = (bf16[256,640]{1,0:T(8,128)(2,1)}, bf16[256,640]{1,0:T(8,128)(2,1)}, u32[]{:S(2)}, u32[]{:S(2)}) collective-permute-start(bf16[256,640]{1,0:T(8,128)(2,1)} %collective-permute-done.refs_1_), channel_id=1, source_target_pairs={{0,4},{4,0},{8,12},{12,8},{16,20},{20,16},{24,28},{28,24},{1,5},{5... | collective-permute-start | bytes 983048 | tf_op jit(solution)/shard_map/ppermute | solution.py:21
  53.4 105.2 %all-gather.7.cloned.1.call-start = ((), (), s32[]{:S(2)}) async-start(), calls=%async_computation.1 | async-start | bytes 6553600 | tf_op jit(solution)/shard_map/all_gather | solution.py:664
  53.5 16.0 %collective-permute-start.7 = (bf16[256,640]{1,0:T(8,128)(2,1)}, bf16[256,640]{1,0:T(8,128)(2,1)S(1)}, u32[]{:S(2)}, u32[]{:S(2)}) collective-permute-start(bf16[256,640]{1,0:T(8,128)(2,1)} %collective-permute-done.4.refs_3_), channel_id=1, source_target_pairs={{0,4},{4,0},{8,12},{12,8},{16,20},{20,16},{24,28},{28,24},{1,5},{5... | collective-permute-start | bytes 983048 | tf_op jit(solution)/shard_map/ppermute | solution.py:21
  107.8 17.7 %collective-permute-start.16 = (bf16[2,256,640]{2,1,0:T(8,128)(2,1)S(1)}, bf16[2,256,640]{2,1,0:T(8,128)(2,1)}, u32[]{:S(2)}, u32[]{:S(2)}) collective-permute-start(bf16[2,256,640]{2,1,0:T(8,128)(2,1)S(1)} %get-tuple-element.62), channel_id=1, source_target_pairs={{0,4},{4,0},{8,12},{12,8},{16,20},{20,16},{24,28},{28,24},{1,5},{5... | collective-permute-start | bytes 1966088 | tf_op jit(solution)/shard_map/ppermute | solution.py:21
  116.6 22.1 %collective-permute-start.14 = (bf16[2,256,640]{2,1,0:T(8,128)(2,1)}, bf16[2,256,640]{2,1,0:T(8,128)(2,1)S(1)}, u32[]{:S(2)}, u32[]{:S(2)}) collective-permute-start(bf16[2,256,640]{2,1,0:T(8,128)(2,1)} %get-tuple-element.61), channel_id=1, source_target_pairs={{0,4},{4,0},{8,12},{12,8},{16,20},{20,16},{24,28},{28,24},{1,5},{5... | collective-permute-start | bytes 1966088 | tf_op jit(solution)/shard_map/ppermute | solution.py:21
  128.9 14.8 %collective-permute-start.13 = (bf16[256,640]{1,0:T(8,128)(2,1)}, bf16[256,640]{1,0:T(8,128)(2,1)S(1)}, u32[]{:S(2)}, u32[]{:S(2)}) collective-permute-start(bf16[256,640]{1,0:T(8,128)(2,1)} %get-tuple-element.43), channel_id=1, source_target_pairs={{0,1},{1,0},{2,3},{3,2},{4,5},{5,4},{6,7},{7,6},{8,9},{9,8},{10,11... | collective-permute-start | bytes 983048 | tf_op jit(solution)/shard_map/ppermute | solution.py:21
  140.4 16.9 %collective-permute-start.21 = (bf16[256,640]{1,0:T(8,128)(2,1)S(1)}, bf16[256,640]{1,0:T(8,128)(2,1)S(1)}, u32[]{:S(2)}, u32[]{:S(2)}) collective-permute-start(bf16[256,640]{1,0:T(8,128)(2,1)S(1)} %get-tuple-element.60), channel_id=1, source_target_pairs={{0,16},{4,20},{8,24},{12,28},{16,0},{20,4},{24,8},{28,12},{1,17},{... | collective-permute-start | bytes 983048 | tf_op jit(solution)/shard_map/ppermute | solution.py:21
  140.4 16.8 %collective-permute-start.19 = (bf16[256,640]{1,0:T(8,128)(2,1)S(1)}, bf16[256,640]{1,0:T(8,128)(2,1)S(1)}, u32[]{:S(2)}, u32[]{:S(2)}) collective-permute-start(bf16[256,640]{1,0:T(8,128)(2,1)S(1)} %get-tuple-element.59), channel_id=1, source_target_pairs={{0,8},{4,12},{8,0},{12,4},{16,24},{20,28},{24,16},{28,20},{1,9},{5... | collective-permute-start | bytes 983048 | tf_op jit(solution)/shard_map/ppermute | solution.py:21
  142.1 16.4 %collective-permute-start.22 = (bf16[512,256]{1,0:T(8,128)(2,1)S(1)}, bf16[512,256]{1,0:T(8,128)(2,1)S(1)}, u32[]{:S(2)}, u32[]{:S(2)}) collective-permute-start(bf16[512,256]{1,0:T(8,128)(2,1)S(1)} %slice.48), channel_id=1, source_target_pairs={{0,2},{1,3},{2,0},{3,1},{4,6},{5,7},{6,4},{7,5},{8,10},{9,11},{10,... | collective-permute-start | bytes 786440 | tf_op jit(solution)/shard_map/ppermute | solution.py:21
  159.6 15.0 %collective-permute-start.24 = (bf16[256,640]{1,0:T(8,128)(2,1)S(1)}, bf16[256,640]{1,0:T(8,128)(2,1)S(1)}, u32[]{:S(2)}, u32[]{:S(2)}) collective-permute-start(bf16[256,640]{1,0:T(8,128)(2,1)S(1)} %bitcast.54), channel_id=1, source_target_pairs={{0,8},{4,12},{8,0},{12,4},{16,24},{20,28},{24,16},{28,20},{1,9},{5... | collective-permute-start | bytes 983048 | tf_op jit(solution)/shard_map/ppermute | solution.py:21
  159.6 16.3 %collective-permute-start.26 = (bf16[256,640]{1,0:T(8,128)(2,1)S(1)}, bf16[256,640]{1,0:T(8,128)(2,1)S(1)}, u32[]{:S(2)}, u32[]{:S(2)}) collective-permute-start(bf16[256,640]{1,0:T(8,128)(2,1)S(1)} %bitcast.55), channel_id=1, source_target_pairs={{0,16},{4,20},{8,24},{12,28},{16,0},{20,4},{24,8},{28,12},{1,17},{... | collective-permute-start | bytes 983048 | tf_op jit(solution)/shard_map/ppermute | solution.py:21
  178.7 16.2 %collective-permute-start.31 = (bf16[256,640]{1,0:T(8,128)(2,1)S(1)}, bf16[256,640]{1,0:T(8,128)(2,1)S(1)}, u32[]{:S(2)}, u32[]{:S(2)}) collective-permute-start(bf16[256,640]{1,0:T(8,128)(2,1)S(1)} %collective-permute-done.24.refs_1_), channel_id=1, source_target_pairs={{0,2},{1,3},{2,0},{3,1},{4,6},{5,7},{6,4},{7,5},{8,10},{9,11},{10,... | collective-permute-start | bytes 983048 | tf_op jit(solution)/shard_map/ppermute | solution.py:21
  179.5 19.1 %collective-permute-start.32 = (bf16[256,640]{1,0:T(8,128)(2,1)S(1)}, bf16[256,640]{1,0:T(8,128)(2,1)}, u32[]{:S(2)}, u32[]{:S(2)}) collective-permute-start(bf16[256,640]{1,0:T(8,128)(2,1)S(1)} %collective-permute-done.23.refs_0_), channel_id=1, source_target_pairs={{0,2},{1,3},{2,0},{3,1},{4,6},{5,7},{6,4},{7,5},{8,10},{9,11},{10,... | collective-permute-start | bytes 983048 | tf_op jit(solution)/shard_map/ppermute | solution.py:21
  201.0 14.2 %collective-permute-start.33 = (bf16[256,640]{1,0:T(8,128)(2,1)}, bf16[256,640]{1,0:T(8,128)(2,1)S(1)}, u32[]{:S(2)}, u32[]{:S(2)}) collective-permute-start(bf16[256,640]{1,0:T(8,128)(2,1)} %copy-done.10), channel_id=1, source_target_pairs={{0,4},{4,0},{8,12},{12,8},{16,20},{20,16},{24,28},{28,24},{1,5},{5... | collective-permute-start | bytes 983048 | tf_op jit(solution)/shard_map/ppermute | solution.py:21
  203.3 15.6 %collective-permute-start.36 = (bf16[256,640]{1,0:T(8,128)(2,1)}, bf16[256,640]{1,0:T(8,128)(2,1)}, u32[]{:S(2)}, u32[]{:S(2)}) collective-permute-start(bf16[256,640]{1,0:T(8,128)(2,1)} %copy-done.9), channel_id=1, source_target_pairs={{0,2},{1,3},{2,0},{3,1},{4,6},{5,7},{6,4},{7,5},{8,10},{9,11},{10,... | collective-permute-start | bytes 983048 | tf_op jit(solution)/shard_map/ppermute | solution.py:21
  203.7 15.2 %collective-permute-start.25 = (bf16[256,640]{1,0:T(8,128)(2,1)}, bf16[256,640]{1,0:T(8,128)(2,1)}, u32[]{:S(2)}, u32[]{:S(2)}) collective-permute-start(bf16[256,640]{1,0:T(8,128)(2,1)} %copy-done.7), channel_id=1, source_target_pairs={{0,4},{4,0},{8,12},{12,8},{16,20},{20,16},{24,28},{28,24},{1,5},{5... | collective-permute-start | bytes 983048 | tf_op jit(solution)/shard_map/ppermute | solution.py:21
  223.0 16.5 %collective-permute-start.40 = (bf16[256,640]{1,0:T(8,128)(2,1)}, bf16[256,640]{1,0:T(8,128)(2,1)}, u32[]{:S(2)}, u32[]{:S(2)}) collective-permute-start(bf16[256,640]{1,0:T(8,128)(2,1)} %copy-done.8), channel_id=1, source_target_pairs={{0,2},{1,3},{2,0},{3,1},{4,6},{5,7},{6,4},{7,5},{8,10},{9,11},{10,... | collective-permute-start | bytes 983048 | tf_op jit(solution)/shard_map/ppermute | solution.py:21
  223.5 23.6 %collective-permute-start.42 = (bf16[256,640]{1,0:T(8,128)(2,1)}, bf16[256,640]{1,0:T(8,128)(2,1)}, u32[]{:S(2)}, u32[]{:S(2)}) collective-permute-start(bf16[256,640]{1,0:T(8,128)(2,1)} %collective-permute-done.27.refs_4_), channel_id=1, source_target_pairs={{0,1},{1,0},{2,3},{3,2},{4,5},{5,4},{6,7},{7,6},{8,9},{9,8},{10,11... | collective-permute-start | bytes 983048 | tf_op jit(solution)/shard_map/ppermute | solution.py:21
  223.5 24.2 %collective-permute-start.43 = (bf16[256,640]{1,0:T(8,128)(2,1)}, bf16[256,640]{1,0:T(8,128)(2,1)}, u32[]{:S(2)}, u32[]{:S(2)}) collective-permute-start(bf16[256,640]{1,0:T(8,128)(2,1)} %collective-permute-done.32.refs_5_), channel_id=1, source_target_pairs={{0,1},{1,0},{2,3},{3,2},{4,5},{5,4},{6,7},{7,6},{8,9},{9,8},{10,11... | collective-permute-start | bytes 983048 | tf_op jit(solution)/shard_map/ppermute | solution.py:21
  224.7 22.9 %collective-permute-start.44 = (bf16[256,640]{1,0:T(8,128)(2,1)S(1)}, bf16[256,640]{1,0:T(8,128)(2,1)}, u32[]{:S(2)}, u32[]{:S(2)}) collective-permute-start(bf16[256,640]{1,0:T(8,128)(2,1)S(1)} %copy-done.17), channel_id=1, source_target_pairs={{0,1},{1,0},{2,3},{3,2},{4,5},{5,4},{6,7},{7,6},{8,9},{9,8},{10,11... | collective-permute-start | bytes 983048 | tf_op jit(solution)/shard_map/ppermute | solution.py:21
  247.1 17.6 %collective-permute-start.46 = (bf16[256,640]{1,0:T(8,128)(2,1)S(1)}, bf16[256,640]{1,0:T(8,128)(2,1)}, u32[]{:S(2)}, u32[]{:S(2)}) collective-permute-start(bf16[256,640]{1,0:T(8,128)(2,1)S(1)} %copy-done.15), channel_id=1, source_target_pairs={{0,1},{1,0},{2,3},{3,2},{4,5},{5,4},{6,7},{7,6},{8,9},{9,8},{10,11... | collective-permute-start | bytes 983048 | tf_op jit(solution)/shard_map/ppermute | solution.py:21
  247.1 17.6 %collective-permute-start.47 = (bf16[256,640]{1,0:T(8,128)(2,1)}, bf16[256,640]{1,0:T(8,128)(2,1)}, u32[]{:S(2)}, u32[]{:S(2)}) collective-permute-start(bf16[256,640]{1,0:T(8,128)(2,1)} %collective-permute-done.36.refs_9_), channel_id=1, source_target_pairs={{0,1},{1,0},{2,3},{3,2},{4,5},{5,4},{6,7},{7,6},{8,9},{9,8},{10,11... | collective-permute-start | bytes 983048 | tf_op jit(solution)/shard_map/ppermute | solution.py:21
  247.6 17.1 %collective-permute-start.48 = (bf16[256,640]{1,0:T(8,128)(2,1)}, bf16[256,640]{1,0:T(8,128)(2,1)}, u32[]{:S(2)}, u32[]{:S(2)}) collective-permute-start(bf16[256,640]{1,0:T(8,128)(2,1)} %collective-permute-done.35.refs_10_), channel_id=1, source_target_pairs={{0,1},{1,0},{2,3},{3,2},{4,5},{5,4},{6,7},{7,6},{8,9},{9,8},{10,11... | collective-permute-start | bytes 983048 | tf_op jit(solution)/shard_map/ppermute | solution.py:21
  247.7 17.0 %collective-permute-start.45 = (bf16[256,640]{1,0:T(8,128)(2,1)}, bf16[256,640]{1,0:T(8,128)(2,1)S(1)}, u32[]{:S(2)}, u32[]{:S(2)}) collective-permute-start(bf16[256,640]{1,0:T(8,128)(2,1)} %collective-permute-done.39.refs_7_), channel_id=1, source_target_pairs={{0,1},{1,0},{2,3},{3,2},{4,5},{5,4},{6,7},{7,6},{8,9},{9,8},{10,11... | collective-permute-start | bytes 983048 | tf_op jit(solution)/shard_map/ppermute | solution.py:21
  249.2 15.5 %collective-permute-start.49 = (bf16[256,640]{1,0:T(8,128)(2,1)}, bf16[256,640]{1,0:T(8,128)(2,1)}, u32[]{:S(2)}, u32[]{:S(2)}) collective-permute-start(bf16[256,640]{1,0:T(8,128)(2,1)} %collective-permute-done.40.refs_11_), channel_id=1, source_target_pairs={{0,1},{1,0},{2,3},{3,2},{4,5},{5,4},{6,7},{7,6},{8,9},{9,8},{10,11... | collective-permute-start | bytes 983048 | tf_op jit(solution)/shard_map/ppermute | solution.py:21
  (46 other events, 679.8 us)
Sparse Core Ops, SparseCore 0:
  53.5 38.9 all-gather.4
  94.0 40.4 all-gather.6

commit v2 on v1

--- a/solution.py
+++ b/solution.py
@@ -25,12 +25,14 @@
     return lax.optimization_barrier((value, *others))[0]
 
 
-def sum_tokens(value):
-    step = 1
-    while step < lax.axis_size("tok"):
-        value = value + exchange(value, "tok", step)
-        step *= 2
-    return value
+def sums_over(value, axis):
+    sums = []
+    step = lax.axis_size(axis) // 2
+    while step:
+        value = value + exchange(value, axis, step)
+        sums.append(value)
+        step //= 2
+    return sums
 
 
 def squares_kernel(ref, out_ref):
@@ -94,9 +96,6 @@
                 early.append(crossed[k | 1])
         if step < count // 2:
             if over_tok:
-                for k in (count // 2, step):
-                    far[k] = exchange(held.get(k, direct[k]), "tok", 2)
-                    early.append(far[k])
                 early.append(far[1])
             else:
                 crossed[step | 1] = exchange(direct[step], "lat", 1)
@@ -394,11 +393,22 @@
     if mode == "sum":
         rest[0][...] = parts[0] + parts[1]
     else:
-        mask_ref, grad_ref = rest
         total = parts[0] + parts[1]
         for ref in sums:
             total = total + ref[...]
-        grad_ref[...] = (mask_ref[...].astype(F32).T * total).astype(BF16)
+        grad = (rest[0][...].astype(F32).T * total).astype(BF16)
+        if len(rest) == 2:
+            rest[1][...] = grad
+        else:
+            own = 2 * pl.program_id(0) < pl.num_programs(0)
+
+            @pl.when(own)
+            def _():
+                rest[1][...] = grad
+
+            @pl.when(jnp.logical_not(own))
+            def _():
+                rest[2][...] = grad
 
 
 def project(matrix, own, near, mode, sums=(), mask=None):
@@ -415,14 +425,22 @@
     in_specs = [layer(l) for l in range(layers)] + [whole] * 2
     in_specs += [flat] * len(sums)
     args = [matrix] * layers + [own, near, *sums]
+    steps = latents // rows
+    out_specs = flat
+    out_shape = jax.ShapeDtypeStruct((latents, tokens), BF16 if mode == "grad" else F32)
     if mode == "grad":
         in_specs.append(across)
         args.append(mask)
-    out_specs = flat
-    out_shape = jax.ShapeDtypeStruct((latents, tokens), BF16 if mode == "grad" else F32)
-    return pl.pallas_call(
+        if steps > 1:
+            middle = steps // 2
+            out_specs = (
+                pl.BlockSpec((rows, tokens), lambda i: (jnp.minimum(i, middle - 1), 0)),
+                pl.BlockSpec((rows, tokens), lambda i: (jnp.maximum(i, middle) - middle, 0)),
+            )
+            out_shape = (jax.ShapeDtypeStruct((latents // 2, tokens), BF16),) * 2
+    out = pl.pallas_call(
         functools.partial(project_kernel, layers=layers, mode=mode, earlier=len(sums)),
-        grid=(latents // rows,),
+        grid=(steps,),
         in_specs=in_specs,
         out_specs=out_specs,
         scratch_shapes=[pltpu.VMEM((layers, tokens, width), BF16)],
@@ -431,6 +449,9 @@
         cost_estimate=SMALL,
         name="project_" + mode,
     )(*args)
+    if mode == "grad" and steps == 1:
+        return out[:latents // 2], out[latents // 2:]
+    return out
 
 
 def recon_kernel(act_ref, *refs, parts):
@@ -634,29 +655,29 @@
     mask = jnp.concatenate([run_slices(mask_low, 0, 1), mask_far], axis=0)
     bias = run_slices(enc_bias.reshape(-1, 1), 0, 0)
 
-    def gather_halves(own, multiply, beside=(), over_tok=False):
+    def gather_halves(own, multiply, beside=(), over_tok=False, hops=()):
         blocks, far = gather_features(own, beside, over_tok)
         first = stack([blocks[k] for k in halves[0]])
         first_near = exchange(first, "tok", 1)
-        sums = multiply(first, first_near)
-        squared = squares(first, layers)
-        early = [sums, squared]
-        if over_tok:
-            early += [far[k] for k in (6, 5)]
+        early = [far[4], far[2]] if over_tok else hops[:1]
+        sums = multiply(first, after(first_near, *early))
         final = halves[1][-1]
-        blocks[final] = after(blocks[final], *early)
+        blocks[final] = after(blocks[final], sums, *hops[1:])
         second = stack([blocks[k] for k in halves[1]])
         near = [first_near, exchange(second, "tok", 1)]
-        return [first, second], near, sums, squared, far
+        return [first, second], near, sums, far
 
     dec_first = rearrange(dec_weight, spot, halves, runs, 0)
     dec_halves = rearrange(dec_weight, spot, halves, runs, 1, dec_first)
-    x_own, x_near, sums, squared, _ = gather_halves(
+    hops = sums_over(jnp.sum(own_f * own_f, axis=(1, 2)), "tok")[-1:]
+    hops += sums_over(hops[0], "lat")
+    square_sums = hops[-1]
+    x_own, x_near, sums, _ = gather_halves(
         own_x,
         lambda own, near: encode(enc_weight, halves[0], own, near, spot, "parts"),
-        beside=([*dec_first, mask, bias], dec_halves),
-    )
-    square_sums = jnp.sum(sum_tokens(squared + squares(x_own[1], layers)), axis=(1, 2))
+        beside=([*dec_first, mask, bias, hops[0]], [*dec_halves, hops[1]]),
+        hops=hops[-2:],
+    )
     norm_scale = lax.rsqrt(square_sums / (tokens * full_width) + 1e-06)
     act_across, act = encode(
         enc_weight, halves[1], x_own[1], x_near[1], spot, "act", [sums], norm_scale, bias, mask
@@ -677,16 +698,19 @@
     act_far = exchange(act[quarter:], "tok", 2)
     if aligned:
         pieces = {}
-        received = None
+        summed = None
         for start, bundle in zip(starts, bundles):
-            if received is not None:
-                bundle = after(bundle, received)
+            if summed is not None:
+                bundle = after(bundle, summed)
             low, high = [
                 keep[i] + send[i].astype(F32) + bundle[i - start].astype(F32)
                 for i in (start, start + 1)
             ]
             received = exchange(high.astype(BF16), "lat", 2)
-            pieces[2 * start] = low + received.astype(F32)
+            summed = low + received.astype(F32)
+            if start:
+                summed = summed.astype(BF16)
+            pieces[2 * start] = summed
         recon = scatter_features(pieces)
     else:
         own = keep + jnp.stack(send).astype(F32)
@@ -699,12 +723,14 @@
     diff = recon - norm_scale[:, None, None] * own_f
     factor = LOSS_SCALE / tokens
     err_low = (diff * factor).astype(BF16).reshape(layers * tok_dev, width_part)
-    err_own, err_near, sums, squared, far = gather_halves(
+    err_own, err_near, sums, far = gather_halves(
         err_low, lambda own, near: project(dec_halves[0], own, near, "sum"), over_tok=True
     )
-    grad = project(dec_halves[1], err_own[1], err_near[1], "grad", [sums], mask=mask)
-    grad_far = exchange(grad[quarter:], "tok", 2)
-    error_sums = squared + squares(err_own[1], layers)
+    squared = squares(err_own[0], layers) + squares(err_own[1], layers)
+    second_near = after(err_near[1], far[6], far[5], squared)
+    grad, grad_away = project(dec_halves[1], err_own[1], second_near, "grad", [sums], mask=mask)
+    grad_far = exchange(grad_away, "tok", 2)
+    error_sums = sums_over(squared, "tok")[-1]
     soon = [k for k in range(block_count) if k not in (3, 7)]
     last = {k: exchange(far[k], "tok", 1) for k in soon}
     grad_far, error_sums, far[3], far[7] = lax.optimization_barrier(
@@ -718,16 +744,14 @@
         grad, grad_far, x_all, [(None, spot) for spot in order] * tok_count, place,
         norm_scale, True, shape,
     )
-    error_sums = error_sums + exchange(error_sums, "tok", 1)
-    act, error_sums = lax.optimization_barrier((act, error_sums))
+    act = after(act, enc_grad)
     for k in (3, 7):
         last[k] = exchange(far[k], "tok", 1)
     where = [(2 * g + h, i) for g in range(2) for h, i in order]
     where += [(4 + g * block_count + k, -1) for g in range(2) for k in range(block_count)]
     sources = err_own + err_near + [group[k] for group in (far, last) for k in range(block_count)]
     dec_grad = weight_grad(act, act_far, sources, where, place, norm_scale, False, shape)
-    error_sum = jnp.sum(error_sums + exchange(error_sums, "tok", 2))
-    mean_error = error_sum / (factor * factor * tokens * layers * full_width)
+    mean_error = jnp.sum(error_sums) / (factor * factor * tokens * layers * full_width)
     return (enc_grad, dec_grad, mean_error)
 
 

time: 288 us -> 312 us (1.083)
  waiting for transfers between devices: 79.6 us -> 98.3 us
  starting transfers between devices: 41.1 us -> 47.6 us
  Pallas kernels: 128 us -> 124 us
  other arithmetic: 14.3 us -> 18.1 us
    ppermute x51 -> x54, waiting for transfers between devices: 79.5 us -> 98.2 us  [exchange(): return lax.ppermute(value, axis, [(i, i ^ mask) for i in range(size)])]
    ppermute x51 -> x54, starting transfers between devices: 41 us -> 47.3 us  [exchange(): return lax.ppermute(value, axis, [(i, i ^ mask) for i in range(size)])]
    pallas_call x4 -> x2, Pallas kernels: 8.09 us -> 4.04 us  [squares(): pl.pallas_call(squares_kernel, out_shape=jax.ShapeDtypeStruct((layers, 8,...]
  transfers between devices with their start and end apart: 53 -> 56, of which waited for: 22 -> 22; matrix products, arithmetic and copies ran while one was open for 6% -> 6% of each run, Pallas kernels for 38% -> 33%
where the time goes in v2:
time: 312 us; the launch traced here: 311 us
  Pallas kernels  124 us (40%)
  waiting for transfers between devices  98.3 us (32%)
  starting transfers between devices  47.6 us (15%)
  other arithmetic  18.1 us (6%)
  between operations  16.2 us (5%)
  local copies, waits for them, and re-layouts  7.19 us (2%)
    ppermute x54, waiting for transfers between devices, exchange(): return lax.ppermute(value, axis, [(i, i ^ mask) for i in range(size)])  98.2 us
    ppermute x54, starting transfers between devices, exchange(): return lax.ppermute(value, axis, [(i, i ^ mask) for i in range(size)])  47.3 us
    pallas_call x2, Pallas kernels, weight_grad(): pl.pallas_call(functools.partial(grad_kernel, groups=groups, where=where,...  26.9 us
    pallas_call x2, Pallas kernels, rearrange(): pl.pallas_call(functools.partial(rearrange_kernel, halves=halves, count=c...  26.1 us
    pallas_call x2, Pallas kernels, encode(): pl.pallas_call(functools.partial(encode_kernel, half=half, mode=mode, ear...  24 us
    pallas_call x2, Pallas kernels, project(): pl.pallas_call(functools.partial(project_kernel, layers=layers, mode=mode...  16.8 us
    pallas_call x2, Pallas kernels, recon_half(): pl.pallas_call(functools.partial(recon_kernel, parts=parts), grid=(blocks...  16.1 us
    pallas_call x4, Pallas kernels, stack(): pl.pallas_call(stack_kernel, out_shape=jax.ShapeDtypeStruct((len(blocks),...  9.9 us
  transfers between devices with their start and end apart: 56, of which 22 were waited for; matrix products, arithmetic and copies ran while one was open for 6% of the time, Pallas kernels for 33%

profile of v2, /device:TPU:0, one launch (start us, length us, event | category | flops | bytes accessed | tf_op | source)
XLA Modules:
  0.0 311.3 jit_solution(8672406579344365489)
XLA Ops:
  8.2 4.1 %collective-permute-start.8 = (bf16[256,640]{1,0:T(8,128)(2,1)S(1)}, bf16[256,640]{1,0:T(8,128)(2,1)}, u32[]{:S(2)}, u32[]{:S(2)}) collective-permute-start(bf16[256,640]{1,0:T(8,128)(2,1)S(1)} %bitcast.50), channel_id=1, source_target_pairs={{0,16},{4,20},{8,24},{12,28},{16,0},{20,4},{24,8},{28,12},{1,17},{... | collective-permute-start | bytes 983048 | tf_op jit(solution)/shard_map/ppermute | solution.py:21
  20.8 13.1 %rearrange.2 = (bf16[2,1024,2560]{2,1,0:T(8,128)(2,1)}, bf16[2,1024,2560]{2,1,0:T(8,128)(2,1)}) custom-call(s32[2]{0:T(128)} %pad_add_fusion.1.place, bf16[2048,2,5120]{2,1,0:T(2,128)(2,1)} %refs_1_.3, bf16[2048,2,5120]{2,1,0:T(2,128)(2,1)} %refs_1_.3), custom_call_target="tpu_custom_call" | custom-call | flops 1024 | bytes 1024 | tf_op jit(solution)/shard_map/rearrange/pallas_call | solution.py:351
  40.2 6.9 %collective-permute-done.2 = f32[2]{0:T(128)S(1)} collective-permute-done((f32[2]{0:T(128)S(1)}, f32[2]{0:T(128)S(1)}, u32[]{:S(2)}, u32[]{:S(2)}) %collective-permute-start.2) | collective-permute-done | bytes 40 | tf_op jit(solution)/shard_map/ppermute | solution.py:21
  47.1 13.0 %rearrange.3 = (bf16[2,1024,2560]{2,1,0:T(8,128)(2,1)}, bf16[2,1024,2560]{2,1,0:T(8,128)(2,1)}) custom-call(s32[2]{0:T(128)} %pad_add_fusion.1.place, bf16[2048,2,5120]{2,1,0:T(2,128)(2,1)} %refs_1_.3, bf16[2048,2,5120]{2,1,0:T(2,128)(2,1)} %refs_1_.3, ...), custom_call_target="tpu_custom_call", output_to_operand_aliasing={{0}: (3, {}), {1}: (4, {})} | custom-call | flops 1024 | bytes 1024 | tf_op jit(solution)/shard_map/rearrange/pallas_call | solution.py:351
  60.1 2.5 stack.29.refs_0_
  68.8 4.5 %collective-permute-done.4 = f32[2]{0:T(128)S(1)} collective-permute-done((f32[2]{0:T(128)S(1)}, f32[2]{0:T(128)S(1)}, u32[]{:S(2)}, u32[]{:S(2)}) %collective-permute-start.4) | collective-permute-done | bytes 40 | tf_op jit(solution)/shard_map/ppermute | solution.py:21
  73.9 11.7 %encode_parts.1.refs_2_ = f32[2,1024,256]{2,1,0:T(8,128)} custom-call(s32[2]{0:T(128)} %pad_add_fusion.1.place, bf16[2048,2,5120]{2,1,0:T(2,128)(2,1)} %w_ref.3, bf16[4,256,640]{2,1,0:T(8,128)(2,1)} %stack.29.refs_0_, bf16[4,256,640]{2,1,0:T(8,128)(2,1)} %collective-permute-done.13.refs_1_), custom_call_target="tpu_custom_call" | custom-call | flops 1024 | bytes 1024 | tf_op jit(solution)/shard_map/encode_parts/pallas_call | solution.py:294
  86.4 2.4 stack.30.refs_0_
  90.0 2.3 collective-permute-done.14.refs_1_
  92.3 12.3 %encode_act.1 = (bf16[256,1024]{1,0:T(8,128)(2,1)}, bf16[1024,256]{1,0:T(8,128)(2,1)}) custom-call(s32[2]{0:T(128)} %pad_add_fusion.1.place, bf16[2048,2,5120]{2,1,0:T(2,128)(2,1)} %w_ref.3, bf16[4,256,640]{2,1,0:T(8,128)(2,1)} %stack.30.refs_0_, bf16[4,256,640]{2,1,0:T(8,128)(2,1)} %collective-permute-done.14.refs_1_, f32[2,1024,256]{2,1,0:T(8,128)} %encode_parts.1.refs_2_, ...), custom_call_target="tpu_custom_call" | custom-call | flops 1024 | bytes 1024 | tf_op jit(solution)/shard_map/encode_act/pallas_call | solution.py:294
  104.6 8.2 %recon_half.2 = (f32[4,256,640]{2,1,0:T(8,128)}, bf16[4,256,640]{2,1,0:T(8,128)(2,1)}) custom-call(bf16[256,1024]{1,0:T(8,128)(2,1)} %get-tuple-element.46.act_ref, bf16[2,1024,2560]{2,1,0:T(8,128)(2,1)} %get-tuple-element.37.refs_0_.refs_1_, bf16[2,1024,2560]{2,1,0:T(8,128)(2,1)} %get-tuple-element.37.refs_0_.refs_1_), custom_call_target="tpu_custom_call" | custom-call | flops 1024 | bytes 1024 | tf_op jit(solution)/shard_map/recon_half/pallas_call | solution.py:507
  112.9 4.3 %collective-permute-done.15 = bf16[4,256,640]{2,1,0:T(8,128)(2,1)S(1)} collective-permute-done((bf16[4,256,640]{2,1,0:T(8,128)(2,1)}, bf16[4,256,640]{2,1,0:T(8,128)(2,1)S(1)}, u32[]{:S(2)}, u32[]{:S(2)}) %collective-permute-start.15) | collective-permute-done | bytes 1310752 | tf_op jit(solution)/shard_map/ppermute | solution.py:21
  120.5 8.0 %recon_half.3 = (f32[4,256,640]{2,1,0:T(8,128)}, bf16[256,640]{1,0:T(8,128)(2,1)}, bf16[256,640]{1,0:T(8,128)(2,1)}, bf16[256,640]{1,0:T(8,128)(2,1)}, bf16[256,640]{1,0:T(8,128)(2,1)}) custom-call(bf16[256,1024]{1,0:T(8,128)(2,1)} %get-tuple-element.46.act_ref, bf16[2,1024,2560]{2,1,0:T(8,128)(2,1)} %get-tuple-element.39.refs_0_.refs_1_, ...), custom_call_target="tpu_custom_call" | custom-call | flops 1024 | bytes 1024 | tf_op jit(solution)/shard_map/recon_half/pallas_call | solution.py:507
  130.8 7.6 %collective-permute-done.19 = bf16[2,256,640]{2,1,0:T(8,128)(2,1)} collective-permute-done((bf16[2,256,640]{2,1,0:T(8,128)(2,1)}, bf16[2,256,640]{2,1,0:T(8,128)(2,1)}, u32[]{:S(2)}, u32[]{:S(2)}) %collective-permute-start.19) | collective-permute-done | bytes 655392 | tf_op jit(solution)/shard_map/ppermute | solution.py:21
  142.0 6.4 %collective-permute-done.21 = bf16[256,640]{1,0:T(8,128)(2,1)S(1)} collective-permute-done((bf16[256,640]{1,0:T(8,128)(2,1)S(1)}, bf16[256,640]{1,0:T(8,128)(2,1)S(1)}, u32[]{:S(2)}, u32[]{:S(2)}) %collective-permute-start.21) | collective-permute-done | bytes 327712 | tf_op jit(solution)/shard_map/ppermute | solution.py:21
  150.5 2.7 collective-permute-start.24
  156.6 10.0 %collective-permute-done.24 = bf16[256,640]{1,0:T(8,128)(2,1)} collective-permute-done((bf16[256,640]{1,0:T(8,128)(2,1)}, bf16[256,640]{1,0:T(8,128)(2,1)}, u32[]{:S(2)}, u32[]{:S(2)}) %collective-permute-start.24) | collective-permute-done | bytes 327712 | tf_op jit(solution)/shard_map/ppermute | solution.py:21
  173.1 3.4 %collective-permute-start.29 = (bf16[256,640]{1,0:T(8,128)(2,1)S(1)}, bf16[256,640]{1,0:T(8,128)(2,1)S(1)}, u32[]{:S(2)}, u32[]{:S(2)}) collective-permute-start(bf16[256,640]{1,0:T(8,128)(2,1)S(1)} %bitcast.56), channel_id=1, source_target_pairs={{0,16},{4,20},{8,24},{12,28},{16,0},{20,4},{24,8},{28,12},{1,17},{... | collective-permute-start | bytes 983048 | tf_op jit(solution)/shard_map/ppermute | solution.py:21
  179.6 6.7 %collective-permute-done.27.refs_1_ = bf16[256,640]{1,0:T(8,128)(2,1)S(1)} collective-permute-done((bf16[256,640]{1,0:T(8,128)(2,1)S(1)}, bf16[256,640]{1,0:T(8,128)(2,1)S(1)}, u32[]{:S(2)}, u32[]{:S(2)}) %collective-permute-start.27) | collective-permute-done | bytes 327712 | tf_op jit(solution)/shard_map/ppermute | solution.py:21
  186.3 3.4 %collective-permute-done.29.refs_2_ = bf16[256,640]{1,0:T(8,128)(2,1)S(1)} collective-permute-done((bf16[256,640]{1,0:T(8,128)(2,1)S(1)}, bf16[256,640]{1,0:T(8,128)(2,1)S(1)}, u32[]{:S(2)}, u32[]{:S(2)}) %collective-permute-start.29) | collective-permute-done | bytes 327712 | tf_op jit(solution)/shard_map/ppermute | solution.py:21
  192.7 4.1 %collective-permute-done.31.refs_2_ = bf16[256,640]{1,0:T(8,128)(2,1)S(1)} collective-permute-done((bf16[256,640]{1,0:T(8,128)(2,1)S(1)}, bf16[256,640]{1,0:T(8,128)(2,1)S(1)}, u32[]{:S(2)}, u32[]{:S(2)}) %collective-permute-start.31) | collective-permute-done | bytes 327712 | tf_op jit(solution)/shard_map/ppermute | solution.py:21
  198.2 2.5 stack.31.refs_2_.ref.refs_0_
  204.7 6.8 %collective-permute-done.36.refs_8_ = bf16[256,640]{1,0:T(8,128)(2,1)} collective-permute-done((bf16[256,640]{1,0:T(8,128)(2,1)}, bf16[256,640]{1,0:T(8,128)(2,1)}, u32[]{:S(2)}, u32[]{:S(2)}) %collective-permute-start.36) | collective-permute-done | bytes 327712 | tf_op jit(solution)/shard_map/ppermute | solution.py:21
  211.6 6.8 %collective-permute-done.37.refs_6_ = bf16[256,640]{1,0:T(8,128)(2,1)} collective-permute-done((bf16[256,640]{1,0:T(8,128)(2,1)}, bf16[256,640]{1,0:T(8,128)(2,1)}, u32[]{:S(2)}, u32[]{:S(2)}) %collective-permute-start.37) | collective-permute-done | bytes 327712 | tf_op jit(solution)/shard_map/ppermute | solution.py:21
  218.4 8.1 %project_sum.1.refs_4_ = f32[1024,256]{1,0:T(8,128)} custom-call(bf16[2,1024,2560]{2,1,0:T(8,128)(2,1)} %get-tuple-element.39.refs_0_.refs_1_, bf16[2,1024,2560]{2,1,0:T(8,128)(2,1)} %get-tuple-element.39.refs_0_.refs_1_, bf16[4,256,640]{2,1,0:T(8,128)(2,1)} %stack.31.refs_2_.ref.refs_0_, bf16[4,256,640]{2,1,0:T(8,128)(2,1)} %collective-permute-done.35.refs_3_.refs_2_), custom_call_target="tpu_custom_call" | custom-call | flops 1024 | bytes 1024 | tf_op jit(solution)/shard_map/project_sum/pallas_call | solution.py:441
  227.2 2.4 stack.32.ref.refs_2_.refs_1_
  242.2 5.3 %collective-permute-done.40.refs_9_ = bf16[256,640]{1,0:T(8,128)(2,1)} collective-permute-done((bf16[256,640]{1,0:T(8,128)(2,1)S(1)}, bf16[256,640]{1,0:T(8,128)(2,1)}, u32[]{:S(2)}, u32[]{:S(2)}) %collective-permute-start.40) | collective-permute-done | bytes 327712 | tf_op jit(solution)/shard_map/ppermute | solution.py:21
  247.5 7.0 %collective-permute-done.44.refs_7_ = bf16[256,640]{1,0:T(8,128)(2,1)} collective-permute-done((bf16[256,640]{1,0:T(8,128)(2,1)}, bf16[256,640]{1,0:T(8,128)(2,1)}, u32[]{:S(2)}, u32[]{:S(2)}) %collective-permute-start.44) | collective-permute-done | bytes 327712 | tf_op jit(solution)/shard_map/ppermute | solution.py:21
  255.2 8.7 %project_grad.1 = (bf16[512,256]{1,0:T(8,128)(2,1)}, bf16[512,256]{1,0:T(8,128)(2,1)}) custom-call(bf16[2,1024,2560]{2,1,0:T(8,128)(2,1)} %get-tuple-element.37.refs_0_.refs_1_, bf16[2,1024,2560]{2,1,0:T(8,128)(2,1)} %get-tuple-element.37.refs_0_.refs_1_, bf16[4,256,640]{2,1,0:T(8,128)(2,1)} %stack.32.ref.refs_2_.refs_1_, ...), custom_call_target="tpu_custom_call" | custom-call | flops 1024 | bytes 1024 | tf_op jit(solution)/shard_map/project_grad/pallas_call | solution.py:441
  265.8 7.0 %collective-permute-done.41.far_ref = bf16[512,256]{1,0:T(8,128)(2,1)S(1)} collective-permute-done((bf16[512,256]{1,0:T(8,128)(2,1)}, bf16[512,256]{1,0:T(8,128)(2,1)S(1)}, u32[]{:S(2)}, u32[]{:S(2)}) %collective-permute-start.41) | collective-permute-done | bytes 262176 | tf_op jit(solution)/shard_map/ppermute | solution.py:21
  274.4 13.6 %weight_grad.2 = bf16[512,2,5120]{2,1,0:T(2,128)(2,1)} custom-call(s32[3]{0:T(128)} %pad_add_fusion.place, f32[2]{0:T(128)} %add_rsqrt_fusion, bf16[512,256]{1,0:T(8,128)(2,1)} %get-tuple-element.60.own_ref, bf16[512,256]{1,0:T(8,128)(2,1)} %copy-done.22, bf16[4,4,256,640]{3,2,1,0:T(8,128)(2,1)} %bitcast.47, bf16[4,4,256,640]{3,2,1,0:T(8,128)(2,1)} %bitcast.48), custom_call_target="tpu_custom_call" | custom-call | flops 1024 | bytes 1024 | tf_op jit(solution)/shard_map/weight_grad/pallas_call | solution.py:603
  290.0 13.3 %weight_grad.3 = bf16[512,2,5120]{2,1,0:T(2,128)(2,1)} custom-call(s32[3]{0:T(128)} %pad_add_fusion.place, f32[2]{0:T(128)} %add_rsqrt_fusion, bf16[1024,256]{1,0:T(8,128)(2,1)} %get-tuple-element.63.own_ref, bf16[512,256]{1,0:T(8,128)(2,1)} %copy-done.21, bf16[4,256,640]{2,1,0:T(8,128)(2,1)} %stack.31.refs_2_.ref.refs_0_, ...), custom_call_target="tpu_custom_call" | custom-call | flops 1024 | bytes 1024 | tf_op jit(solution)/shard_map/weight_grad/pallas_call | solution.py:603
  (177 shorter events, 76.1 us)
Async XLA Ops:
  7.2 163.9 %all-gather.5.cloned.1.call-start = ((), (), s32[]{:S(2)}) async-start(), calls=%async_computation | async-start | bytes 6553600 | tf_op jit(solution)/shard_map/all_gather | solution.py:685
  8.2 29.1 %collective-permute-start.8 = (bf16[256,640]{1,0:T(8,128)(2,1)S(1)}, bf16[256,640]{1,0:T(8,128)(2,1)}, u32[]{:S(2)}, u32[]{:S(2)}) collective-permute-start(bf16[256,640]{1,0:T(8,128)(2,1)S(1)} %bitcast.50), channel_id=1, source_target_pairs={{0,16},{4,20},{8,24},{12,28},{16,0},{20,4},{24,8},{28,12},{1,17},{... | collective-permute-start | bytes 983048 | tf_op jit(solution)/shard_map/ppermute | solution.py:21
  12.4 25.0 %collective-permute-start.6 = (bf16[256,640]{1,0:T(8,128)(2,1)S(1)}, bf16[256,640]{1,0:T(8,128)(2,1)}, u32[]{:S(2)}, u32[]{:S(2)}) collective-permute-start(bf16[256,640]{1,0:T(8,128)(2,1)S(1)} %bitcast.51), channel_id=1, source_target_pairs={{0,8},{4,12},{8,0},{12,4},{16,24},{20,28},{24,16},{28,20},{1,9},{5... | collective-permute-start | bytes 983048 | tf_op jit(solution)/shard_map/ppermute | solution.py:21
  13.9 23.4 %collective-permute-start.5 = (bf16[256,640]{1,0:T(8,128)(2,1)S(1)}, bf16[256,640]{1,0:T(8,128)(2,1)S(1)}, u32[]{:S(2)}, u32[]{:S(2)}) collective-permute-start(bf16[256,640]{1,0:T(8,128)(2,1)S(1)} %bitcast.52), channel_id=1, source_target_pairs={{0,4},{4,0},{8,12},{12,8},{16,20},{20,16},{24,28},{28,24},{1,5},{5... | collective-permute-start | bytes 983048 | tf_op jit(solution)/shard_map/ppermute | solution.py:21
  16.6 17.5 %collective-permute-start = (f32[2]{0:T(128)S(1)}, f32[2]{0:T(128)S(1)}, u32[]{:S(2)}, u32[]{:S(2)}) collective-permute-start(f32[2]{0:T(128)S(1)} %fusion), channel_id=1, source_target_pairs={{0,2},{1,3},{2,0},{3,1},{4,6},{5,7},{6,4},{7,5},{8,10},{9,11},{10,... | collective-permute-start | bytes 32 | tf_op jit(solution)/shard_map/ppermute | solution.py:21
  37.3 22.8 %collective-permute-start.7 = (bf16[256,640]{1,0:T(8,128)(2,1)}, bf16[256,640]{1,0:T(8,128)(2,1)S(1)}, u32[]{:S(2)}, u32[]{:S(2)}) collective-permute-start(bf16[256,640]{1,0:T(8,128)(2,1)} %collective-permute-done.6.refs_1_), channel_id=1, source_target_pairs={{0,4},{4,0},{8,12},{12,8},{16,20},{20,16},{24,28},{28,24},{1,5},{5... | collective-permute-start | bytes 983048 | tf_op jit(solution)/shard_map/ppermute | solution.py:21
  37.9 22.2 %collective-permute-start.10 = (bf16[256,640]{1,0:T(8,128)(2,1)}, bf16[256,640]{1,0:T(8,128)(2,1)}, u32[]{:S(2)}, u32[]{:S(2)}) collective-permute-start(bf16[256,640]{1,0:T(8,128)(2,1)} %collective-permute-done.8.refs_2_), channel_id=1, source_target_pairs={{0,4},{4,0},{8,12},{12,8},{16,20},{20,16},{24,28},{28,24},{1,5},{5... | collective-permute-start | bytes 983048 | tf_op jit(solution)/shard_map/ppermute | solution.py:21
  39.4 20.7 %collective-permute-start.11 = (bf16[256,640]{1,0:T(8,128)(2,1)}, bf16[256,640]{1,0:T(8,128)(2,1)}, u32[]{:S(2)}, u32[]{:S(2)}) collective-permute-start(bf16[256,640]{1,0:T(8,128)(2,1)} %collective-permute-done.8.refs_2_), channel_id=1, source_target_pairs={{0,8},{4,12},{8,0},{12,4},{16,24},{20,28},{24,16},{28,20},{1,9},{5... | collective-permute-start | bytes 983048 | tf_op jit(solution)/shard_map/ppermute | solution.py:21
  62.7 108.4 %all-gather.7.cloned.1.call-start = ((), (), s32[]{:S(2)}) async-start(), calls=%async_computation.1 | async-start | bytes 6553600 | tf_op jit(solution)/shard_map/all_gather | solution.py:685
  63.0 22.7 %collective-permute-start.12 = (bf16[256,640]{1,0:T(8,128)(2,1)}, bf16[256,640]{1,0:T(8,128)(2,1)S(1)}, u32[]{:S(2)}, u32[]{:S(2)}) collective-permute-start(bf16[256,640]{1,0:T(8,128)(2,1)} %collective-permute-done.11.refs_3_), channel_id=1, source_target_pairs={{0,4},{4,0},{8,12},{12,8},{16,20},{20,16},{24,28},{28,24},{1,5},{5... | collective-permute-start | bytes 983048 | tf_op jit(solution)/shard_map/ppermute | solution.py:21
  120.5 17.9 %collective-permute-start.19 = (bf16[2,256,640]{2,1,0:T(8,128)(2,1)}, bf16[2,256,640]{2,1,0:T(8,128)(2,1)}, u32[]{:S(2)}, u32[]{:S(2)}) collective-permute-start(bf16[2,256,640]{2,1,0:T(8,128)(2,1)} %get-tuple-element.70), channel_id=1, source_target_pairs={{0,4},{4,0},{8,12},{12,8},{16,20},{20,16},{24,28},{28,24},{1,5},{5... | collective-permute-start | bytes 1966088 | tf_op jit(solution)/shard_map/ppermute | solution.py:21
  128.7 24.5 %collective-permute-start.17 = (bf16[2,256,640]{2,1,0:T(8,128)(2,1)}, bf16[2,256,640]{2,1,0:T(8,128)(2,1)S(1)}, u32[]{:S(2)}, u32[]{:S(2)}) collective-permute-start(bf16[2,256,640]{2,1,0:T(8,128)(2,1)} %get-tuple-element.69), channel_id=1, source_target_pairs={{0,4},{4,0},{8,12},{12,8},{16,20},{20,16},{24,28},{28,24},{1,5},{5... | collective-permute-start | bytes 1966088 | tf_op jit(solution)/shard_map/ppermute | solution.py:21
  150.5 16.1 %collective-permute-start.24 = (bf16[256,640]{1,0:T(8,128)(2,1)}, bf16[256,640]{1,0:T(8,128)(2,1)}, u32[]{:S(2)}, u32[]{:S(2)}) collective-permute-start(bf16[256,640]{1,0:T(8,128)(2,1)} %fusion.9), channel_id=1, source_target_pairs={{0,16},{4,20},{8,24},{12,28},{16,0},{20,4},{24,8},{28,12},{1,17},{... | collective-permute-start | bytes 983048 | tf_op jit(solution)/shard_map/ppermute | solution.py:21
  155.3 15.8 %collective-permute-start.25 = (bf16[512,256]{1,0:T(8,128)(2,1)S(1)}, bf16[512,256]{1,0:T(8,128)(2,1)S(1)}, u32[]{:S(2)}, u32[]{:S(2)}) collective-permute-start(bf16[512,256]{1,0:T(8,128)(2,1)S(1)} %slice.45), channel_id=1, source_target_pairs={{0,2},{1,3},{2,0},{3,1},{4,6},{5,7},{6,4},{7,5},{8,10},{9,11},{10,... | collective-permute-start | bytes 786440 | tf_op jit(solution)/shard_map/ppermute | solution.py:21
  173.1 16.6 %collective-permute-start.29 = (bf16[256,640]{1,0:T(8,128)(2,1)S(1)}, bf16[256,640]{1,0:T(8,128)(2,1)S(1)}, u32[]{:S(2)}, u32[]{:S(2)}) collective-permute-start(bf16[256,640]{1,0:T(8,128)(2,1)S(1)} %bitcast.56), channel_id=1, source_target_pairs={{0,16},{4,20},{8,24},{12,28},{16,0},{20,4},{24,8},{28,12},{1,17},{... | collective-permute-start | bytes 983048 | tf_op jit(solution)/shard_map/ppermute | solution.py:21
  200.7 17.7 %collective-permute-start.35 = (bf16[4,256,640]{2,1,0:T(8,128)(2,1)}, bf16[4,256,640]{2,1,0:T(8,128)(2,1)}, u32[]{:S(2)}, u32[]{:S(2)}) collective-permute-start(bf16[4,256,640]{2,1,0:T(8,128)(2,1)} %stack.31.refs_2_.ref.refs_0_), channel_id=1, source_target_pairs={{0,1},{1,0},{2,3},{3,2},{4,5},{5,4},{6,7},{7,6},{8,9},{9,8},{10,11... | collective-permute-start | bytes 3932168 | tf_op jit(solution)/shard_map/ppermute | solution.py:21
  202.7 15.7 %collective-permute-start.37 = (bf16[256,640]{1,0:T(8,128)(2,1)}, bf16[256,640]{1,0:T(8,128)(2,1)}, u32[]{:S(2)}, u32[]{:S(2)}) collective-permute-start(bf16[256,640]{1,0:T(8,128)(2,1)} %copy-done.15), channel_id=1, source_target_pairs={{0,2},{1,3},{2,0},{3,1},{4,6},{5,7},{6,4},{7,5},{8,10},{9,11},{10,... | collective-permute-start | bytes 983048 | tf_op jit(solution)/shard_map/ppermute | solution.py:21
  202.7 23.8 %collective-permute-start.34 = (bf16[256,640]{1,0:T(8,128)(2,1)}, bf16[256,640]{1,0:T(8,128)(2,1)S(1)}, u32[]{:S(2)}, u32[]{:S(2)}) collective-permute-start(bf16[256,640]{1,0:T(8,128)(2,1)} %copy-done.14), channel_id=1, source_target_pairs={{0,4},{4,0},{8,12},{12,8},{16,20},{20,16},{24,28},{28,24},{1,5},{5... | collective-permute-start | bytes 983048 | tf_op jit(solution)/shard_map/ppermute | solution.py:21
  204.1 22.5 %collective-permute-start.28 = (bf16[256,640]{1,0:T(8,128)(2,1)}, bf16[256,640]{1,0:T(8,128)(2,1)}, u32[]{:S(2)}, u32[]{:S(2)}) collective-permute-start(bf16[256,640]{1,0:T(8,128)(2,1)} %copy-done.15), channel_id=1, source_target_pairs={{0,4},{4,0},{8,12},{12,8},{16,20},{20,16},{24,28},{28,24},{1,5},{5... | collective-permute-start | bytes 983048 | tf_op jit(solution)/shard_map/ppermute | solution.py:21
  229.7 25.4 %collective-permute-start.38 = (bf16[4,256,640]{2,1,0:T(8,128)(2,1)}, bf16[4,256,640]{2,1,0:T(8,128)(2,1)}, u32[]{:S(2)}, u32[]{:S(2)}) collective-permute-start(bf16[4,256,640]{2,1,0:T(8,128)(2,1)} %stack.32.ref.refs_2_.refs_1_), channel_id=1, source_target_pairs={{0,1},{1,0},{2,3},{3,2},{4,5},{5,4},{6,7},{7,6},{8,9},{9,8},{10,11... | collective-permute-start | bytes 3932168 | tf_op jit(solution)/shard_map/ppermute | solution.py:21
  231.4 16.1 %collective-permute-start.40 = (bf16[256,640]{1,0:T(8,128)(2,1)S(1)}, bf16[256,640]{1,0:T(8,128)(2,1)}, u32[]{:S(2)}, u32[]{:S(2)}) collective-permute-start(bf16[256,640]{1,0:T(8,128)(2,1)S(1)} %copy-done.11), channel_id=1, source_target_pairs={{0,2},{1,3},{2,0},{3,1},{4,6},{5,7},{6,4},{7,5},{8,10},{9,11},{10,... | collective-permute-start | bytes 983048 | tf_op jit(solution)/shard_map/ppermute | solution.py:21
  231.7 22.8 %collective-permute-start.44 = (bf16[256,640]{1,0:T(8,128)(2,1)}, bf16[256,640]{1,0:T(8,128)(2,1)}, u32[]{:S(2)}, u32[]{:S(2)}) collective-permute-start(bf16[256,640]{1,0:T(8,128)(2,1)} %collective-permute-done.28.refs_1_), channel_id=1, source_target_pairs={{0,2},{1,3},{2,0},{3,1},{4,6},{5,7},{6,4},{7,5},{8,10},{9,11},{10,... | collective-permute-start | bytes 983048 | tf_op jit(solution)/shard_map/ppermute | solution.py:21
  238.2 16.4 %collective-permute-start.42 = (f32[2,8,128]{2,1,0:T(8,128)S(1)}, f32[2,8,128]{2,1,0:T(8,128)S(1)}, u32[]{:S(2)}, u32[]{:S(2)}) collective-permute-start(f32[2,8,128]{2,1,0:T(8,128)S(1)} %add.113), channel_id=1, source_target_pairs={{0,2},{1,3},{2,0},{3,1},{4,6},{5,7},{6,4},{7,5},{8,10},{9,11},{10,... | collective-permute-start | bytes 24584 | tf_op jit(solution)/shard_map/ppermute | solution.py:21
  240.5 25.1 %collective-permute-start.45 = (bf16[256,640]{1,0:T(8,128)(2,1)S(1)}, bf16[256,640]{1,0:T(8,128)(2,1)}, u32[]{:S(2)}, u32[]{:S(2)}) collective-permute-start(bf16[256,640]{1,0:T(8,128)(2,1)S(1)} %copy-done.9), channel_id=1, source_target_pairs={{0,2},{1,3},{2,0},{3,1},{4,6},{5,7},{6,4},{7,5},{8,10},{9,11},{10,... | collective-permute-start | bytes 983048 | tf_op jit(solution)/shard_map/ppermute | solution.py:21
  247.5 25.2 %collective-permute-start.46 = (bf16[256,640]{1,0:T(8,128)(2,1)}, bf16[256,640]{1,0:T(8,128)(2,1)S(1)}, u32[]{:S(2)}, u32[]{:S(2)}) collective-permute-start(bf16[256,640]{1,0:T(8,128)(2,1)} %copy-done.18), channel_id=1, source_target_pairs={{0,1},{1,0},{2,3},{3,2},{4,5},{5,4},{6,7},{7,6},{8,9},{9,8},{10,11... | collective-permute-start | bytes 983048 | tf_op jit(solution)/shard_map/ppermute | solution.py:21
  254.5 18.7 %collective-permute-start.47 = (bf16[256,640]{1,0:T(8,128)(2,1)}, bf16[256,640]{1,0:T(8,128)(2,1)}, u32[]{:S(2)}, u32[]{:S(2)}) collective-permute-start(bf16[256,640]{1,0:T(8,128)(2,1)} %collective-permute-done.33.refs_5_), channel_id=1, source_target_pairs={{0,1},{1,0},{2,3},{3,2},{4,5},{5,4},{6,7},{7,6},{8,9},{9,8},{10,11... | collective-permute-start | bytes 983048 | tf_op jit(solution)/shard_map/ppermute | solution.py:21
  254.6 18.7 %collective-permute-start.48 = (bf16[256,640]{1,0:T(8,128)(2,1)}, bf16[256,640]{1,0:T(8,128)(2,1)}, u32[]{:S(2)}, u32[]{:S(2)}) collective-permute-start(bf16[256,640]{1,0:T(8,128)(2,1)} %collective-permute-done.37.refs_6_), channel_id=1, source_target_pairs={{0,1},{1,0},{2,3},{3,2},{4,5},{5,4},{6,7},{7,6},{8,9},{9,8},{10,11... | collective-permute-start | bytes 983048 | tf_op jit(solution)/shard_map/ppermute | solution.py:21
  265.6 23.6 %collective-permute-start.50 = (bf16[256,640]{1,0:T(8,128)(2,1)}, bf16[256,640]{1,0:T(8,128)(2,1)S(1)}, u32[]{:S(2)}, u32[]{:S(2)}) collective-permute-start(bf16[256,640]{1,0:T(8,128)(2,1)} %collective-permute-done.36.refs_8_), channel_id=1, source_target_pairs={{0,1},{1,0},{2,3},{3,2},{4,5},{5,4},{6,7},{7,6},{8,9},{9,8},{10,11... | collective-permute-start | bytes 983048 | tf_op jit(solution)/shard_map/ppermute | solution.py:21
  272.7 16.5 %collective-permute-start.51 = (bf16[256,640]{1,0:T(8,128)(2,1)}, bf16[256,640]{1,0:T(8,128)(2,1)}, u32[]{:S(2)}, u32[]{:S(2)}) collective-permute-start(bf16[256,640]{1,0:T(8,128)(2,1)} %collective-permute-done.40.refs_9_), channel_id=1, source_target_pairs={{0,1},{1,0},{2,3},{3,2},{4,5},{5,4},{6,7},{7,6},{8,9},{9,8},{10,11... | collective-permute-start | bytes 983048 | tf_op jit(solution)/shard_map/ppermute | solution.py:21
  272.8 16.5 %collective-permute-start.52 = (bf16[256,640]{1,0:T(8,128)(2,1)}, bf16[256,640]{1,0:T(8,128)(2,1)}, u32[]{:S(2)}, u32[]{:S(2)}) collective-permute-start(bf16[256,640]{1,0:T(8,128)(2,1)} %collective-permute-done.39.refs_10_), channel_id=1, source_target_pairs={{0,1},{1,0},{2,3},{3,2},{4,5},{5,4},{6,7},{7,6},{8,9},{9,8},{10,11... | collective-permute-start | bytes 983048 | tf_op jit(solution)/shard_map/ppermute | solution.py:21
  273.3 16.0 %collective-permute-start.49 = (bf16[256,640]{1,0:T(8,128)(2,1)}, bf16[256,640]{1,0:T(8,128)(2,1)}, u32[]{:S(2)}, u32[]{:S(2)}) collective-permute-start(bf16[256,640]{1,0:T(8,128)(2,1)} %collective-permute-done.44.refs_7_), channel_id=1, source_target_pairs={{0,1},{1,0},{2,3},{3,2},{4,5},{5,4},{6,7},{7,6},{8,9},{9,8},{10,11... | collective-permute-start | bytes 983048 | tf_op jit(solution)/shard_map/ppermute | solution.py:21
  273.3 15.9 %collective-permute-start.53 = (bf16[256,640]{1,0:T(8,128)(2,1)}, bf16[256,640]{1,0:T(8,128)(2,1)}, u32[]{:S(2)}, u32[]{:S(2)}) collective-permute-start(bf16[256,640]{1,0:T(8,128)(2,1)} %collective-permute-done.45.refs_11_), channel_id=1, source_target_pairs={{0,1},{1,0},{2,3},{3,2},{4,5},{5,4},{6,7},{7,6},{8,9},{9,8},{10,11... | collective-permute-start | bytes 983048 | tf_op jit(solution)/shard_map/ppermute | solution.py:21
  (49 other events, 712.5 us)
Sparse Core Ops, SparseCore 0:
  62.8 39.4 all-gather.4
  103.9 40.4 all-gather.6

commit v3 on v1

--- a/solution.py
+++ b/solution.py
@@ -70,7 +70,7 @@
     count = lax.axis_size("lat")
     if own.shape[1] % LANES:
         blocks = jnp.split(lax.all_gather(own, "lat", axis=1, tiled=True), 8, axis=1)
-        return blocks, {k: exchange(block, "tok", 2) for k, block in enumerate(blocks) if over_tok}
+        return blocks, {k: exchange(blocks[k], "tok", 2) for k in (0, 1) if over_tok}
     direct = {}
     step = count // 2
     while step:
@@ -94,9 +94,6 @@
                 early.append(crossed[k | 1])
         if step < count // 2:
             if over_tok:
-                for k in (count // 2, step):
-                    far[k] = exchange(held.get(k, direct[k]), "tok", 2)
-                    early.append(far[k])
                 early.append(far[1])
             else:
                 crossed[step | 1] = exchange(direct[step], "lat", 1)
@@ -109,8 +106,6 @@
         if k | 1 not in crossed:
             crossed[k | 1] = exchange(value, "lat", 1)
     held.update(crossed)
-    if over_tok:
-        far.update({k: exchange(held[k], "tok", 2) for k in held if k not in far})
     return [held[k] for k in range(count)], far
 
 
@@ -394,11 +389,22 @@
     if mode == "sum":
         rest[0][...] = parts[0] + parts[1]
     else:
-        mask_ref, grad_ref = rest
         total = parts[0] + parts[1]
         for ref in sums:
             total = total + ref[...]
-        grad_ref[...] = (mask_ref[...].astype(F32).T * total).astype(BF16)
+        grad = (rest[0][...].astype(F32).T * total).astype(BF16)
+        if len(rest) == 2:
+            rest[1][...] = grad
+        else:
+            own = 2 * pl.program_id(0) < pl.num_programs(0)
+
+            @pl.when(own)
+            def _():
+                rest[1][...] = grad
+
+            @pl.when(jnp.logical_not(own))
+            def _():
+                rest[2][...] = grad
 
 
 def project(matrix, own, near, mode, sums=(), mask=None):
@@ -415,14 +421,22 @@
     in_specs = [layer(l) for l in range(layers)] + [whole] * 2
     in_specs += [flat] * len(sums)
     args = [matrix] * layers + [own, near, *sums]
+    steps = latents // rows
+    out_specs = flat
+    out_shape = jax.ShapeDtypeStruct((latents, tokens), BF16 if mode == "grad" else F32)
     if mode == "grad":
         in_specs.append(across)
         args.append(mask)
-    out_specs = flat
-    out_shape = jax.ShapeDtypeStruct((latents, tokens), BF16 if mode == "grad" else F32)
-    return pl.pallas_call(
+        if steps > 1:
+            middle = steps // 2
+            out_specs = (
+                pl.BlockSpec((rows, tokens), lambda i: (jnp.minimum(i, middle - 1), 0)),
+                pl.BlockSpec((rows, tokens), lambda i: (jnp.maximum(i, middle) - middle, 0)),
+            )
+            out_shape = (jax.ShapeDtypeStruct((latents // 2, tokens), BF16),) * 2
+    out = pl.pallas_call(
         functools.partial(project_kernel, layers=layers, mode=mode, earlier=len(sums)),
-        grid=(latents // rows,),
+        grid=(steps,),
         in_specs=in_specs,
         out_specs=out_specs,
         scratch_shapes=[pltpu.VMEM((layers, tokens, width), BF16)],
@@ -431,6 +445,9 @@
         cost_estimate=SMALL,
         name="project_" + mode,
     )(*args)
+    if mode == "grad" and steps == 1:
+        return out[:latents // 2], out[latents // 2:]
+    return out
 
 
 def recon_kernel(act_ref, *refs, parts):
@@ -604,7 +621,11 @@
         ),
         out_shape=jax.ShapeDtypeStruct((rows, layers, full), BF16),
         compiler_params=pltpu.CompilerParams(vmem_limit_bytes=VMEM_BYTES),
-        cost_estimate=SMALL,
+        cost_estimate=pl.CostEstimate(
+            flops=4 * rows * depth * layers * full,
+            bytes_accessed=8 * rows * layers * full,
+            transcendentals=0,
+        ),
         name="weight_grad",
     )(place, scale, own, far, *sources)
 
@@ -642,16 +663,17 @@
         squared = squares(first, layers)
         early = [sums, squared]
         if over_tok:
-            early += [far[k] for k in (6, 5)]
+            far.update({k: exchange(blocks[k], "tok", 2) for k in (4, 2)})
+            early += [far[4], far[2]]
         final = halves[1][-1]
         blocks[final] = after(blocks[final], *early)
         second = stack([blocks[k] for k in halves[1]])
         near = [first_near, exchange(second, "tok", 1)]
-        return [first, second], near, sums, squared, far
+        return blocks, [first, second], near, sums, squared, far
 
     dec_first = rearrange(dec_weight, spot, halves, runs, 0)
     dec_halves = rearrange(dec_weight, spot, halves, runs, 1, dec_first)
-    x_own, x_near, sums, squared, _ = gather_halves(
+    _, x_own, x_near, sums, squared, _ = gather_halves(
         own_x,
         lambda own, near: encode(enc_weight, halves[0], own, near, spot, "parts"),
         beside=([*dec_first, mask, bias], dec_halves),
@@ -699,17 +721,21 @@
     diff = recon - norm_scale[:, None, None] * own_f
     factor = LOSS_SCALE / tokens
     err_low = (diff * factor).astype(BF16).reshape(layers * tok_dev, width_part)
-    err_own, err_near, sums, squared, far = gather_halves(
+    err_blocks, err_own, err_near, sums, squared, far = gather_halves(
         err_low, lambda own, near: project(dec_halves[0], own, near, "sum"), over_tok=True
     )
-    grad = project(dec_halves[1], err_own[1], err_near[1], "grad", [sums], mask=mask)
-    grad_far = exchange(grad[quarter:], "tok", 2)
+    far.update({k: exchange(err_blocks[k], "tok", 2) for k in (6, 5)})
+    for k in (3, 7):
+        far[k] = exchange(far[k ^ 1], "lat", 1) if aligned else exchange(err_blocks[k], "tok", 2)
+    grad, grad_away = project(dec_halves[1], err_own[1], err_near[1], "grad", [sums], mask=mask)
+    grad_far = exchange(grad_away, "tok", 2)
     error_sums = squared + squares(err_own[1], layers)
-    soon = [k for k in range(block_count) if k not in (3, 7)]
-    last = {k: exchange(far[k], "tok", 1) for k in soon}
-    grad_far, error_sums, far[3], far[7] = lax.optimization_barrier(
-        (grad_far, error_sums, far[3], far[7])
-    )
+    late = (3, 5, 6, 7)
+    grad_far, error_sums, *values = lax.optimization_barrier(
+        (grad_far, error_sums, *[far[k] for k in late])
+    )
+    far.update(zip(late, values))
+    last = {k: exchange(value, "tok", 1) for k, value in far.items()}
 
     shape = (layers, full_width)
     spots = {k: (h, i) for h, half in enumerate(halves) for i, k in enumerate(half)}
@@ -720,8 +746,6 @@
     )
     error_sums = error_sums + exchange(error_sums, "tok", 1)
     act, error_sums = lax.optimization_barrier((act, error_sums))
-    for k in (3, 7):
-        last[k] = exchange(far[k], "tok", 1)
     where = [(2 * g + h, i) for g in range(2) for h, i in order]
     where += [(4 + g * block_count + k, -1) for g in range(2) for k in range(block_count)]
     sources = err_own + err_near + [group[k] for group in (far, last) for k in range(block_count)]

time: 288 us -> 281 us (0.976)
  waiting for transfers between devices: 79.6 us -> 72.6 us
    ppermute x51, waiting for transfers between devices: 79.5 us -> 72.6 us  [exchange(): return lax.ppermute(value, axis, [(i, i ^ mask) for i in range(size)])]
  transfers between devices with their start and end apart: 53 -> 53, of which waited for: 22 -> 20; matrix products, arithmetic and copies ran while one was open for 6% -> 6% of each run, Pallas kernels for 38% -> 38%
where the time goes in v3:
time: 281 us; the launch traced here: 279 us
  Pallas kernels  128 us (46%)
  waiting for transfers between devices  72.6 us (26%)
  starting transfers between devices  40.6 us (14%)
  between operations  16.2 us (6%)
  other arithmetic  14.4 us (5%)
  local copies, waits for them, and re-layouts  7.32 us (3%)
    ppermute x51, waiting for transfers between devices, exchange(): return lax.ppermute(value, axis, [(i, i ^ mask) for i in range(size)])  72.6 us
    ppermute x51, starting transfers between devices, exchange(): return lax.ppermute(value, axis, [(i, i ^ mask) for i in range(size)])  40.3 us
    pallas_call x2, Pallas kernels, weight_grad(): pl.pallas_call(functools.partial(grad_kernel, groups=groups, where=where,...  26.9 us
    pallas_call x2, Pallas kernels, rearrange(): pl.pallas_call(functools.partial(rearrange_kernel, halves=halves, count=c...  26.1 us
    pallas_call x2, Pallas kernels, encode(): pl.pallas_call(functools.partial(encode_kernel, half=half, mode=mode, ear...  24.7 us
    pallas_call x2, Pallas kernels, project(): pl.pallas_call(functools.partial(project_kernel, layers=layers, mode=mode...  16.7 us
    pallas_call x2, Pallas kernels, recon_half(): pl.pallas_call(functools.partial(recon_kernel, parts=parts), grid=(blocks...  15.8 us
    pallas_call x4, Pallas kernels, stack(): pl.pallas_call(stack_kernel, out_shape=jax.ShapeDtypeStruct((len(blocks),...  9.85 us
  transfers between devices with their start and end apart: 53, of which 20 were waited for; matrix products, arithmetic and copies ran while one was open for 6% of the time, Pallas kernels for 38%

profile of v3, /device:TPU:0, one launch (start us, length us, event | category | flops | bytes accessed | tf_op | source)
XLA Modules:
  0.0 279.4 jit_solution(16751484608231646809)
XLA Ops:
  8.2 3.1 %collective-permute-start = (bf16[256,640]{1,0:T(8,128)(2,1)S(1)}, bf16[256,640]{1,0:T(8,128)(2,1)}, u32[]{:S(2)}, u32[]{:S(2)}) collective-permute-start(bf16[256,640]{1,0:T(8,128)(2,1)S(1)} %bitcast.47), channel_id=1, source_target_pairs={{0,8},{4,12},{8,0},{12,4},{16,24},{20,28},{24,16},{28,20},{1,9},{5... | collective-permute-start | bytes 983048 | tf_op jit(solution)/shard_map/ppermute | solution.py:21
  11.3 2.6 collective-permute-start.1
  18.2 13.1 %rearrange.2 = (bf16[2,1024,2560]{2,1,0:T(8,128)(2,1)}, bf16[2,1024,2560]{2,1,0:T(8,128)(2,1)}) custom-call(s32[2]{0:T(128)} %pad_add_fusion.1.place, bf16[2048,2,5120]{2,1,0:T(2,128)(2,1)} %refs_1_.3, bf16[2048,2,5120]{2,1,0:T(2,128)(2,1)} %refs_1_.3), custom_call_target="tpu_custom_call" | custom-call | flops 1024 | bytes 1024 | tf_op jit(solution)/shard_map/rearrange/pallas_call | solution.py:347
  35.8 13.0 %rearrange.3 = (bf16[2,1024,2560]{2,1,0:T(8,128)(2,1)}, bf16[2,1024,2560]{2,1,0:T(8,128)(2,1)}) custom-call(s32[2]{0:T(128)} %pad_add_fusion.1.place, bf16[2048,2,5120]{2,1,0:T(2,128)(2,1)} %refs_1_.3, bf16[2048,2,5120]{2,1,0:T(2,128)(2,1)} %refs_1_.3, ...), custom_call_target="tpu_custom_call", output_to_operand_aliasing={{0}: (3, {}), {1}: (4, {})} | custom-call | flops 1024 | bytes 1024 | tf_op jit(solution)/shard_map/rearrange/pallas_call | solution.py:347
  48.8 2.1 collective-permute-done.6.refs_1_
  50.9 2.5 stack.29.ref.refs_0_
  57.1 12.4 %encode_parts.1.refs_2_ = f32[2,1024,256]{2,1,0:T(8,128)} custom-call(s32[2]{0:T(128)} %pad_add_fusion.1.place, bf16[2048,2,5120]{2,1,0:T(2,128)(2,1)} %w_ref.3, bf16[4,256,640]{2,1,0:T(8,128)(2,1)} %stack.29.ref.refs_0_, bf16[4,256,640]{2,1,0:T(8,128)(2,1)} %collective-permute-done.8.refs_1_), custom_call_target="tpu_custom_call" | custom-call | flops 1024 | bytes 1024 | tf_op jit(solution)/shard_map/encode_parts/pallas_call | solution.py:290
  70.3 2.5 stack.30.ref.refs_0_
  72.8 2.0 squares.5
  81.4 12.3 %encode_act.1 = (bf16[256,1024]{1,0:T(8,128)(2,1)}, bf16[1024,256]{1,0:T(8,128)(2,1)}) custom-call(s32[2]{0:T(128)} %pad_add_fusion.1.place, bf16[2048,2,5120]{2,1,0:T(2,128)(2,1)} %w_ref.3, bf16[4,256,640]{2,1,0:T(8,128)(2,1)} %stack.30.ref.refs_0_, bf16[4,256,640]{2,1,0:T(8,128)(2,1)} %collective-permute-done.11.refs_1_, ...), custom_call_target="tpu_custom_call" | custom-call | flops 1024 | bytes 1024 | tf_op jit(solution)/shard_map/encode_act/pallas_call | solution.py:290
  93.7 7.8 %recon_half.2 = (f32[4,256,640]{2,1,0:T(8,128)}, bf16[4,256,640]{2,1,0:T(8,128)(2,1)}) custom-call(bf16[256,1024]{1,0:T(8,128)(2,1)} %get-tuple-element.45.act_ref, bf16[2,1024,2560]{2,1,0:T(8,128)(2,1)} %get-tuple-element.39.refs_0_.refs_1_, bf16[2,1024,2560]{2,1,0:T(8,128)(2,1)} %get-tuple-element.39.refs_0_.refs_1_), custom_call_target="tpu_custom_call" | custom-call | flops 1024 | bytes 1024 | tf_op jit(solution)/shard_map/recon_half/pallas_call | solution.py:503
  101.6 3.2 %collective-permute-done.12 = bf16[4,256,640]{2,1,0:T(8,128)(2,1)S(1)} collective-permute-done((bf16[4,256,640]{2,1,0:T(8,128)(2,1)}, bf16[4,256,640]{2,1,0:T(8,128)(2,1)S(1)}, u32[]{:S(2)}, u32[]{:S(2)}) %collective-permute-start.12) | collective-permute-done | bytes 1310752 | tf_op jit(solution)/shard_map/ppermute | solution.py:21
  104.8 2.1 add_convert_fusion
  108.6 8.0 %recon_half.3 = (f32[4,256,640]{2,1,0:T(8,128)}, bf16[256,640]{1,0:T(8,128)(2,1)}, bf16[256,640]{1,0:T(8,128)(2,1)}, bf16[256,640]{1,0:T(8,128)(2,1)}, bf16[256,640]{1,0:T(8,128)(2,1)}) custom-call(bf16[256,1024]{1,0:T(8,128)(2,1)} %get-tuple-element.45.act_ref, bf16[2,1024,2560]{2,1,0:T(8,128)(2,1)} %get-tuple-element.38.refs_0_.refs_1_, ...), custom_call_target="tpu_custom_call" | custom-call | flops 1024 | bytes 1024 | tf_op jit(solution)/shard_map/recon_half/pallas_call | solution.py:503
  118.4 7.4 %collective-permute-done.16 = bf16[2,256,640]{2,1,0:T(8,128)(2,1)} collective-permute-done((bf16[2,256,640]{2,1,0:T(8,128)(2,1)}, bf16[2,256,640]{2,1,0:T(8,128)(2,1)}, u32[]{:S(2)}, u32[]{:S(2)}) %collective-permute-start.16) | collective-permute-done | bytes 655392 | tf_op jit(solution)/shard_map/ppermute | solution.py:21
  129.1 9.8 %collective-permute-done.14 = bf16[2,256,640]{2,1,0:T(8,128)(2,1)S(1)} collective-permute-done((bf16[2,256,640]{2,1,0:T(8,128)(2,1)S(1)}, bf16[2,256,640]{2,1,0:T(8,128)(2,1)S(1)}, u32[]{:S(2)}, u32[]{:S(2)}) %collective-permute-start.14) | collective-permute-done | bytes 655392 | tf_op jit(solution)/shard_map/ppermute | solution.py:21
  144.9 12.6 %collective-permute-done.21 = bf16[256,640]{1,0:T(8,128)(2,1)S(1)} collective-permute-done((bf16[256,640]{1,0:T(8,128)(2,1)S(1)}, bf16[256,640]{1,0:T(8,128)(2,1)S(1)}, u32[]{:S(2)}, u32[]{:S(2)}) %collective-permute-start.21) | collective-permute-done | bytes 327712 | tf_op jit(solution)/shard_map/ppermute | solution.py:21
  159.9 3.2 %collective-permute-start.26 = (bf16[256,640]{1,0:T(8,128)(2,1)S(1)}, bf16[256,640]{1,0:T(8,128)(2,1)S(1)}, u32[]{:S(2)}, u32[]{:S(2)}) collective-permute-start(bf16[256,640]{1,0:T(8,128)(2,1)S(1)} %bitcast.53), channel_id=1, source_target_pairs={{0,16},{4,20},{8,24},{12,28},{16,0},{20,4},{24,8},{28,12},{1,17},{... | collective-permute-start | bytes 983048 | tf_op jit(solution)/shard_map/ppermute | solution.py:21
  164.6 3.2 %collective-permute-done.23.refs_0_ = bf16[256,640]{1,0:T(8,128)(2,1)S(1)} collective-permute-done((bf16[256,640]{1,0:T(8,128)(2,1)S(1)}, bf16[256,640]{1,0:T(8,128)(2,1)S(1)}, u32[]{:S(2)}, u32[]{:S(2)}) %collective-permute-start.23) | collective-permute-done | bytes 327712 | tf_op jit(solution)/shard_map/ppermute | solution.py:21
  167.9 7.0 %collective-permute-done.24.refs_1_ = bf16[256,640]{1,0:T(8,128)(2,1)S(1)} collective-permute-done((bf16[256,640]{1,0:T(8,128)(2,1)S(1)}, bf16[256,640]{1,0:T(8,128)(2,1)S(1)}, u32[]{:S(2)}, u32[]{:S(2)}) %collective-permute-start.24) | collective-permute-done | bytes 327712 | tf_op jit(solution)/shard_map/ppermute | solution.py:21
  179.8 4.6 %collective-permute-done.28.refs_2_ = bf16[256,640]{1,0:T(8,128)(2,1)S(1)} collective-permute-done((bf16[256,640]{1,0:T(8,128)(2,1)S(1)}, bf16[256,640]{1,0:T(8,128)(2,1)S(1)}, u32[]{:S(2)}, u32[]{:S(2)}) %collective-permute-start.28) | collective-permute-done | bytes 327712 | tf_op jit(solution)/shard_map/ppermute | solution.py:21
  186.2 2.5 stack.31.refs_2_.ref.refs_0_
  192.8 2.0 squares.6
  194.8 8.1 %project_sum.1.refs_4_ = f32[1024,256]{1,0:T(8,128)} custom-call(bf16[2,1024,2560]{2,1,0:T(8,128)(2,1)} %get-tuple-element.38.refs_0_.refs_1_, bf16[2,1024,2560]{2,1,0:T(8,128)(2,1)} %get-tuple-element.38.refs_0_.refs_1_, bf16[4,256,640]{2,1,0:T(8,128)(2,1)} %stack.31.refs_2_.ref.refs_0_, bf16[4,256,640]{2,1,0:T(8,128)(2,1)} %collective-permute-done.32.refs_3_.refs_2_), custom_call_target="tpu_custom_call" | custom-call | flops 1024 | bytes 1024 | tf_op jit(solution)/shard_map/project_sum/pallas_call | solution.py:437
  202.9 3.3 %collective-permute-done.34.refs_6_ = bf16[256,640]{1,0:T(8,128)(2,1)} collective-permute-done((bf16[256,640]{1,0:T(8,128)(2,1)}, bf16[256,640]{1,0:T(8,128)(2,1)}, u32[]{:S(2)}, u32[]{:S(2)}) %collective-permute-start.34) | collective-permute-done | bytes 327712 | tf_op jit(solution)/shard_map/ppermute | solution.py:21
  207.6 2.5 stack.32.refs_2_.ref.refs_1_
  212.9 7.9 %collective-permute-done.39.refs_10_ = bf16[256,640]{1,0:T(8,128)(2,1)} collective-permute-done((bf16[256,640]{1,0:T(8,128)(2,1)S(1)}, bf16[256,640]{1,0:T(8,128)(2,1)}, u32[]{:S(2)}, u32[]{:S(2)}) %collective-permute-start.39) | collective-permute-done | bytes 327712 | tf_op jit(solution)/shard_map/ppermute | solution.py:21
  221.5 8.7 %project_grad.1 = (bf16[512,256]{1,0:T(8,128)(2,1)}, bf16[512,256]{1,0:T(8,128)(2,1)}) custom-call(bf16[2,1024,2560]{2,1,0:T(8,128)(2,1)} %get-tuple-element.39.refs_0_.refs_1_, bf16[2,1024,2560]{2,1,0:T(8,128)(2,1)} %get-tuple-element.39.refs_0_.refs_1_, bf16[4,256,640]{2,1,0:T(8,128)(2,1)} %stack.32.refs_2_.ref.refs_1_, ...), custom_call_target="tpu_custom_call" | custom-call | flops 1024 | bytes 1024 | tf_op jit(solution)/shard_map/project_grad/pallas_call | solution.py:437
  232.4 2.0 squares.7
  235.1 2.4 collective-permute-done.36.far_ref
  242.4 13.6 %weight_grad.2 = bf16[512,2,5120]{2,1,0:T(2,128)(2,1)} custom-call(s32[3]{0:T(128)} %pad_add_fusion.place, f32[2]{0:T(128)} %add_rsqrt_fusion.refs_3_.scale_ref, bf16[512,256]{1,0:T(8,128)(2,1)} %get-tuple-element.57.own_ref, bf16[512,256]{1,0:T(8,128)(2,1)} %copy-done.23, bf16[4,4,256,640]{3,2,1,0:T(8,128)(2,1)} %bitcast.58, bf16[4,4,256,640]{3,2,1,0:T(8,128)(2,1)} %bitcast.59), custom_call_target="tpu_custom_call" | custom-call | flops 10737418240 | bytes 41943040 | tf_op jit(solution)/shard_map/weight_grad/pallas_call | solution.py:599
  258.1 13.3 %weight_grad.3 = bf16[512,2,5120]{2,1,0:T(2,128)(2,1)} custom-call(s32[3]{0:T(128)} %pad_add_fusion.place, f32[2]{0:T(128)} %add_rsqrt_fusion.refs_3_.scale_ref, bf16[1024,256]{1,0:T(8,128)(2,1)} %get-tuple-element.61.own_ref, bf16[512,256]{1,0:T(8,128)(2,1)} %copy-done.22, bf16[4,256,640]{2,1,0:T(8,128)(2,1)} %stack.31.refs_2_.ref.refs_0_, ...), custom_call_target="tpu_custom_call" | custom-call | flops 10737418240 | bytes 41943040 | tf_op jit(solution)/shard_map/weight_grad/pallas_call | solution.py:599
  (167 shorter events, 62.4 us)
Async XLA Ops:
  7.2 151.7 %all-gather.5.cloned.1.call-start = ((), (), s32[]{:S(2)}) async-start(), calls=%async_computation | async-start | bytes 6553600 | tf_op jit(solution)/shard_map/all_gather | solution.py:686
  8.2 25.0 %collective-permute-start = (bf16[256,640]{1,0:T(8,128)(2,1)S(1)}, bf16[256,640]{1,0:T(8,128)(2,1)}, u32[]{:S(2)}, u32[]{:S(2)}) collective-permute-start(bf16[256,640]{1,0:T(8,128)(2,1)S(1)} %bitcast.47), channel_id=1, source_target_pairs={{0,8},{4,12},{8,0},{12,4},{16,24},{20,28},{24,16},{28,20},{1,9},{5... | collective-permute-start | bytes 983048 | tf_op jit(solution)/shard_map/ppermute | solution.py:21
  11.3 21.9 %collective-permute-start.1 = (bf16[256,640]{1,0:T(8,128)(2,1)S(1)}, bf16[256,640]{1,0:T(8,128)(2,1)}, u32[]{:S(2)}, u32[]{:S(2)}) collective-permute-start(bf16[256,640]{1,0:T(8,128)(2,1)S(1)} %bitcast.48), channel_id=1, source_target_pairs={{0,16},{4,20},{8,24},{12,28},{16,0},{20,4},{24,8},{28,12},{1,17},{... | collective-permute-start | bytes 983048 | tf_op jit(solution)/shard_map/ppermute | solution.py:21
  13.9 19.3 %collective-permute-start.2 = (bf16[256,640]{1,0:T(8,128)(2,1)S(1)}, bf16[256,640]{1,0:T(8,128)(2,1)S(1)}, u32[]{:S(2)}, u32[]{:S(2)}) collective-permute-start(bf16[256,640]{1,0:T(8,128)(2,1)S(1)} %bitcast.49), channel_id=1, source_target_pairs={{0,4},{4,0},{8,12},{12,8},{16,20},{20,16},{24,28},{28,24},{1,5},{5... | collective-permute-start | bytes 983048 | tf_op jit(solution)/shard_map/ppermute | solution.py:21
  17.5 13.9 %collective-permute-start.3 = (bf16[128,1024]{1,0:T(8,128)(2,1)}, bf16[128,1024]{1,0:T(8,128)(2,1)}, u32[]{:S(2)}, u32[]{:S(2)}) collective-permute-start(bf16[128,1024]{1,0:T(8,128)(2,1)} %pad_maximum_fusion.1), channel_id=1, source_target_pairs={{0,1},{1,0},{2,3},{3,2},{4,5},{5,4},{6,7},{7,6},{8,9},{9,8},{10,11... | collective-permute-start | bytes 786440 | tf_op jit(solution)/shard_map/ppermute | solution.py:21
  33.2 15.6 %collective-permute-start.4 = (bf16[256,640]{1,0:T(8,128)(2,1)}, bf16[256,640]{1,0:T(8,128)(2,1)}, u32[]{:S(2)}, u32[]{:S(2)}) collective-permute-start(bf16[256,640]{1,0:T(8,128)(2,1)} %collective-permute-done.1.refs_2_), channel_id=1, source_target_pairs={{0,8},{4,12},{8,0},{12,4},{16,24},{20,28},{24,16},{28,20},{1,9},{5... | collective-permute-start | bytes 983048 | tf_op jit(solution)/shard_map/ppermute | solution.py:21
  33.8 15.0 %collective-permute-start.5 = (bf16[256,640]{1,0:T(8,128)(2,1)}, bf16[256,640]{1,0:T(8,128)(2,1)S(1)}, u32[]{:S(2)}, u32[]{:S(2)}) collective-permute-start(bf16[256,640]{1,0:T(8,128)(2,1)} %collective-permute-done.1.refs_2_), channel_id=1, source_target_pairs={{0,4},{4,0},{8,12},{12,8},{16,20},{20,16},{24,28},{28,24},{1,5},{5... | collective-permute-start | bytes 983048 | tf_op jit(solution)/shard_map/ppermute | solution.py:21
  34.3 16.6 %collective-permute-start.6 = (bf16[256,640]{1,0:T(8,128)(2,1)}, bf16[256,640]{1,0:T(8,128)(2,1)}, u32[]{:S(2)}, u32[]{:S(2)}) collective-permute-start(bf16[256,640]{1,0:T(8,128)(2,1)} %collective-permute-done.refs_1_), channel_id=1, source_target_pairs={{0,4},{4,0},{8,12},{12,8},{16,20},{20,16},{24,28},{28,24},{1,5},{5... | collective-permute-start | bytes 983048 | tf_op jit(solution)/shard_map/ppermute | solution.py:21
  53.4 105.5 %all-gather.7.cloned.1.call-start = ((), (), s32[]{:S(2)}) async-start(), calls=%async_computation.1 | async-start | bytes 6553600 | tf_op jit(solution)/shard_map/all_gather | solution.py:686
  53.7 15.8 %collective-permute-start.7 = (bf16[256,640]{1,0:T(8,128)(2,1)}, bf16[256,640]{1,0:T(8,128)(2,1)S(1)}, u32[]{:S(2)}, u32[]{:S(2)}) collective-permute-start(bf16[256,640]{1,0:T(8,128)(2,1)} %collective-permute-done.4.refs_3_), channel_id=1, source_target_pairs={{0,4},{4,0},{8,12},{12,8},{16,20},{20,16},{24,28},{28,24},{1,5},{5... | collective-permute-start | bytes 983048 | tf_op jit(solution)/shard_map/ppermute | solution.py:21
  107.9 17.9 %collective-permute-start.16 = (bf16[2,256,640]{2,1,0:T(8,128)(2,1)}, bf16[2,256,640]{2,1,0:T(8,128)(2,1)}, u32[]{:S(2)}, u32[]{:S(2)}) collective-permute-start(bf16[2,256,640]{2,1,0:T(8,128)(2,1)} %get-tuple-element.70), channel_id=1, source_target_pairs={{0,4},{4,0},{8,12},{12,8},{16,20},{20,16},{24,28},{28,24},{1,5},{5... | collective-permute-start | bytes 1966088 | tf_op jit(solution)/shard_map/ppermute | solution.py:21
  116.6 22.4 %collective-permute-start.14 = (bf16[2,256,640]{2,1,0:T(8,128)(2,1)S(1)}, bf16[2,256,640]{2,1,0:T(8,128)(2,1)S(1)}, u32[]{:S(2)}, u32[]{:S(2)}) collective-permute-start(bf16[2,256,640]{2,1,0:T(8,128)(2,1)S(1)} %get-tuple-element.69), channel_id=1, source_target_pairs={{0,4},{4,0},{8,12},{12,8},{16,20},{20,16},{24,28},{28,24},{1,5},{5... | collective-permute-start | bytes 1966088 | tf_op jit(solution)/shard_map/ppermute | solution.py:21
  127.1 11.8 %collective-permute-start.17 = (bf16[256,640]{1,0:T(8,128)(2,1)S(1)}, bf16[256,640]{1,0:T(8,128)(2,1)S(1)}, u32[]{:S(2)}, u32[]{:S(2)}) collective-permute-start(bf16[256,640]{1,0:T(8,128)(2,1)S(1)} %fusion.5), channel_id=1, source_target_pairs={{0,8},{4,12},{8,0},{12,4},{16,24},{20,28},{24,16},{28,20},{1,9},{5... | collective-permute-start | bytes 983048 | tf_op jit(solution)/shard_map/ppermute | solution.py:21
  129.1 15.8 %collective-permute-start.13 = (bf16[256,640]{1,0:T(8,128)(2,1)}, bf16[256,640]{1,0:T(8,128)(2,1)S(1)}, u32[]{:S(2)}, u32[]{:S(2)}) collective-permute-start(bf16[256,640]{1,0:T(8,128)(2,1)} %get-tuple-element.47), channel_id=1, source_target_pairs={{0,1},{1,0},{2,3},{3,2},{4,5},{5,4},{6,7},{7,6},{8,9},{9,8},{10,11... | collective-permute-start | bytes 983048 | tf_op jit(solution)/shard_map/ppermute | solution.py:21
  140.6 16.9 %collective-permute-start.21 = (bf16[256,640]{1,0:T(8,128)(2,1)S(1)}, bf16[256,640]{1,0:T(8,128)(2,1)S(1)}, u32[]{:S(2)}, u32[]{:S(2)}) collective-permute-start(bf16[256,640]{1,0:T(8,128)(2,1)S(1)} %get-tuple-element.68), channel_id=1, source_target_pairs={{0,16},{4,20},{8,24},{12,28},{16,0},{20,4},{24,8},{28,12},{1,17},{... | collective-permute-start | bytes 983048 | tf_op jit(solution)/shard_map/ppermute | solution.py:21
  140.7 16.8 %collective-permute-start.19 = (bf16[256,640]{1,0:T(8,128)(2,1)S(1)}, bf16[256,640]{1,0:T(8,128)(2,1)S(1)}, u32[]{:S(2)}, u32[]{:S(2)}) collective-permute-start(bf16[256,640]{1,0:T(8,128)(2,1)S(1)} %get-tuple-element.67), channel_id=1, source_target_pairs={{0,8},{4,12},{8,0},{12,4},{16,24},{20,28},{24,16},{28,20},{1,9},{5... | collective-permute-start | bytes 983048 | tf_op jit(solution)/shard_map/ppermute | solution.py:21
  143.3 15.5 %collective-permute-start.22 = (bf16[512,256]{1,0:T(8,128)(2,1)S(1)}, bf16[512,256]{1,0:T(8,128)(2,1)S(1)}, u32[]{:S(2)}, u32[]{:S(2)}) collective-permute-start(bf16[512,256]{1,0:T(8,128)(2,1)S(1)} %slice.45), channel_id=1, source_target_pairs={{0,2},{1,3},{2,0},{3,1},{4,6},{5,7},{6,4},{7,5},{8,10},{9,11},{10,... | collective-permute-start | bytes 786440 | tf_op jit(solution)/shard_map/ppermute | solution.py:21
  159.9 15.0 %collective-permute-start.24 = (bf16[256,640]{1,0:T(8,128)(2,1)S(1)}, bf16[256,640]{1,0:T(8,128)(2,1)S(1)}, u32[]{:S(2)}, u32[]{:S(2)}) collective-permute-start(bf16[256,640]{1,0:T(8,128)(2,1)S(1)} %bitcast.52), channel_id=1, source_target_pairs={{0,8},{4,12},{8,0},{12,4},{16,24},{20,28},{24,16},{28,20},{1,9},{5... | collective-permute-start | bytes 983048 | tf_op jit(solution)/shard_map/ppermute | solution.py:21
  159.9 16.3 %collective-permute-start.26 = (bf16[256,640]{1,0:T(8,128)(2,1)S(1)}, bf16[256,640]{1,0:T(8,128)(2,1)S(1)}, u32[]{:S(2)}, u32[]{:S(2)}) collective-permute-start(bf16[256,640]{1,0:T(8,128)(2,1)S(1)} %bitcast.53), channel_id=1, source_target_pairs={{0,16},{4,20},{8,24},{12,28},{16,0},{20,4},{24,8},{28,12},{1,17},{... | collective-permute-start | bytes 983048 | tf_op jit(solution)/shard_map/ppermute | solution.py:21
  163.1 13.1 %collective-permute-start.27 = (bf16[256,640]{1,0:T(8,128)(2,1)S(1)}, bf16[256,640]{1,0:T(8,128)(2,1)S(1)}, u32[]{:S(2)}, u32[]{:S(2)}) collective-permute-start(bf16[256,640]{1,0:T(8,128)(2,1)S(1)} %bitcast.54), channel_id=1, source_target_pairs={{0,2},{1,3},{2,0},{3,1},{4,6},{5,7},{6,4},{7,5},{8,10},{9,11},{10,... | collective-permute-start | bytes 983048 | tf_op jit(solution)/shard_map/ppermute | solution.py:21
  188.7 14.2 %collective-permute-start.33 = (bf16[256,640]{1,0:T(8,128)(2,1)}, bf16[256,640]{1,0:T(8,128)(2,1)}, u32[]{:S(2)}, u32[]{:S(2)}) collective-permute-start(bf16[256,640]{1,0:T(8,128)(2,1)} %copy-done.11), channel_id=1, source_target_pairs={{0,2},{1,3},{2,0},{3,1},{4,6},{5,7},{6,4},{7,5},{8,10},{9,11},{10,... | collective-permute-start | bytes 983048 | tf_op jit(solution)/shard_map/ppermute | solution.py:21
  190.0 16.2 %collective-permute-start.34 = (bf16[256,640]{1,0:T(8,128)(2,1)}, bf16[256,640]{1,0:T(8,128)(2,1)}, u32[]{:S(2)}, u32[]{:S(2)}) collective-permute-start(bf16[256,640]{1,0:T(8,128)(2,1)} %copy-done.8), channel_id=1, source_target_pairs={{0,2},{1,3},{2,0},{3,1},{4,6},{5,7},{6,4},{7,5},{8,10},{9,11},{10,... | collective-permute-start | bytes 983048 | tf_op jit(solution)/shard_map/ppermute | solution.py:21
  190.7 15.4 %collective-permute-start.31 = (bf16[256,640]{1,0:T(8,128)(2,1)}, bf16[256,640]{1,0:T(8,128)(2,1)}, u32[]{:S(2)}, u32[]{:S(2)}) collective-permute-start(bf16[256,640]{1,0:T(8,128)(2,1)} %copy-done.9), channel_id=1, source_target_pairs={{0,4},{4,0},{8,12},{12,8},{16,20},{20,16},{24,28},{28,24},{1,5},{5... | collective-permute-start | bytes 983048 | tf_op jit(solution)/shard_map/ppermute | solution.py:21
  191.5 16.2 %collective-permute-start.25 = (bf16[256,640]{1,0:T(8,128)(2,1)}, bf16[256,640]{1,0:T(8,128)(2,1)}, u32[]{:S(2)}, u32[]{:S(2)}) collective-permute-start(bf16[256,640]{1,0:T(8,128)(2,1)} %copy-done.8), channel_id=1, source_target_pairs={{0,4},{4,0},{8,12},{12,8},{16,20},{20,16},{24,28},{28,24},{1,5},{5... | collective-permute-start | bytes 983048 | tf_op jit(solution)/shard_map/ppermute | solution.py:21
  211.5 20.3 %collective-permute-start.37 = (bf16[256,640]{1,0:T(8,128)(2,1)}, bf16[256,640]{1,0:T(8,128)(2,1)}, u32[]{:S(2)}, u32[]{:S(2)}) collective-permute-start(bf16[256,640]{1,0:T(8,128)(2,1)} %collective-permute-done.34.refs_6_), channel_id=1, source_target_pairs={{0,4},{4,0},{8,12},{12,8},{16,20},{20,16},{24,28},{28,24},{1,5},{5... | collective-permute-start | bytes 983048 | tf_op jit(solution)/shard_map/ppermute | solution.py:21
  212.5 19.8 %collective-permute-start.38 = (bf16[256,640]{1,0:T(8,128)(2,1)S(1)}, bf16[256,640]{1,0:T(8,128)(2,1)}, u32[]{:S(2)}, u32[]{:S(2)}) collective-permute-start(bf16[256,640]{1,0:T(8,128)(2,1)S(1)} %copy-done.6), channel_id=1, source_target_pairs={{0,2},{1,3},{2,0},{3,1},{4,6},{5,7},{6,4},{7,5},{8,10},{9,11},{10,... | collective-permute-start | bytes 983048 | tf_op jit(solution)/shard_map/ppermute | solution.py:21
  220.8 14.3 %collective-permute-start.40 = (bf16[256,640]{1,0:T(8,128)(2,1)}, bf16[256,640]{1,0:T(8,128)(2,1)}, u32[]{:S(2)}, u32[]{:S(2)}) collective-permute-start(bf16[256,640]{1,0:T(8,128)(2,1)} %collective-permute-done.39.refs_10_), channel_id=1, source_target_pairs={{0,4},{4,0},{8,12},{12,8},{16,20},{20,16},{24,28},{28,24},{1,5},{5... | collective-permute-start | bytes 983048 | tf_op jit(solution)/shard_map/ppermute | solution.py:21
  240.9 16.3 %collective-permute-start.46 = (bf16[256,640]{1,0:T(8,128)(2,1)}, bf16[256,640]{1,0:T(8,128)(2,1)}, u32[]{:S(2)}, u32[]{:S(2)}) collective-permute-start(bf16[256,640]{1,0:T(8,128)(2,1)} %collective-permute-done.33.refs_8_), channel_id=1, source_target_pairs={{0,1},{1,0},{2,3},{3,2},{4,5},{5,4},{6,7},{7,6},{8,9},{9,8},{10,11... | collective-permute-start | bytes 983048 | tf_op jit(solution)/shard_map/ppermute | solution.py:21
  240.9 16.3 %collective-permute-start.45 = (bf16[256,640]{1,0:T(8,128)(2,1)}, bf16[256,640]{1,0:T(8,128)(2,1)S(1)}, u32[]{:S(2)}, u32[]{:S(2)}) collective-permute-start(bf16[256,640]{1,0:T(8,128)(2,1)} %collective-permute-done.37.refs_7_), channel_id=1, source_target_pairs={{0,1},{1,0},{2,3},{3,2},{4,5},{5,4},{6,7},{7,6},{8,9},{9,8},{10,11... | collective-permute-start | bytes 983048 | tf_op jit(solution)/shard_map/ppermute | solution.py:21
  241.5 15.8 %collective-permute-start.47 = (bf16[256,640]{1,0:T(8,128)(2,1)}, bf16[256,640]{1,0:T(8,128)(2,1)S(1)}, u32[]{:S(2)}, u32[]{:S(2)}) collective-permute-start(bf16[256,640]{1,0:T(8,128)(2,1)} %collective-permute-done.38.refs_9_), channel_id=1, source_target_pairs={{0,1},{1,0},{2,3},{3,2},{4,5},{5,4},{6,7},{7,6},{8,9},{9,8},{10,11... | collective-permute-start | bytes 983048 | tf_op jit(solution)/shard_map/ppermute | solution.py:21
  241.5 15.7 %collective-permute-start.48 = (bf16[256,640]{1,0:T(8,128)(2,1)}, bf16[256,640]{1,0:T(8,128)(2,1)}, u32[]{:S(2)}, u32[]{:S(2)}) collective-permute-start(bf16[256,640]{1,0:T(8,128)(2,1)} %collective-permute-done.39.refs_10_), channel_id=1, source_target_pairs={{0,1},{1,0},{2,3},{3,2},{4,5},{5,4},{6,7},{7,6},{8,9},{9,8},{10,11... | collective-permute-start | bytes 983048 | tf_op jit(solution)/shard_map/ppermute | solution.py:21
  242.4 14.9 %collective-permute-start.49 = (bf16[256,640]{1,0:T(8,128)(2,1)}, bf16[256,640]{1,0:T(8,128)(2,1)}, u32[]{:S(2)}, u32[]{:S(2)}) collective-permute-start(bf16[256,640]{1,0:T(8,128)(2,1)} %collective-permute-done.40.refs_11_), channel_id=1, source_target_pairs={{0,1},{1,0},{2,3},{3,2},{4,5},{5,4},{6,7},{7,6},{8,9},{9,8},{10,11... | collective-permute-start | bytes 983048 | tf_op jit(solution)/shard_map/ppermute | solution.py:21
  (45 other events, 580.8 us)
Sparse Core Ops, SparseCore 0:
  53.5 38.9 all-gather.4
  94.0 40.4 all-gather.6

commit v4 on v3

--- a/solution.py
+++ b/solution.py
@@ -541,12 +541,19 @@
             sems.at[(g * blocks + k) * layers + l],
         )
 
-    def copy_out(turn):
-        return pltpu.make_async_copy(
-            results.at[lax.rem(turn, 2)],
-            flat.at[:, pl.ds(pl.multiple_of((place[0] ^ turn) * width, LANES), width)],
-            out_sems.at[lax.rem(turn, 2)],
-        )
+    def copies_out(turn):
+        part = rows * layers // 2
+        return [
+            pltpu.make_async_copy(
+                results.at[lax.rem(turn, 2), pl.ds(i * part, part)],
+                flat.at[
+                    pl.ds(i * part, part),
+                    pl.ds(pl.multiple_of((place[0] ^ turn) * width, LANES), width),
+                ],
+                out_sems.at[2 * lax.rem(turn, 2) + i],
+            )
+            for i in range(2)
+        ]
 
     @pl.when(pair == 0)
     def _():
@@ -576,16 +583,18 @@
 
     @pl.when(pair >= 2)
     def _():
-        copy_out(pair - 2).wait()
+        for copy in copies_out(pair - 2):
+            copy.wait()
 
     for c in range(width // LANES):
         results[lax.rem(pair, 2), :, c * LANES:(c + 1) * LANES] = wide[c].astype(BF16)
-    copy_out(pair).start()
+    for copy in copies_out(pair):
+        copy.start()
 
     @pl.when(pair == pairs - 1)
     def _():
-        copy_out(pair - 1).wait()
-        copy_out(pair).wait()
+        for copy in copies_out(pair - 1) + copies_out(pair):
+            copy.wait()
 
 
 def weight_grad(own, far, sources, where, place, scale, scaled, shape):
@@ -616,7 +625,7 @@
                 pltpu.VMEM((width // LANES, rows * layers, LANES), F32),
                 pltpu.VMEM((2, rows * layers, width), BF16),
                 pltpu.SemaphoreType.DMA((groups * blocks * layers,)),
-                pltpu.SemaphoreType.DMA((2,)),
+                pltpu.SemaphoreType.DMA((4,)),
             ],
         ),
         out_shape=jax.ShapeDtypeStruct((rows, layers, full), BF16),
@@ -725,10 +734,10 @@
         err_low, lambda own, near: project(dec_halves[0], own, near, "sum"), over_tok=True
     )
     far.update({k: exchange(err_blocks[k], "tok", 2) for k in (6, 5)})
-    for k in (3, 7):
-        far[k] = exchange(far[k ^ 1], "lat", 1) if aligned else exchange(err_blocks[k], "tok", 2)
     grad, grad_away = project(dec_halves[1], err_own[1], err_near[1], "grad", [sums], mask=mask)
     grad_far = exchange(grad_away, "tok", 2)
+    for k, value in ((3, far[2]), (7, after(far[6], grad_away))):
+        far[k] = exchange(value, "lat", 1) if aligned else exchange(err_blocks[k], "tok", 2)
     error_sums = squared + squares(err_own[1], layers)
     late = (3, 5, 6, 7)
     grad_far, error_sums, *values = lax.optimization_barrier(

time: 281 us -> 275 us (0.979)
  waiting for transfers between devices: 72.6 us -> 68.8 us
    ppermute x51, waiting for transfers between devices: 72.6 us -> 68.7 us  [exchange(): return lax.ppermute(value, axis, [(i, i ^ mask) for i in range(size)])]
  transfers between devices with their start and end apart: 53 -> 53, of which waited for: 20 -> 21; matrix products, arithmetic and copies ran while one was open for 6% -> 6% of each run, Pallas kernels for 38% -> 39%
where the time goes in v4:
time: 275 us; the launch traced here: 274 us
  Pallas kernels  128 us (47%)
  waiting for transfers between devices  68.8 us (25%)
  starting transfers between devices  40.5 us (15%)
  between operations  16.2 us (6%)
  other arithmetic  14.3 us (5%)
  local copies, waits for them, and re-layouts  5.66 us (2%)
    ppermute x51, waiting for transfers between devices, exchange(): return lax.ppermute(value, axis, [(i, i ^ mask) for i in range(size)])  68.7 us
    ppermute x51, starting transfers between devices, exchange(): return lax.ppermute(value, axis, [(i, i ^ mask) for i in range(size)])  40.2 us
    pallas_call x2, Pallas kernels, weight_grad(): pl.pallas_call(functools.partial(grad_kernel, groups=groups, where=where,...  27 us
    pallas_call x2, Pallas kernels, rearrange(): pl.pallas_call(functools.partial(rearrange_kernel, halves=halves, count=c...  26.1 us
    pallas_call x2, Pallas kernels, encode(): pl.pallas_call(functools.partial(encode_kernel, half=half, mode=mode, ear...  24.7 us
    pallas_call x2, Pallas kernels, project(): pl.pallas_call(functools.partial(project_kernel, layers=layers, mode=mode...  16.8 us
    pallas_call x2, Pallas kernels, recon_half(): pl.pallas_call(functools.partial(recon_kernel, parts=parts), grid=(blocks...  15.8 us
    pallas_call x4, Pallas kernels, stack(): pl.pallas_call(stack_kernel, out_shape=jax.ShapeDtypeStruct((len(blocks),...  9.84 us
  transfers between devices with their start and end apart: 53, of which 21 were waited for; matrix products, arithmetic and copies ran while one was open for 6% of the time, Pallas kernels for 39%

profile of v4, /device:TPU:0, one launch (start us, length us, event | category | flops | bytes accessed | tf_op | source)
XLA Modules:
  0.0 273.8 jit_solution(11173381463208963807)
XLA Ops:
  8.2 3.1 %collective-permute-start = (bf16[256,640]{1,0:T(8,128)(2,1)S(1)}, bf16[256,640]{1,0:T(8,128)(2,1)}, u32[]{:S(2)}, u32[]{:S(2)}) collective-permute-start(bf16[256,640]{1,0:T(8,128)(2,1)S(1)} %bitcast.47), channel_id=1, source_target_pairs={{0,8},{4,12},{8,0},{12,4},{16,24},{20,28},{24,16},{28,20},{1,9},{5... | collective-permute-start | bytes 983048 | tf_op jit(solution)/shard_map/ppermute | solution.py:21
  11.3 2.6 collective-permute-start.1
  18.2 13.1 %rearrange.2 = (bf16[2,1024,2560]{2,1,0:T(8,128)(2,1)}, bf16[2,1024,2560]{2,1,0:T(8,128)(2,1)}) custom-call(s32[2]{0:T(128)} %pad_add_fusion.1.place, bf16[2048,2,5120]{2,1,0:T(2,128)(2,1)} %refs_1_.3, bf16[2048,2,5120]{2,1,0:T(2,128)(2,1)} %refs_1_.3), custom_call_target="tpu_custom_call" | custom-call | flops 1024 | bytes 1024 | tf_op jit(solution)/shard_map/rearrange/pallas_call | solution.py:347
  35.8 13.0 %rearrange.3 = (bf16[2,1024,2560]{2,1,0:T(8,128)(2,1)}, bf16[2,1024,2560]{2,1,0:T(8,128)(2,1)}) custom-call(s32[2]{0:T(128)} %pad_add_fusion.1.place, bf16[2048,2,5120]{2,1,0:T(2,128)(2,1)} %refs_1_.3, bf16[2048,2,5120]{2,1,0:T(2,128)(2,1)} %refs_1_.3, ...), custom_call_target="tpu_custom_call", output_to_operand_aliasing={{0}: (3, {}), {1}: (4, {})} | custom-call | flops 1024 | bytes 1024 | tf_op jit(solution)/shard_map/rearrange/pallas_call | solution.py:347
  48.8 2.1 collective-permute-done.6.refs_1_
  50.9 2.4 stack.29.ref.refs_0_
  54.3 2.0 squares.4
  57.1 12.4 %encode_parts.1.refs_2_ = f32[2,1024,256]{2,1,0:T(8,128)} custom-call(s32[2]{0:T(128)} %pad_add_fusion.1.place, bf16[2048,2,5120]{2,1,0:T(2,128)(2,1)} %w_ref.3, bf16[4,256,640]{2,1,0:T(8,128)(2,1)} %stack.29.ref.refs_0_, bf16[4,256,640]{2,1,0:T(8,128)(2,1)} %collective-permute-done.8.refs_1_), custom_call_target="tpu_custom_call" | custom-call | flops 1024 | bytes 1024 | tf_op jit(solution)/shard_map/encode_parts/pallas_call | solution.py:290
  70.3 2.5 stack.30.ref.refs_0_
  72.8 2.0 squares.5
  81.4 12.3 %encode_act.1 = (bf16[256,1024]{1,0:T(8,128)(2,1)}, bf16[1024,256]{1,0:T(8,128)(2,1)}) custom-call(s32[2]{0:T(128)} %pad_add_fusion.1.place, bf16[2048,2,5120]{2,1,0:T(2,128)(2,1)} %w_ref.3, bf16[4,256,640]{2,1,0:T(8,128)(2,1)} %stack.30.ref.refs_0_, bf16[4,256,640]{2,1,0:T(8,128)(2,1)} %collective-permute-done.11.refs_1_, ...), custom_call_target="tpu_custom_call" | custom-call | flops 1024 | bytes 1024 | tf_op jit(solution)/shard_map/encode_act/pallas_call | solution.py:290
  93.7 7.9 %recon_half.2 = (f32[4,256,640]{2,1,0:T(8,128)}, bf16[4,256,640]{2,1,0:T(8,128)(2,1)}) custom-call(bf16[256,1024]{1,0:T(8,128)(2,1)} %get-tuple-element.46.act_ref, bf16[2,1024,2560]{2,1,0:T(8,128)(2,1)} %get-tuple-element.40.refs_0_.refs_1_, bf16[2,1024,2560]{2,1,0:T(8,128)(2,1)} %get-tuple-element.40.refs_0_.refs_1_), custom_call_target="tpu_custom_call" | custom-call | flops 1024 | bytes 1024 | tf_op jit(solution)/shard_map/recon_half/pallas_call | solution.py:503
  101.5 3.2 %collective-permute-done.12 = bf16[4,256,640]{2,1,0:T(8,128)(2,1)S(1)} collective-permute-done((bf16[4,256,640]{2,1,0:T(8,128)(2,1)}, bf16[4,256,640]{2,1,0:T(8,128)(2,1)S(1)}, u32[]{:S(2)}, u32[]{:S(2)}) %collective-permute-start.12) | collective-permute-done | bytes 1310752 | tf_op jit(solution)/shard_map/ppermute | solution.py:21
  104.8 2.1 add_convert_fusion
  108.6 8.0 %recon_half.3 = (f32[4,256,640]{2,1,0:T(8,128)}, bf16[256,640]{1,0:T(8,128)(2,1)}, bf16[256,640]{1,0:T(8,128)(2,1)}, bf16[256,640]{1,0:T(8,128)(2,1)}, bf16[256,640]{1,0:T(8,128)(2,1)}) custom-call(bf16[256,1024]{1,0:T(8,128)(2,1)} %get-tuple-element.46.act_ref, bf16[2,1024,2560]{2,1,0:T(8,128)(2,1)} %get-tuple-element.39.refs_0_.refs_1_, ...), custom_call_target="tpu_custom_call" | custom-call | flops 1024 | bytes 1024 | tf_op jit(solution)/shard_map/recon_half/pallas_call | solution.py:503
  118.4 7.4 %collective-permute-done.16 = bf16[2,256,640]{2,1,0:T(8,128)(2,1)} collective-permute-done((bf16[2,256,640]{2,1,0:T(8,128)(2,1)}, bf16[2,256,640]{2,1,0:T(8,128)(2,1)}, u32[]{:S(2)}, u32[]{:S(2)}) %collective-permute-start.16) | collective-permute-done | bytes 655392 | tf_op jit(solution)/shard_map/ppermute | solution.py:21
  129.1 9.8 %collective-permute-done.14 = bf16[2,256,640]{2,1,0:T(8,128)(2,1)S(1)} collective-permute-done((bf16[2,256,640]{2,1,0:T(8,128)(2,1)S(1)}, bf16[2,256,640]{2,1,0:T(8,128)(2,1)S(1)}, u32[]{:S(2)}, u32[]{:S(2)}) %collective-permute-start.14) | collective-permute-done | bytes 655392 | tf_op jit(solution)/shard_map/ppermute | solution.py:21
  144.9 12.6 %collective-permute-done.21 = bf16[256,640]{1,0:T(8,128)(2,1)S(1)} collective-permute-done((bf16[256,640]{1,0:T(8,128)(2,1)S(1)}, bf16[256,640]{1,0:T(8,128)(2,1)S(1)}, u32[]{:S(2)}, u32[]{:S(2)}) %collective-permute-start.21) | collective-permute-done | bytes 327712 | tf_op jit(solution)/shard_map/ppermute | solution.py:21
  159.9 3.2 %collective-permute-start.26 = (bf16[256,640]{1,0:T(8,128)(2,1)S(1)}, bf16[256,640]{1,0:T(8,128)(2,1)S(1)}, u32[]{:S(2)}, u32[]{:S(2)}) collective-permute-start(bf16[256,640]{1,0:T(8,128)(2,1)S(1)} %bitcast.53), channel_id=1, source_target_pairs={{0,16},{4,20},{8,24},{12,28},{16,0},{20,4},{24,8},{28,12},{1,17},{... | collective-permute-start | bytes 983048 | tf_op jit(solution)/shard_map/ppermute | solution.py:21
  164.6 3.2 %collective-permute-done.23.refs_0_ = bf16[256,640]{1,0:T(8,128)(2,1)S(1)} collective-permute-done((bf16[256,640]{1,0:T(8,128)(2,1)S(1)}, bf16[256,640]{1,0:T(8,128)(2,1)S(1)}, u32[]{:S(2)}, u32[]{:S(2)}) %collective-permute-start.23) | collective-permute-done | bytes 327712 | tf_op jit(solution)/shard_map/ppermute | solution.py:21
  167.8 7.0 %collective-permute-done.24.refs_1_ = bf16[256,640]{1,0:T(8,128)(2,1)S(1)} collective-permute-done((bf16[256,640]{1,0:T(8,128)(2,1)S(1)}, bf16[256,640]{1,0:T(8,128)(2,1)S(1)}, u32[]{:S(2)}, u32[]{:S(2)}) %collective-permute-start.24) | collective-permute-done | bytes 327712 | tf_op jit(solution)/shard_map/ppermute | solution.py:21
  179.0 5.2 %collective-permute-done.28.refs_2_ = bf16[256,640]{1,0:T(8,128)(2,1)S(1)} collective-permute-done((bf16[256,640]{1,0:T(8,128)(2,1)S(1)}, bf16[256,640]{1,0:T(8,128)(2,1)S(1)}, u32[]{:S(2)}, u32[]{:S(2)}) %collective-permute-start.28) | collective-permute-done | bytes 327712 | tf_op jit(solution)/shard_map/ppermute | solution.py:21
  186.0 2.5 stack.31.refs_2_.ref.refs_0_
  194.5 8.1 %project_sum.1.refs_4_ = f32[1024,256]{1,0:T(8,128)} custom-call(bf16[2,1024,2560]{2,1,0:T(8,128)(2,1)} %get-tuple-element.39.refs_0_.refs_1_, bf16[2,1024,2560]{2,1,0:T(8,128)(2,1)} %get-tuple-element.39.refs_0_.refs_1_, bf16[4,256,640]{2,1,0:T(8,128)(2,1)} %stack.31.refs_2_.ref.refs_0_, bf16[4,256,640]{2,1,0:T(8,128)(2,1)} %collective-permute-done.32.refs_3_.refs_2_), custom_call_target="tpu_custom_call" | custom-call | flops 1024 | bytes 1024 | tf_op jit(solution)/shard_map/project_sum/pallas_call | solution.py:437
  202.7 3.3 %collective-permute-done.34.refs_6_ = bf16[256,640]{1,0:T(8,128)(2,1)} collective-permute-done((bf16[256,640]{1,0:T(8,128)(2,1)}, bf16[256,640]{1,0:T(8,128)(2,1)}, u32[]{:S(2)}, u32[]{:S(2)}) %collective-permute-start.34) | collective-permute-done | bytes 327712 | tf_op jit(solution)/shard_map/ppermute | solution.py:21
  207.4 2.4 stack.32.refs_2_.ref.refs_1_
  213.2 8.7 %project_grad.1 = (bf16[512,256]{1,0:T(8,128)(2,1)}, bf16[512,256]{1,0:T(8,128)(2,1)}) custom-call(bf16[2,1024,2560]{2,1,0:T(8,128)(2,1)} %get-tuple-element.40.refs_0_.refs_1_, bf16[2,1024,2560]{2,1,0:T(8,128)(2,1)} %get-tuple-element.40.refs_0_.refs_1_, bf16[4,256,640]{2,1,0:T(8,128)(2,1)} %stack.32.refs_2_.ref.refs_1_, ...), custom_call_target="tpu_custom_call" | custom-call | flops 1024 | bytes 1024 | tf_op jit(solution)/shard_map/project_grad/pallas_call | solution.py:437
  224.8 2.8 %collective-permute-done.38.refs_9_ = bf16[256,640]{1,0:T(8,128)(2,1)} collective-permute-done((bf16[256,640]{1,0:T(8,128)(2,1)S(1)}, bf16[256,640]{1,0:T(8,128)(2,1)}, u32[]{:S(2)}, u32[]{:S(2)}) %collective-permute-start.38) | collective-permute-done | bytes 327712 | tf_op jit(solution)/shard_map/ppermute | solution.py:21
  227.6 2.0 squares.7
  230.3 2.3 collective-permute-done.36.far_ref
  237.5 13.6 %weight_grad.2 = bf16[512,2,5120]{2,1,0:T(2,128)(2,1)} custom-call(s32[3]{0:T(128)} %pad_add_fusion.place, f32[2]{0:T(128)} %add_rsqrt_fusion.refs_3_.scale_ref, bf16[512,256]{1,0:T(8,128)(2,1)} %get-tuple-element.58.own_ref, bf16[512,256]{1,0:T(8,128)(2,1)} %copy-done.21, bf16[4,4,256,640]{3,2,1,0:T(8,128)(2,1)} %bitcast.58, bf16[4,4,256,640]{3,2,1,0:T(8,128)(2,1)} %bitcast.59), custom_call_target="tpu_custom_call" | custom-call | flops 10737418240 | bytes 41943040 | tf_op jit(solution)/shard_map/weight_grad/pallas_call | solution.py:608
  252.4 13.4 %weight_grad.3 = bf16[512,2,5120]{2,1,0:T(2,128)(2,1)} custom-call(s32[3]{0:T(128)} %pad_add_fusion.place, f32[2]{0:T(128)} %add_rsqrt_fusion.refs_3_.scale_ref, bf16[1024,256]{1,0:T(8,128)(2,1)} %get-tuple-element.63.own_ref, bf16[512,256]{1,0:T(8,128)(2,1)} %copy-done.20, bf16[4,256,640]{2,1,0:T(8,128)(2,1)} %stack.31.refs_2_.ref.refs_0_, ...), custom_call_target="tpu_custom_call" | custom-call | flops 10737418240 | bytes 41943040 | tf_op jit(solution)/shard_map/weight_grad/pallas_call | solution.py:608
  (163 shorter events, 61.3 us)
Async XLA Ops:
  7.2 151.6 %all-gather.5.cloned.1.call-start = ((), (), s32[]{:S(2)}) async-start(), calls=%async_computation | async-start | bytes 6553600 | tf_op jit(solution)/shard_map/all_gather | solution.py:695
  8.2 25.0 %collective-permute-start = (bf16[256,640]{1,0:T(8,128)(2,1)S(1)}, bf16[256,640]{1,0:T(8,128)(2,1)}, u32[]{:S(2)}, u32[]{:S(2)}) collective-permute-start(bf16[256,640]{1,0:T(8,128)(2,1)S(1)} %bitcast.47), channel_id=1, source_target_pairs={{0,8},{4,12},{8,0},{12,4},{16,24},{20,28},{24,16},{28,20},{1,9},{5... | collective-permute-start | bytes 983048 | tf_op jit(solution)/shard_map/ppermute | solution.py:21
  11.3 21.9 %collective-permute-start.1 = (bf16[256,640]{1,0:T(8,128)(2,1)S(1)}, bf16[256,640]{1,0:T(8,128)(2,1)}, u32[]{:S(2)}, u32[]{:S(2)}) collective-permute-start(bf16[256,640]{1,0:T(8,128)(2,1)S(1)} %bitcast.48), channel_id=1, source_target_pairs={{0,16},{4,20},{8,24},{12,28},{16,0},{20,4},{24,8},{28,12},{1,17},{... | collective-permute-start | bytes 983048 | tf_op jit(solution)/shard_map/ppermute | solution.py:21
  13.9 19.3 %collective-permute-start.2 = (bf16[256,640]{1,0:T(8,128)(2,1)S(1)}, bf16[256,640]{1,0:T(8,128)(2,1)S(1)}, u32[]{:S(2)}, u32[]{:S(2)}) collective-permute-start(bf16[256,640]{1,0:T(8,128)(2,1)S(1)} %bitcast.49), channel_id=1, source_target_pairs={{0,4},{4,0},{8,12},{12,8},{16,20},{20,16},{24,28},{28,24},{1,5},{5... | collective-permute-start | bytes 983048 | tf_op jit(solution)/shard_map/ppermute | solution.py:21
  17.5 13.9 %collective-permute-start.3 = (bf16[128,1024]{1,0:T(8,128)(2,1)}, bf16[128,1024]{1,0:T(8,128)(2,1)}, u32[]{:S(2)}, u32[]{:S(2)}) collective-permute-start(bf16[128,1024]{1,0:T(8,128)(2,1)} %pad_maximum_fusion.1), channel_id=1, source_target_pairs={{0,1},{1,0},{2,3},{3,2},{4,5},{5,4},{6,7},{7,6},{8,9},{9,8},{10,11... | collective-permute-start | bytes 786440 | tf_op jit(solution)/shard_map/ppermute | solution.py:21
  33.2 15.6 %collective-permute-start.4 = (bf16[256,640]{1,0:T(8,128)(2,1)}, bf16[256,640]{1,0:T(8,128)(2,1)}, u32[]{:S(2)}, u32[]{:S(2)}) collective-permute-start(bf16[256,640]{1,0:T(8,128)(2,1)} %collective-permute-done.1.refs_2_), channel_id=1, source_target_pairs={{0,8},{4,12},{8,0},{12,4},{16,24},{20,28},{24,16},{28,20},{1,9},{5... | collective-permute-start | bytes 983048 | tf_op jit(solution)/shard_map/ppermute | solution.py:21
  33.8 15.0 %collective-permute-start.5 = (bf16[256,640]{1,0:T(8,128)(2,1)}, bf16[256,640]{1,0:T(8,128)(2,1)S(1)}, u32[]{:S(2)}, u32[]{:S(2)}) collective-permute-start(bf16[256,640]{1,0:T(8,128)(2,1)} %collective-permute-done.1.refs_2_), channel_id=1, source_target_pairs={{0,4},{4,0},{8,12},{12,8},{16,20},{20,16},{24,28},{28,24},{1,5},{5... | collective-permute-start | bytes 983048 | tf_op jit(solution)/shard_map/ppermute | solution.py:21
  34.3 16.6 %collective-permute-start.6 = (bf16[256,640]{1,0:T(8,128)(2,1)}, bf16[256,640]{1,0:T(8,128)(2,1)}, u32[]{:S(2)}, u32[]{:S(2)}) collective-permute-start(bf16[256,640]{1,0:T(8,128)(2,1)} %collective-permute-done.refs_1_), channel_id=1, source_target_pairs={{0,4},{4,0},{8,12},{12,8},{16,20},{20,16},{24,28},{28,24},{1,5},{5... | collective-permute-start | bytes 983048 | tf_op jit(solution)/shard_map/ppermute | solution.py:21
  53.4 105.4 %all-gather.7.cloned.1.call-start = ((), (), s32[]{:S(2)}) async-start(), calls=%async_computation.1 | async-start | bytes 6553600 | tf_op jit(solution)/shard_map/all_gather | solution.py:695
  53.7 15.8 %collective-permute-start.7 = (bf16[256,640]{1,0:T(8,128)(2,1)}, bf16[256,640]{1,0:T(8,128)(2,1)S(1)}, u32[]{:S(2)}, u32[]{:S(2)}) collective-permute-start(bf16[256,640]{1,0:T(8,128)(2,1)} %collective-permute-done.4.refs_3_), channel_id=1, source_target_pairs={{0,4},{4,0},{8,12},{12,8},{16,20},{20,16},{24,28},{28,24},{1,5},{5... | collective-permute-start | bytes 983048 | tf_op jit(solution)/shard_map/ppermute | solution.py:21
  107.9 17.9 %collective-permute-start.16 = (bf16[2,256,640]{2,1,0:T(8,128)(2,1)}, bf16[2,256,640]{2,1,0:T(8,128)(2,1)}, u32[]{:S(2)}, u32[]{:S(2)}) collective-permute-start(bf16[2,256,640]{2,1,0:T(8,128)(2,1)} %get-tuple-element.72), channel_id=1, source_target_pairs={{0,4},{4,0},{8,12},{12,8},{16,20},{20,16},{24,28},{28,24},{1,5},{5... | collective-permute-start | bytes 1966088 | tf_op jit(solution)/shard_map/ppermute | solution.py:21
  116.6 22.3 %collective-permute-start.14 = (bf16[2,256,640]{2,1,0:T(8,128)(2,1)S(1)}, bf16[2,256,640]{2,1,0:T(8,128)(2,1)S(1)}, u32[]{:S(2)}, u32[]{:S(2)}) collective-permute-start(bf16[2,256,640]{2,1,0:T(8,128)(2,1)S(1)} %get-tuple-element.71), channel_id=1, source_target_pairs={{0,4},{4,0},{8,12},{12,8},{16,20},{20,16},{24,28},{28,24},{1,5},{5... | collective-permute-start | bytes 1966088 | tf_op jit(solution)/shard_map/ppermute | solution.py:21
  129.1 15.8 %collective-permute-start.13 = (bf16[256,640]{1,0:T(8,128)(2,1)}, bf16[256,640]{1,0:T(8,128)(2,1)S(1)}, u32[]{:S(2)}, u32[]{:S(2)}) collective-permute-start(bf16[256,640]{1,0:T(8,128)(2,1)} %get-tuple-element.48), channel_id=1, source_target_pairs={{0,1},{1,0},{2,3},{3,2},{4,5},{5,4},{6,7},{7,6},{8,9},{9,8},{10,11... | collective-permute-start | bytes 983048 | tf_op jit(solution)/shard_map/ppermute | solution.py:21
  140.6 16.9 %collective-permute-start.21 = (bf16[256,640]{1,0:T(8,128)(2,1)S(1)}, bf16[256,640]{1,0:T(8,128)(2,1)S(1)}, u32[]{:S(2)}, u32[]{:S(2)}) collective-permute-start(bf16[256,640]{1,0:T(8,128)(2,1)S(1)} %get-tuple-element.70), channel_id=1, source_target_pairs={{0,16},{4,20},{8,24},{12,28},{16,0},{20,4},{24,8},{28,12},{1,17},{... | collective-permute-start | bytes 983048 | tf_op jit(solution)/shard_map/ppermute | solution.py:21
  140.7 16.8 %collective-permute-start.19 = (bf16[256,640]{1,0:T(8,128)(2,1)S(1)}, bf16[256,640]{1,0:T(8,128)(2,1)S(1)}, u32[]{:S(2)}, u32[]{:S(2)}) collective-permute-start(bf16[256,640]{1,0:T(8,128)(2,1)S(1)} %get-tuple-element.69), channel_id=1, source_target_pairs={{0,8},{4,12},{8,0},{12,4},{16,24},{20,28},{24,16},{28,20},{1,9},{5... | collective-permute-start | bytes 983048 | tf_op jit(solution)/shard_map/ppermute | solution.py:21
  143.3 15.5 %collective-permute-start.22 = (bf16[512,256]{1,0:T(8,128)(2,1)S(1)}, bf16[512,256]{1,0:T(8,128)(2,1)S(1)}, u32[]{:S(2)}, u32[]{:S(2)}) collective-permute-start(bf16[512,256]{1,0:T(8,128)(2,1)S(1)} %slice.45), channel_id=1, source_target_pairs={{0,2},{1,3},{2,0},{3,1},{4,6},{5,7},{6,4},{7,5},{8,10},{9,11},{10,... | collective-permute-start | bytes 786440 | tf_op jit(solution)/shard_map/ppermute | solution.py:21
  159.9 15.0 %collective-permute-start.24 = (bf16[256,640]{1,0:T(8,128)(2,1)S(1)}, bf16[256,640]{1,0:T(8,128)(2,1)S(1)}, u32[]{:S(2)}, u32[]{:S(2)}) collective-permute-start(bf16[256,640]{1,0:T(8,128)(2,1)S(1)} %bitcast.52), channel_id=1, source_target_pairs={{0,8},{4,12},{8,0},{12,4},{16,24},{20,28},{24,16},{28,20},{1,9},{5... | collective-permute-start | bytes 983048 | tf_op jit(solution)/shard_map/ppermute | solution.py:21
  159.9 16.3 %collective-permute-start.26 = (bf16[256,640]{1,0:T(8,128)(2,1)S(1)}, bf16[256,640]{1,0:T(8,128)(2,1)S(1)}, u32[]{:S(2)}, u32[]{:S(2)}) collective-permute-start(bf16[256,640]{1,0:T(8,128)(2,1)S(1)} %bitcast.53), channel_id=1, source_target_pairs={{0,16},{4,20},{8,24},{12,28},{16,0},{20,4},{24,8},{28,12},{1,17},{... | collective-permute-start | bytes 983048 | tf_op jit(solution)/shard_map/ppermute | solution.py:21
  163.0 13.1 %collective-permute-start.27 = (bf16[256,640]{1,0:T(8,128)(2,1)S(1)}, bf16[256,640]{1,0:T(8,128)(2,1)S(1)}, u32[]{:S(2)}, u32[]{:S(2)}) collective-permute-start(bf16[256,640]{1,0:T(8,128)(2,1)S(1)} %bitcast.54), channel_id=1, source_target_pairs={{0,2},{1,3},{2,0},{3,1},{4,6},{5,7},{6,4},{7,5},{8,10},{9,11},{10,... | collective-permute-start | bytes 983048 | tf_op jit(solution)/shard_map/ppermute | solution.py:21
  188.5 14.2 %collective-permute-start.33 = (bf16[256,640]{1,0:T(8,128)(2,1)}, bf16[256,640]{1,0:T(8,128)(2,1)}, u32[]{:S(2)}, u32[]{:S(2)}) collective-permute-start(bf16[256,640]{1,0:T(8,128)(2,1)} %copy-done.11), channel_id=1, source_target_pairs={{0,2},{1,3},{2,0},{3,1},{4,6},{5,7},{6,4},{7,5},{8,10},{9,11},{10,... | collective-permute-start | bytes 983048 | tf_op jit(solution)/shard_map/ppermute | solution.py:21
  189.8 16.2 %collective-permute-start.34 = (bf16[256,640]{1,0:T(8,128)(2,1)}, bf16[256,640]{1,0:T(8,128)(2,1)}, u32[]{:S(2)}, u32[]{:S(2)}) collective-permute-start(bf16[256,640]{1,0:T(8,128)(2,1)} %copy-done.10), channel_id=1, source_target_pairs={{0,2},{1,3},{2,0},{3,1},{4,6},{5,7},{6,4},{7,5},{8,10},{9,11},{10,... | collective-permute-start | bytes 983048 | tf_op jit(solution)/shard_map/ppermute | solution.py:21
  190.5 15.4 %collective-permute-start.31 = (bf16[256,640]{1,0:T(8,128)(2,1)}, bf16[256,640]{1,0:T(8,128)(2,1)}, u32[]{:S(2)}, u32[]{:S(2)}) collective-permute-start(bf16[256,640]{1,0:T(8,128)(2,1)} %copy-done.8), channel_id=1, source_target_pairs={{0,4},{4,0},{8,12},{12,8},{16,20},{20,16},{24,28},{28,24},{1,5},{5... | collective-permute-start | bytes 983048 | tf_op jit(solution)/shard_map/ppermute | solution.py:21
  191.2 16.2 %collective-permute-start.25 = (bf16[256,640]{1,0:T(8,128)(2,1)}, bf16[256,640]{1,0:T(8,128)(2,1)}, u32[]{:S(2)}, u32[]{:S(2)}) collective-permute-start(bf16[256,640]{1,0:T(8,128)(2,1)} %copy-done.10), channel_id=1, source_target_pairs={{0,4},{4,0},{8,12},{12,8},{16,20},{20,16},{24,28},{28,24},{1,5},{5... | collective-permute-start | bytes 983048 | tf_op jit(solution)/shard_map/ppermute | solution.py:21
  209.8 12.0 %collective-permute-start.39 = (bf16[256,640]{1,0:T(8,128)(2,1)S(1)}, bf16[256,640]{1,0:T(8,128)(2,1)}, u32[]{:S(2)}, u32[]{:S(2)}) collective-permute-start(bf16[256,640]{1,0:T(8,128)(2,1)S(1)} %copy-done.9), channel_id=1, source_target_pairs={{0,2},{1,3},{2,0},{3,1},{4,6},{5,7},{6,4},{7,5},{8,10},{9,11},{10,... | collective-permute-start | bytes 983048 | tf_op jit(solution)/shard_map/ppermute | solution.py:21
  211.2 13.1 %collective-permute-start.37 = (bf16[256,640]{1,0:T(8,128)(2,1)}, bf16[256,640]{1,0:T(8,128)(2,1)}, u32[]{:S(2)}, u32[]{:S(2)}) collective-permute-start(bf16[256,640]{1,0:T(8,128)(2,1)} %collective-permute-done.34.refs_6_), channel_id=1, source_target_pairs={{0,4},{4,0},{8,12},{12,8},{16,20},{20,16},{24,28},{28,24},{1,5},{5... | collective-permute-start | bytes 983048 | tf_op jit(solution)/shard_map/ppermute | solution.py:21
  212.2 15.3 %collective-permute-start.38 = (bf16[256,640]{1,0:T(8,128)(2,1)S(1)}, bf16[256,640]{1,0:T(8,128)(2,1)}, u32[]{:S(2)}, u32[]{:S(2)}) collective-permute-start(bf16[256,640]{1,0:T(8,128)(2,1)S(1)} %copy-done.6), channel_id=1, source_target_pairs={{0,2},{1,3},{2,0},{3,1},{4,6},{5,7},{6,4},{7,5},{8,10},{9,11},{10,... | collective-permute-start | bytes 983048 | tf_op jit(solution)/shard_map/ppermute | solution.py:21
  224.3 12.0 %collective-permute-start.43 = (bf16[256,640]{1,0:T(8,128)(2,1)}, bf16[256,640]{1,0:T(8,128)(2,1)}, u32[]{:S(2)}, u32[]{:S(2)}) collective-permute-start(bf16[256,640]{1,0:T(8,128)(2,1)} %collective-permute-done.30.refs_5_), channel_id=1, source_target_pairs={{0,1},{1,0},{2,3},{3,2},{4,5},{5,4},{6,7},{7,6},{8,9},{9,8},{10,11... | collective-permute-start | bytes 983048 | tf_op jit(solution)/shard_map/ppermute | solution.py:21
  235.8 16.6 %collective-permute-start.46 = (bf16[256,640]{1,0:T(8,128)(2,1)}, bf16[256,640]{1,0:T(8,128)(2,1)}, u32[]{:S(2)}, u32[]{:S(2)}) collective-permute-start(bf16[256,640]{1,0:T(8,128)(2,1)} %collective-permute-done.33.refs_8_), channel_id=1, source_target_pairs={{0,1},{1,0},{2,3},{3,2},{4,5},{5,4},{6,7},{7,6},{8,9},{9,8},{10,11... | collective-permute-start | bytes 983048 | tf_op jit(solution)/shard_map/ppermute | solution.py:21
  235.8 16.6 %collective-permute-start.45 = (bf16[256,640]{1,0:T(8,128)(2,1)}, bf16[256,640]{1,0:T(8,128)(2,1)}, u32[]{:S(2)}, u32[]{:S(2)}) collective-permute-start(bf16[256,640]{1,0:T(8,128)(2,1)} %collective-permute-done.37.refs_7_), channel_id=1, source_target_pairs={{0,1},{1,0},{2,3},{3,2},{4,5},{5,4},{6,7},{7,6},{8,9},{9,8},{10,11... | collective-permute-start | bytes 983048 | tf_op jit(solution)/shard_map/ppermute | solution.py:21
  236.3 16.1 %collective-permute-start.47 = (bf16[256,640]{1,0:T(8,128)(2,1)}, bf16[256,640]{1,0:T(8,128)(2,1)}, u32[]{:S(2)}, u32[]{:S(2)}) collective-permute-start(bf16[256,640]{1,0:T(8,128)(2,1)} %collective-permute-done.38.refs_9_), channel_id=1, source_target_pairs={{0,1},{1,0},{2,3},{3,2},{4,5},{5,4},{6,7},{7,6},{8,9},{9,8},{10,11... | collective-permute-start | bytes 983048 | tf_op jit(solution)/shard_map/ppermute | solution.py:21
  236.4 16.0 %collective-permute-start.48 = (bf16[256,640]{1,0:T(8,128)(2,1)}, bf16[256,640]{1,0:T(8,128)(2,1)}, u32[]{:S(2)}, u32[]{:S(2)}) collective-permute-start(bf16[256,640]{1,0:T(8,128)(2,1)} %collective-permute-done.39.refs_10_), channel_id=1, source_target_pairs={{0,1},{1,0},{2,3},{3,2},{4,5},{5,4},{6,7},{7,6},{8,9},{9,8},{10,11... | collective-permute-start | bytes 983048 | tf_op jit(solution)/shard_map/ppermute | solution.py:21
  237.5 14.9 %collective-permute-start.49 = (bf16[256,640]{1,0:T(8,128)(2,1)S(1)}, bf16[256,640]{1,0:T(8,128)(2,1)}, u32[]{:S(2)}, u32[]{:S(2)}) collective-permute-start(bf16[256,640]{1,0:T(8,128)(2,1)S(1)} %collective-permute-done.40.refs_11_), channel_id=1, source_target_pairs={{0,1},{1,0},{2,3},{3,2},{4,5},{5,4},{6,7},{7,6},{8,9},{9,8},{10,11... | collective-permute-start | bytes 983048 | tf_op jit(solution)/shard_map/ppermute | solution.py:21
  (43 other events, 580.6 us)
Sparse Core Ops, SparseCore 0:
  53.5 38.8 all-gather.4
  94.0 40.4 all-gather.6

commit v5 on v4

--- a/solution.py
+++ b/solution.py
@@ -26,11 +26,10 @@
 
 
 def sum_tokens(value):
-    step = 1
-    while step < lax.axis_size("tok"):
-        value = value + exchange(value, "tok", step)
-        step *= 2
-    return value
+    sums = [value] + [exchange(value, "tok", g) for g in range(1, lax.axis_size("tok"))]
+    while len(sums) > 1:
+        sums = [sums[i] + sums[i + 1] for i in range(0, len(sums), 2)]
+    return sums[0]
 
 
 def squares_kernel(ref, out_ref):
@@ -697,12 +696,17 @@
 
     bias_part = lax.dynamic_slice_in_dim(dec_bias, me * width_part, width_part, 1)
     keep, send = recon_half(act_across, dec_halves[1], block_count // 2, False)
-    cross = keep + exchange(send[0], "tok", 1).astype(F32)
+    send = exchange(send[0], "tok", 1)
     starts = range(block_count // 2 - 2, -2, -2)
     if aligned:
-        bundles = [cross[start:start + 2].astype(BF16) for start in starts]
+        bundles = [
+            (keep[start:start + 2] + send[start:start + 2].astype(F32)).astype(BF16)
+            for start in starts
+        ]
         act_across = after(act_across, *bundles)
         bundles = [exchange(bundle, "lat", 1) for bundle in bundles]
+    else:
+        cross = keep + send.astype(F32)
     keep, send = recon_half(act_across, dec_halves[0], block_count // 2, True)
     send = [exchange(value, "tok", 1) for value in send]
     act_far = exchange(act[quarter:], "tok", 2)
@@ -753,14 +757,13 @@
         grad, grad_far, x_all, [(None, spot) for spot in order] * tok_count, place,
         norm_scale, True, shape,
     )
-    error_sums = error_sums + exchange(error_sums, "tok", 1)
+    error_sums = sum_tokens(error_sums)
     act, error_sums = lax.optimization_barrier((act, error_sums))
     where = [(2 * g + h, i) for g in range(2) for h, i in order]
     where += [(4 + g * block_count + k, -1) for g in range(2) for k in range(block_count)]
     sources = err_own + err_near + [group[k] for group in (far, last) for k in range(block_count)]
     dec_grad = weight_grad(act, act_far, sources, where, place, norm_scale, False, shape)
-    error_sum = jnp.sum(error_sums + exchange(error_sums, "tok", 2))
-    mean_error = error_sum / (factor * factor * tokens * layers * full_width)
+    mean_error = jnp.sum(error_sums) / (factor * factor * tokens * layers * full_width)
     return (enc_grad, dec_grad, mean_error)
 
 

time: 275 us -> 275 us (level)
    convert_element_type x0 -> x1, other arithmetic: none -> 2.9 us  [per_device(): (keep[start:start + 2] + send[start:start + 2].astype(F32)).astype(BF16)]
    ppermute x51 -> x53, starting transfers between devices: 40.2 us -> 40.6 us  [exchange(): return lax.ppermute(value, axis, [(i, i ^ mask) for i in range(size)])]
    ppermute x51 -> x53, waiting for transfers between devices: 68.7 us -> 68.3 us  [exchange(): return lax.ppermute(value, axis, [(i, i ^ mask) for i in range(size)])]
  transfers between devices with their start and end apart: 53 -> 55, of which waited for: 21 -> 21; matrix products, arithmetic and copies ran while one was open for 6% -> 6% of each run, Pallas kernels for 39% -> 39%
where the time goes in v5:
time: 275 us; the launch traced here: 273 us
  Pallas kernels  128 us (47%)
  waiting for transfers between devices  68.4 us (25%)
  starting transfers between devices  40.9 us (15%)
  between operations  16.2 us (6%)
  other arithmetic  15 us (5%)
  local copies, waits for them, and re-layouts  4.69 us (2%)
    ppermute x53, waiting for transfers between devices, exchange(): return lax.ppermute(value, axis, [(i, i ^ mask) for i in range(size)])  68.3 us
    ppermute x53, starting transfers between devices, exchange(): return lax.ppermute(value, axis, [(i, i ^ mask) for i in range(size)])  40.6 us
    pallas_call x2, Pallas kernels, weight_grad(): pl.pallas_call(functools.partial(grad_kernel, groups=groups, where=where,...  27 us
    pallas_call x2, Pallas kernels, rearrange(): pl.pallas_call(functools.partial(rearrange_kernel, halves=halves, count=c...  26.1 us
    pallas_call x2, Pallas kernels, encode(): pl.pallas_call(functools.partial(encode_kernel, half=half, mode=mode, ear...  24.7 us
    pallas_call x2, Pallas kernels, project(): pl.pallas_call(functools.partial(project_kernel, layers=layers, mode=mode...  16.7 us
    pallas_call x2, Pallas kernels, recon_half(): pl.pallas_call(functools.partial(recon_kernel, parts=parts), grid=(blocks...  15.8 us
    pallas_call x4, Pallas kernels, stack(): pl.pallas_call(stack_kernel, out_shape=jax.ShapeDtypeStruct((len(blocks),...  9.85 us
  transfers between devices with their start and end apart: 55, of which 21 were waited for; matrix products, arithmetic and copies ran while one was open for 6% of the time, Pallas kernels for 39%

profile of v5, /device:TPU:0, one launch (start us, length us, event | category | flops | bytes accessed | tf_op | source)
XLA Modules:
  0.0 273.5 jit_solution(13375458070730486241)
XLA Ops:
  8.2 3.1 %collective-permute-start = (bf16[256,640]{1,0:T(8,128)(2,1)S(1)}, bf16[256,640]{1,0:T(8,128)(2,1)}, u32[]{:S(2)}, u32[]{:S(2)}) collective-permute-start(bf16[256,640]{1,0:T(8,128)(2,1)S(1)} %bitcast.47), channel_id=1, source_target_pairs={{0,8},{4,12},{8,0},{12,4},{16,24},{20,28},{24,16},{28,20},{1,9},{5... | collective-permute-start | bytes 983048 | tf_op jit(solution)/shard_map/ppermute | solution.py:21
  11.3 2.6 collective-permute-start.1
  18.1 13.1 %rearrange.2 = (bf16[2,1024,2560]{2,1,0:T(8,128)(2,1)}, bf16[2,1024,2560]{2,1,0:T(8,128)(2,1)}) custom-call(s32[2]{0:T(128)} %pad_add_fusion.1.place, bf16[2048,2,5120]{2,1,0:T(2,128)(2,1)} %refs_1_.3, bf16[2048,2,5120]{2,1,0:T(2,128)(2,1)} %refs_1_.3), custom_call_target="tpu_custom_call" | custom-call | flops 1024 | bytes 1024 | tf_op jit(solution)/shard_map/rearrange/pallas_call | solution.py:346
  35.7 13.0 %rearrange.3 = (bf16[2,1024,2560]{2,1,0:T(8,128)(2,1)}, bf16[2,1024,2560]{2,1,0:T(8,128)(2,1)}) custom-call(s32[2]{0:T(128)} %pad_add_fusion.1.place, bf16[2048,2,5120]{2,1,0:T(2,128)(2,1)} %refs_1_.3, bf16[2048,2,5120]{2,1,0:T(2,128)(2,1)} %refs_1_.3, ...), custom_call_target="tpu_custom_call", output_to_operand_aliasing={{0}: (3, {}), {1}: (4, {})} | custom-call | flops 1024 | bytes 1024 | tf_op jit(solution)/shard_map/rearrange/pallas_call | solution.py:346
  48.7 2.1 collective-permute-done.6.refs_1_
  50.8 2.5 stack.29.ref.refs_0_
  57.0 12.4 %encode_parts.1.refs_2_ = f32[2,1024,256]{2,1,0:T(8,128)} custom-call(s32[2]{0:T(128)} %pad_add_fusion.1.place, bf16[2048,2,5120]{2,1,0:T(2,128)(2,1)} %w_ref.3, bf16[4,256,640]{2,1,0:T(8,128)(2,1)} %stack.29.ref.refs_0_, bf16[4,256,640]{2,1,0:T(8,128)(2,1)} %collective-permute-done.8.refs_1_), custom_call_target="tpu_custom_call" | custom-call | flops 1024 | bytes 1024 | tf_op jit(solution)/shard_map/encode_parts/pallas_call | solution.py:289
  70.2 2.5 stack.30.ref.refs_0_
  72.7 2.0 squares.5
  80.7 12.2 %encode_act.1 = (bf16[256,1024]{1,0:T(8,128)(2,1)}, bf16[1024,256]{1,0:T(8,128)(2,1)}) custom-call(s32[2]{0:T(128)} %pad_add_fusion.1.place, bf16[2048,2,5120]{2,1,0:T(2,128)(2,1)} %w_ref.3, bf16[4,256,640]{2,1,0:T(8,128)(2,1)} %stack.30.ref.refs_0_, bf16[4,256,640]{2,1,0:T(8,128)(2,1)} %collective-permute-done.12.refs_1_, ...), custom_call_target="tpu_custom_call" | custom-call | flops 1024 | bytes 1024 | tf_op jit(solution)/shard_map/encode_act/pallas_call | solution.py:289
  92.9 7.8 %recon_half.2 = (f32[4,256,640]{2,1,0:T(8,128)}, bf16[4,256,640]{2,1,0:T(8,128)(2,1)}) custom-call(bf16[256,1024]{1,0:T(8,128)(2,1)} %get-tuple-element.46.act_ref, bf16[2,1024,2560]{2,1,0:T(8,128)(2,1)} %get-tuple-element.40.refs_0_.refs_1_, bf16[2,1024,2560]{2,1,0:T(8,128)(2,1)} %get-tuple-element.40.refs_0_.refs_1_), custom_call_target="tpu_custom_call" | custom-call | flops 1024 | bytes 1024 | tf_op jit(solution)/shard_map/recon_half/pallas_call | solution.py:502
  101.4 2.9 %collective-permute-done.13 = bf16[4,256,640]{2,1,0:T(8,128)(2,1)S(1)} collective-permute-done((bf16[4,256,640]{2,1,0:T(8,128)(2,1)}, bf16[4,256,640]{2,1,0:T(8,128)(2,1)S(1)}, u32[]{:S(2)}, u32[]{:S(2)}) %collective-permute-start.13) | collective-permute-done | bytes 1310752 | tf_op jit(solution)/shard_map/ppermute | solution.py:21
  104.2 2.9 %add_convert_fusion = (bf16[2,256,640]{2,1,0:T(8,128)(2,1)S(1)}, bf16[2,256,640]{2,1,0:T(8,128)(2,1)}) fusion(f32[4,256,640]{2,1,0:T(8,128)} %get-tuple-element.44, bf16[4,256,640]{2,1,0:T(8,128)(2,1)S(1)} %collective-permute-done.13), kind=kLoop, calls=%fused_computation | loop fusion | flops 1966080 | bytes 5242880 | tf_op jit(solution)/shard_map/convert_element_type | solution.py:703
  108.2 8.0 %recon_half.3 = (f32[4,256,640]{2,1,0:T(8,128)}, bf16[256,640]{1,0:T(8,128)(2,1)}, bf16[256,640]{1,0:T(8,128)(2,1)}, bf16[256,640]{1,0:T(8,128)(2,1)}, bf16[256,640]{1,0:T(8,128)(2,1)}) custom-call(bf16[256,1024]{1,0:T(8,128)(2,1)} %get-tuple-element.46.act_ref, bf16[2,1024,2560]{2,1,0:T(8,128)(2,1)} %get-tuple-element.39.refs_0_.refs_1_, ...), custom_call_target="tpu_custom_call" | custom-call | flops 1024 | bytes 1024 | tf_op jit(solution)/shard_map/recon_half/pallas_call | solution.py:502
  118.0 7.1 %collective-permute-done.17 = bf16[2,256,640]{2,1,0:T(8,128)(2,1)} collective-permute-done((bf16[2,256,640]{2,1,0:T(8,128)(2,1)}, bf16[2,256,640]{2,1,0:T(8,128)(2,1)}, u32[]{:S(2)}, u32[]{:S(2)}) %collective-permute-start.17) | collective-permute-done | bytes 655392 | tf_op jit(solution)/shard_map/ppermute | solution.py:21
  128.6 9.8 %collective-permute-done.15 = bf16[2,256,640]{2,1,0:T(8,128)(2,1)S(1)} collective-permute-done((bf16[2,256,640]{2,1,0:T(8,128)(2,1)S(1)}, bf16[2,256,640]{2,1,0:T(8,128)(2,1)S(1)}, u32[]{:S(2)}, u32[]{:S(2)}) %collective-permute-start.15) | collective-permute-done | bytes 655392 | tf_op jit(solution)/shard_map/ppermute | solution.py:21
  143.7 13.6 %collective-permute-done.22 = bf16[256,640]{1,0:T(8,128)(2,1)S(1)} collective-permute-done((bf16[256,640]{1,0:T(8,128)(2,1)S(1)}, bf16[256,640]{1,0:T(8,128)(2,1)S(1)}, u32[]{:S(2)}, u32[]{:S(2)}) %collective-permute-start.22) | collective-permute-done | bytes 327712 | tf_op jit(solution)/shard_map/ppermute | solution.py:21
  159.9 3.2 %collective-permute-start.27 = (bf16[256,640]{1,0:T(8,128)(2,1)S(1)}, bf16[256,640]{1,0:T(8,128)(2,1)S(1)}, u32[]{:S(2)}, u32[]{:S(2)}) collective-permute-start(bf16[256,640]{1,0:T(8,128)(2,1)S(1)} %bitcast.53), channel_id=1, source_target_pairs={{0,16},{4,20},{8,24},{12,28},{16,0},{20,4},{24,8},{28,12},{1,17},{... | collective-permute-start | bytes 983048 | tf_op jit(solution)/shard_map/ppermute | solution.py:21
  164.4 3.1 %collective-permute-done.24.refs_0_ = bf16[256,640]{1,0:T(8,128)(2,1)S(1)} collective-permute-done((bf16[256,640]{1,0:T(8,128)(2,1)S(1)}, bf16[256,640]{1,0:T(8,128)(2,1)S(1)}, u32[]{:S(2)}, u32[]{:S(2)}) %collective-permute-start.24) | collective-permute-done | bytes 327712 | tf_op jit(solution)/shard_map/ppermute | solution.py:21
  167.5 7.6 %collective-permute-done.25.refs_1_ = bf16[256,640]{1,0:T(8,128)(2,1)S(1)} collective-permute-done((bf16[256,640]{1,0:T(8,128)(2,1)S(1)}, bf16[256,640]{1,0:T(8,128)(2,1)S(1)}, u32[]{:S(2)}, u32[]{:S(2)}) %collective-permute-start.25) | collective-permute-done | bytes 327712 | tf_op jit(solution)/shard_map/ppermute | solution.py:21
  178.7 5.8 %collective-permute-done.29.refs_2_ = bf16[256,640]{1,0:T(8,128)(2,1)S(1)} collective-permute-done((bf16[256,640]{1,0:T(8,128)(2,1)S(1)}, bf16[256,640]{1,0:T(8,128)(2,1)S(1)}, u32[]{:S(2)}, u32[]{:S(2)}) %collective-permute-start.29) | collective-permute-done | bytes 327712 | tf_op jit(solution)/shard_map/ppermute | solution.py:21
  186.0 2.5 stack.31.refs_2_.ref.refs_0_
  192.5 2.0 squares.6
  194.6 8.1 %project_sum.1.refs_4_ = f32[1024,256]{1,0:T(8,128)} custom-call(bf16[2,1024,2560]{2,1,0:T(8,128)(2,1)} %get-tuple-element.39.refs_0_.refs_1_, bf16[2,1024,2560]{2,1,0:T(8,128)(2,1)} %get-tuple-element.39.refs_0_.refs_1_, bf16[4,256,640]{2,1,0:T(8,128)(2,1)} %stack.31.refs_2_.ref.refs_0_, bf16[4,256,640]{2,1,0:T(8,128)(2,1)} %collective-permute-done.33.refs_3_.refs_2_), custom_call_target="tpu_custom_call" | custom-call | flops 1024 | bytes 1024 | tf_op jit(solution)/shard_map/project_sum/pallas_call | solution.py:436
  202.7 3.3 %collective-permute-done.35.refs_6_ = bf16[256,640]{1,0:T(8,128)(2,1)} collective-permute-done((bf16[256,640]{1,0:T(8,128)(2,1)}, bf16[256,640]{1,0:T(8,128)(2,1)}, u32[]{:S(2)}, u32[]{:S(2)}) %collective-permute-start.35) | collective-permute-done | bytes 327712 | tf_op jit(solution)/shard_map/ppermute | solution.py:21
  207.4 2.5 stack.32.refs_2_.ref.refs_1_
  213.2 8.6 %project_grad.1 = (bf16[512,256]{1,0:T(8,128)(2,1)}, bf16[512,256]{1,0:T(8,128)(2,1)}) custom-call(bf16[2,1024,2560]{2,1,0:T(8,128)(2,1)} %get-tuple-element.40.refs_0_.refs_1_, bf16[2,1024,2560]{2,1,0:T(8,128)(2,1)} %get-tuple-element.40.refs_0_.refs_1_, bf16[4,256,640]{2,1,0:T(8,128)(2,1)} %stack.32.refs_2_.ref.refs_1_, ...), custom_call_target="tpu_custom_call" | custom-call | flops 1024 | bytes 1024 | tf_op jit(solution)/shard_map/project_grad/pallas_call | solution.py:436
  224.0 3.6 %collective-permute-done.39.refs_9_ = bf16[256,640]{1,0:T(8,128)(2,1)} collective-permute-done((bf16[256,640]{1,0:T(8,128)(2,1)S(1)}, bf16[256,640]{1,0:T(8,128)(2,1)}, u32[]{:S(2)}, u32[]{:S(2)}) %collective-permute-start.39) | collective-permute-done | bytes 327712 | tf_op jit(solution)/shard_map/ppermute | solution.py:21
  227.6 2.0 squares.7
  230.3 2.3 collective-permute-done.37.far_ref
  237.2 13.6 %weight_grad.2 = bf16[512,2,5120]{2,1,0:T(2,128)(2,1)} custom-call(s32[3]{0:T(128)} %pad_add_fusion.place, f32[2]{0:T(128)} %add_rsqrt_fusion.refs_3_.scale_ref, bf16[512,256]{1,0:T(8,128)(2,1)} %get-tuple-element.58.own_ref, bf16[512,256]{1,0:T(8,128)(2,1)} %copy-done.21, bf16[4,4,256,640]{3,2,1,0:T(8,128)(2,1)} %bitcast.58, bf16[4,4,256,640]{3,2,1,0:T(8,128)(2,1)} %bitcast.59), custom_call_target="tpu_custom_call" | custom-call | flops 10737418240 | bytes 41943040 | tf_op jit(solution)/shard_map/weight_grad/pallas_call | solution.py:607
  252.1 13.4 %weight_grad.3 = bf16[512,2,5120]{2,1,0:T(2,128)(2,1)} custom-call(s32[3]{0:T(128)} %pad_add_fusion.place, f32[2]{0:T(128)} %add_rsqrt_fusion.refs_3_.scale_ref, bf16[1024,256]{1,0:T(8,128)(2,1)} %get-tuple-element.63.own_ref, bf16[512,256]{1,0:T(8,128)(2,1)} %copy-done.20, bf16[4,256,640]{2,1,0:T(8,128)(2,1)} %stack.31.refs_2_.ref.refs_0_, ...), custom_call_target="tpu_custom_call" | custom-call | flops 10737418240 | bytes 41943040 | tf_op jit(solution)/shard_map/weight_grad/pallas_call | solution.py:607
  (165 shorter events, 58.2 us)
Async XLA Ops:
  7.2 151.5 %all-gather.5.cloned.1.call-start = ((), (), s32[]{:S(2)}) async-start(), calls=%async_computation | async-start | bytes 6553600 | tf_op jit(solution)/shard_map/all_gather | solution.py:694
  8.2 24.9 %collective-permute-start = (bf16[256,640]{1,0:T(8,128)(2,1)S(1)}, bf16[256,640]{1,0:T(8,128)(2,1)}, u32[]{:S(2)}, u32[]{:S(2)}) collective-permute-start(bf16[256,640]{1,0:T(8,128)(2,1)S(1)} %bitcast.47), channel_id=1, source_target_pairs={{0,8},{4,12},{8,0},{12,4},{16,24},{20,28},{24,16},{28,20},{1,9},{5... | collective-permute-start | bytes 983048 | tf_op jit(solution)/shard_map/ppermute | solution.py:21
  11.3 21.8 %collective-permute-start.1 = (bf16[256,640]{1,0:T(8,128)(2,1)S(1)}, bf16[256,640]{1,0:T(8,128)(2,1)}, u32[]{:S(2)}, u32[]{:S(2)}) collective-permute-start(bf16[256,640]{1,0:T(8,128)(2,1)S(1)} %bitcast.48), channel_id=1, source_target_pairs={{0,16},{4,20},{8,24},{12,28},{16,0},{20,4},{24,8},{28,12},{1,17},{... | collective-permute-start | bytes 983048 | tf_op jit(solution)/shard_map/ppermute | solution.py:21
  13.9 19.2 %collective-permute-start.2 = (bf16[256,640]{1,0:T(8,128)(2,1)S(1)}, bf16[256,640]{1,0:T(8,128)(2,1)S(1)}, u32[]{:S(2)}, u32[]{:S(2)}) collective-permute-start(bf16[256,640]{1,0:T(8,128)(2,1)S(1)} %bitcast.49), channel_id=1, source_target_pairs={{0,4},{4,0},{8,12},{12,8},{16,20},{20,16},{24,28},{28,24},{1,5},{5... | collective-permute-start | bytes 983048 | tf_op jit(solution)/shard_map/ppermute | solution.py:21
  17.5 13.8 %collective-permute-start.3 = (bf16[128,1024]{1,0:T(8,128)(2,1)}, bf16[128,1024]{1,0:T(8,128)(2,1)}, u32[]{:S(2)}, u32[]{:S(2)}) collective-permute-start(bf16[128,1024]{1,0:T(8,128)(2,1)} %pad_maximum_fusion.1), channel_id=1, source_target_pairs={{0,1},{1,0},{2,3},{3,2},{4,5},{5,4},{6,7},{7,6},{8,9},{9,8},{10,11... | collective-permute-start | bytes 786440 | tf_op jit(solution)/shard_map/ppermute | solution.py:21
  33.2 15.6 %collective-permute-start.4 = (bf16[256,640]{1,0:T(8,128)(2,1)}, bf16[256,640]{1,0:T(8,128)(2,1)}, u32[]{:S(2)}, u32[]{:S(2)}) collective-permute-start(bf16[256,640]{1,0:T(8,128)(2,1)} %collective-permute-done.1.refs_2_), channel_id=1, source_target_pairs={{0,8},{4,12},{8,0},{12,4},{16,24},{20,28},{24,16},{28,20},{1,9},{5... | collective-permute-start | bytes 983048 | tf_op jit(solution)/shard_map/ppermute | solution.py:21
  33.7 15.0 %collective-permute-start.5 = (bf16[256,640]{1,0:T(8,128)(2,1)}, bf16[256,640]{1,0:T(8,128)(2,1)S(1)}, u32[]{:S(2)}, u32[]{:S(2)}) collective-permute-start(bf16[256,640]{1,0:T(8,128)(2,1)} %collective-permute-done.1.refs_2_), channel_id=1, source_target_pairs={{0,4},{4,0},{8,12},{12,8},{16,20},{20,16},{24,28},{28,24},{1,5},{5... | collective-permute-start | bytes 983048 | tf_op jit(solution)/shard_map/ppermute | solution.py:21
  34.2 16.6 %collective-permute-start.6 = (bf16[256,640]{1,0:T(8,128)(2,1)}, bf16[256,640]{1,0:T(8,128)(2,1)}, u32[]{:S(2)}, u32[]{:S(2)}) collective-permute-start(bf16[256,640]{1,0:T(8,128)(2,1)} %collective-permute-done.refs_1_), channel_id=1, source_target_pairs={{0,4},{4,0},{8,12},{12,8},{16,20},{20,16},{24,28},{28,24},{1,5},{5... | collective-permute-start | bytes 983048 | tf_op jit(solution)/shard_map/ppermute | solution.py:21
  53.3 105.3 %all-gather.7.cloned.1.call-start = ((), (), s32[]{:S(2)}) async-start(), calls=%async_computation.1 | async-start | bytes 6553600 | tf_op jit(solution)/shard_map/all_gather | solution.py:694
  53.6 15.8 %collective-permute-start.7 = (bf16[256,640]{1,0:T(8,128)(2,1)}, bf16[256,640]{1,0:T(8,128)(2,1)S(1)}, u32[]{:S(2)}, u32[]{:S(2)}) collective-permute-start(bf16[256,640]{1,0:T(8,128)(2,1)} %collective-permute-done.4.refs_3_), channel_id=1, source_target_pairs={{0,4},{4,0},{8,12},{12,8},{16,20},{20,16},{24,28},{28,24},{1,5},{5... | collective-permute-start | bytes 983048 | tf_op jit(solution)/shard_map/ppermute | solution.py:21
  107.1 17.9 %collective-permute-start.17 = (bf16[2,256,640]{2,1,0:T(8,128)(2,1)}, bf16[2,256,640]{2,1,0:T(8,128)(2,1)}, u32[]{:S(2)}, u32[]{:S(2)}) collective-permute-start(bf16[2,256,640]{2,1,0:T(8,128)(2,1)} %get-tuple-element.70), channel_id=1, source_target_pairs={{0,4},{4,0},{8,12},{12,8},{16,20},{20,16},{24,28},{28,24},{1,5},{5... | collective-permute-start | bytes 1966088 | tf_op jit(solution)/shard_map/ppermute | solution.py:21
  116.2 22.2 %collective-permute-start.15 = (bf16[2,256,640]{2,1,0:T(8,128)(2,1)S(1)}, bf16[2,256,640]{2,1,0:T(8,128)(2,1)S(1)}, u32[]{:S(2)}, u32[]{:S(2)}) collective-permute-start(bf16[2,256,640]{2,1,0:T(8,128)(2,1)S(1)} %get-tuple-element.69), channel_id=1, source_target_pairs={{0,4},{4,0},{8,12},{12,8},{16,20},{20,16},{24,28},{28,24},{1,5},{5... | collective-permute-start | bytes 1966088 | tf_op jit(solution)/shard_map/ppermute | solution.py:21
  126.3 12.1 %collective-permute-start.18 = (bf16[256,640]{1,0:T(8,128)(2,1)S(1)}, bf16[256,640]{1,0:T(8,128)(2,1)S(1)}, u32[]{:S(2)}, u32[]{:S(2)}) collective-permute-start(bf16[256,640]{1,0:T(8,128)(2,1)S(1)} %fusion.5), channel_id=1, source_target_pairs={{0,8},{4,12},{8,0},{12,4},{16,24},{20,28},{24,16},{28,20},{1,9},{5... | collective-permute-start | bytes 983048 | tf_op jit(solution)/shard_map/ppermute | solution.py:21
  128.6 15.2 %collective-permute-start.14 = (bf16[256,640]{1,0:T(8,128)(2,1)}, bf16[256,640]{1,0:T(8,128)(2,1)S(1)}, u32[]{:S(2)}, u32[]{:S(2)}) collective-permute-start(bf16[256,640]{1,0:T(8,128)(2,1)} %get-tuple-element.48), channel_id=1, source_target_pairs={{0,1},{1,0},{2,3},{3,2},{4,5},{5,4},{6,7},{7,6},{8,9},{9,8},{10,11... | collective-permute-start | bytes 983048 | tf_op jit(solution)/shard_map/ppermute | solution.py:21
  140.1 17.2 %collective-permute-start.22 = (bf16[256,640]{1,0:T(8,128)(2,1)S(1)}, bf16[256,640]{1,0:T(8,128)(2,1)S(1)}, u32[]{:S(2)}, u32[]{:S(2)}) collective-permute-start(bf16[256,640]{1,0:T(8,128)(2,1)S(1)} %get-tuple-element.72), channel_id=1, source_target_pairs={{0,16},{4,20},{8,24},{12,28},{16,0},{20,4},{24,8},{28,12},{1,17},{... | collective-permute-start | bytes 983048 | tf_op jit(solution)/shard_map/ppermute | solution.py:21
  140.4 16.9 %collective-permute-start.20 = (bf16[256,640]{1,0:T(8,128)(2,1)S(1)}, bf16[256,640]{1,0:T(8,128)(2,1)S(1)}, u32[]{:S(2)}, u32[]{:S(2)}) collective-permute-start(bf16[256,640]{1,0:T(8,128)(2,1)S(1)} %get-tuple-element.71), channel_id=1, source_target_pairs={{0,8},{4,12},{8,0},{12,4},{16,24},{20,28},{24,16},{28,20},{1,9},{5... | collective-permute-start | bytes 983048 | tf_op jit(solution)/shard_map/ppermute | solution.py:21
  143.0 15.6 %collective-permute-start.23 = (bf16[512,256]{1,0:T(8,128)(2,1)S(1)}, bf16[512,256]{1,0:T(8,128)(2,1)S(1)}, u32[]{:S(2)}, u32[]{:S(2)}) collective-permute-start(bf16[512,256]{1,0:T(8,128)(2,1)S(1)} %slice.51), channel_id=1, source_target_pairs={{0,2},{1,3},{2,0},{3,1},{4,6},{5,7},{6,4},{7,5},{8,10},{9,11},{10,... | collective-permute-start | bytes 786440 | tf_op jit(solution)/shard_map/ppermute | solution.py:21
  159.9 15.2 %collective-permute-start.25 = (bf16[256,640]{1,0:T(8,128)(2,1)S(1)}, bf16[256,640]{1,0:T(8,128)(2,1)S(1)}, u32[]{:S(2)}, u32[]{:S(2)}) collective-permute-start(bf16[256,640]{1,0:T(8,128)(2,1)S(1)} %bitcast.52), channel_id=1, source_target_pairs={{0,8},{4,12},{8,0},{12,4},{16,24},{20,28},{24,16},{28,20},{1,9},{5... | collective-permute-start | bytes 983048 | tf_op jit(solution)/shard_map/ppermute | solution.py:21
  159.9 16.3 %collective-permute-start.27 = (bf16[256,640]{1,0:T(8,128)(2,1)S(1)}, bf16[256,640]{1,0:T(8,128)(2,1)S(1)}, u32[]{:S(2)}, u32[]{:S(2)}) collective-permute-start(bf16[256,640]{1,0:T(8,128)(2,1)S(1)} %bitcast.53), channel_id=1, source_target_pairs={{0,16},{4,20},{8,24},{12,28},{16,0},{20,4},{24,8},{28,12},{1,17},{... | collective-permute-start | bytes 983048 | tf_op jit(solution)/shard_map/ppermute | solution.py:21
  163.1 13.1 %collective-permute-start.28 = (bf16[256,640]{1,0:T(8,128)(2,1)S(1)}, bf16[256,640]{1,0:T(8,128)(2,1)S(1)}, u32[]{:S(2)}, u32[]{:S(2)}) collective-permute-start(bf16[256,640]{1,0:T(8,128)(2,1)S(1)} %bitcast.54), channel_id=1, source_target_pairs={{0,2},{1,3},{2,0},{3,1},{4,6},{5,7},{6,4},{7,5},{8,10},{9,11},{10,... | collective-permute-start | bytes 983048 | tf_op jit(solution)/shard_map/ppermute | solution.py:21
  188.5 14.2 %collective-permute-start.34 = (bf16[256,640]{1,0:T(8,128)(2,1)}, bf16[256,640]{1,0:T(8,128)(2,1)}, u32[]{:S(2)}, u32[]{:S(2)}) collective-permute-start(bf16[256,640]{1,0:T(8,128)(2,1)} %copy-done.11), channel_id=1, source_target_pairs={{0,2},{1,3},{2,0},{3,1},{4,6},{5,7},{6,4},{7,5},{8,10},{9,11},{10,... | collective-permute-start | bytes 983048 | tf_op jit(solution)/shard_map/ppermute | solution.py:21
  189.4 16.6 %collective-permute-start.35 = (bf16[256,640]{1,0:T(8,128)(2,1)}, bf16[256,640]{1,0:T(8,128)(2,1)}, u32[]{:S(2)}, u32[]{:S(2)}) collective-permute-start(bf16[256,640]{1,0:T(8,128)(2,1)} %copy-done.10), channel_id=1, source_target_pairs={{0,2},{1,3},{2,0},{3,1},{4,6},{5,7},{6,4},{7,5},{8,10},{9,11},{10,... | collective-permute-start | bytes 983048 | tf_op jit(solution)/shard_map/ppermute | solution.py:21
  190.5 15.4 %collective-permute-start.32 = (bf16[256,640]{1,0:T(8,128)(2,1)}, bf16[256,640]{1,0:T(8,128)(2,1)}, u32[]{:S(2)}, u32[]{:S(2)}) collective-permute-start(bf16[256,640]{1,0:T(8,128)(2,1)} %copy-done.8), channel_id=1, source_target_pairs={{0,4},{4,0},{8,12},{12,8},{16,20},{20,16},{24,28},{28,24},{1,5},{5... | collective-permute-start | bytes 983048 | tf_op jit(solution)/shard_map/ppermute | solution.py:21
  191.5 15.9 %collective-permute-start.26 = (bf16[256,640]{1,0:T(8,128)(2,1)}, bf16[256,640]{1,0:T(8,128)(2,1)}, u32[]{:S(2)}, u32[]{:S(2)}) collective-permute-start(bf16[256,640]{1,0:T(8,128)(2,1)} %copy-done.10), channel_id=1, source_target_pairs={{0,4},{4,0},{8,12},{12,8},{16,20},{20,16},{24,28},{28,24},{1,5},{5... | collective-permute-start | bytes 983048 | tf_op jit(solution)/shard_map/ppermute | solution.py:21
  209.9 12.0 %collective-permute-start.40 = (bf16[256,640]{1,0:T(8,128)(2,1)S(1)}, bf16[256,640]{1,0:T(8,128)(2,1)}, u32[]{:S(2)}, u32[]{:S(2)}) collective-permute-start(bf16[256,640]{1,0:T(8,128)(2,1)S(1)} %copy-done.9), channel_id=1, source_target_pairs={{0,2},{1,3},{2,0},{3,1},{4,6},{5,7},{6,4},{7,5},{8,10},{9,11},{10,... | collective-permute-start | bytes 983048 | tf_op jit(solution)/shard_map/ppermute | solution.py:21
  210.8 12.9 %collective-permute-start.38 = (bf16[256,640]{1,0:T(8,128)(2,1)}, bf16[256,640]{1,0:T(8,128)(2,1)}, u32[]{:S(2)}, u32[]{:S(2)}) collective-permute-start(bf16[256,640]{1,0:T(8,128)(2,1)} %collective-permute-done.35.refs_6_), channel_id=1, source_target_pairs={{0,4},{4,0},{8,12},{12,8},{16,20},{20,16},{24,28},{28,24},{1,5},{5... | collective-permute-start | bytes 983048 | tf_op jit(solution)/shard_map/ppermute | solution.py:21
  211.7 15.8 %collective-permute-start.39 = (bf16[256,640]{1,0:T(8,128)(2,1)S(1)}, bf16[256,640]{1,0:T(8,128)(2,1)}, u32[]{:S(2)}, u32[]{:S(2)}) collective-permute-start(bf16[256,640]{1,0:T(8,128)(2,1)S(1)} %copy-done.6), channel_id=1, source_target_pairs={{0,2},{1,3},{2,0},{3,1},{4,6},{5,7},{6,4},{7,5},{8,10},{9,11},{10,... | collective-permute-start | bytes 983048 | tf_op jit(solution)/shard_map/ppermute | solution.py:21
  235.5 16.6 %collective-permute-start.49 = (bf16[256,640]{1,0:T(8,128)(2,1)}, bf16[256,640]{1,0:T(8,128)(2,1)}, u32[]{:S(2)}, u32[]{:S(2)}) collective-permute-start(bf16[256,640]{1,0:T(8,128)(2,1)} %collective-permute-done.34.refs_8_), channel_id=1, source_target_pairs={{0,1},{1,0},{2,3},{3,2},{4,5},{5,4},{6,7},{7,6},{8,9},{9,8},{10,11... | collective-permute-start | bytes 983048 | tf_op jit(solution)/shard_map/ppermute | solution.py:21
  235.5 16.6 %collective-permute-start.48 = (bf16[256,640]{1,0:T(8,128)(2,1)}, bf16[256,640]{1,0:T(8,128)(2,1)}, u32[]{:S(2)}, u32[]{:S(2)}) collective-permute-start(bf16[256,640]{1,0:T(8,128)(2,1)} %collective-permute-done.38.refs_7_), channel_id=1, source_target_pairs={{0,1},{1,0},{2,3},{3,2},{4,5},{5,4},{6,7},{7,6},{8,9},{9,8},{10,11... | collective-permute-start | bytes 983048 | tf_op jit(solution)/shard_map/ppermute | solution.py:21
  236.4 15.7 %collective-permute-start.50 = (bf16[256,640]{1,0:T(8,128)(2,1)}, bf16[256,640]{1,0:T(8,128)(2,1)}, u32[]{:S(2)}, u32[]{:S(2)}) collective-permute-start(bf16[256,640]{1,0:T(8,128)(2,1)} %collective-permute-done.39.refs_9_), channel_id=1, source_target_pairs={{0,1},{1,0},{2,3},{3,2},{4,5},{5,4},{6,7},{7,6},{8,9},{9,8},{10,11... | collective-permute-start | bytes 983048 | tf_op jit(solution)/shard_map/ppermute | solution.py:21
  236.7 15.4 %collective-permute-start.51 = (bf16[256,640]{1,0:T(8,128)(2,1)}, bf16[256,640]{1,0:T(8,128)(2,1)}, u32[]{:S(2)}, u32[]{:S(2)}) collective-permute-start(bf16[256,640]{1,0:T(8,128)(2,1)} %collective-permute-done.40.refs_10_), channel_id=1, source_target_pairs={{0,1},{1,0},{2,3},{3,2},{4,5},{5,4},{6,7},{7,6},{8,9},{9,8},{10,11... | collective-permute-start | bytes 983048 | tf_op jit(solution)/shard_map/ppermute | solution.py:21
  236.9 15.2 %collective-permute-start.52 = (bf16[256,640]{1,0:T(8,128)(2,1)S(1)}, bf16[256,640]{1,0:T(8,128)(2,1)}, u32[]{:S(2)}, u32[]{:S(2)}) collective-permute-start(bf16[256,640]{1,0:T(8,128)(2,1)S(1)} %collective-permute-done.41.refs_11_), channel_id=1, source_target_pairs={{0,1},{1,0},{2,3},{3,2},{4,5},{5,4},{6,7},{7,6},{8,9},{9,8},{10,11... | collective-permute-start | bytes 983048 | tf_op jit(solution)/shard_map/ppermute | solution.py:21
  (45 other events, 564.8 us)
Sparse Core Ops, SparseCore 0:
  53.4 39.0 all-gather.4
  94.1 40.4 all-gather.6
